TPU v7x, 32 devices: a whole 2x2x4 slice. The times are simulated.
32 devices in a mesh: expert: 16 (over z, y, core), seq: 2 (over x).
Axes of the slice: x: 2, y: 2, z: 4, core: 2. Of those that a mesh axis runs over, the one named last changes fastest.
Arguments:
- tokens: bfloat16 [1536, 4096], P('expert', 'seq'), may hold values from -6 to 6
- cotangent: bfloat16 [1536, 4096], P('expert', 'seq'), may hold values from -0.59765625 to 0.59765625
- expert_ids: int32 [1536, 8], P('expert'), may hold values from 0 to 15, all different within a row; in each aligned block of 96 rows (0 to 95, 96 to 191, ...) at most 54 rows name the same one
- gate_values: bfloat16 [1536, 8], P('expert'), may hold values from 0.019897461 to 0.5
- gate_weight: bfloat16 [16, 4096, 768], P('expert', 'seq'), may hold values from -0.09375 to 0.09375
- up_weight: bfloat16 [16, 4096, 768], P('expert', 'seq'), may hold values from -0.09375 to 0.09375
- down_weight: bfloat16 [16, 768, 4096], P('expert', None, 'seq'), may hold values from -0.21875 to 0.21875
Outputs:
- input_grad: bfloat16 [1536, 4096], P('expert', 'seq')
- gate_grad: bfloat16 [1536, 8], P('expert')
- gate_weight_grad: bfloat16 [16, 4096, 768], P('expert', 'seq')
- up_weight_grad: bfloat16 [16, 4096, 768], P('expert', 'seq')
- down_weight_grad: bfloat16 [16, 768, 4096], P('expert', None, 'seq')
Inputs may be any that keep to these rules, and one draw needn't show every extreme that they name: `expert_ids`: each row names 8 different experts; within each aligned block of 96 rows no expert is named by more than 54 rows, a bound that some block reaches.
All inputs are finite; a program needn't handle non-finite values.
Results may differ from a plain program's by a relative error of at most 0.019.
Values may be sent and summed in bfloat16 or wider, within the bound.
No kernel may reach another device: no remote copies, remote signals or barrier semaphores. Data moves between devices by JAX's collectives and lax.ppermute only.
A program may use at most 128 MiB of HBM per device.

v0:
```python
import jax
import jax.numpy as jnp
from jax import lax
from jax.sharding import PartitionSpec as P


def pointwise(summed, gate_rows, hidden):
    gate_pre = summed[:, :hidden]
    up_pre = summed[:, hidden : 2 * hidden]
    down_back = summed[:, 2 * hidden :]
    sigmoid_val = jax.nn.sigmoid(gate_pre)
    silu_val = gate_pre * sigmoid_val
    activation = silu_val * up_pre
    slot_grad = jnp.sum(activation * down_back, axis=-1)
    act_grad = gate_rows.astype(jnp.float32)[:, None] * down_back
    pre_gate_grad = act_grad * up_pre * sigmoid_val * (1.0 + gate_pre * (1.0 - sigmoid_val))
    pre_up_grad = act_grad * silu_val
    return (
        activation.astype(jnp.bfloat16),
        pre_gate_grad.astype(jnp.bfloat16),
        pre_up_grad.astype(jnp.bfloat16),
        slot_grad.astype(jnp.bfloat16),
    )


def local(tokens, cotangent, expert_ids, gate_values, gate_weight, up_weight, down_weight):
    expert_count = lax.axis_size("expert")
    seq_count = lax.axis_size("seq")
    token_count, quarter = tokens.shape
    top_count = expert_ids.shape[1]
    hidden = gate_weight.shape[2]
    capacity = min(
        token_count,
        token_count * top_count // expert_count + token_count * top_count // (8 * expert_count),
    )
    total_rows = expert_count * capacity
    onehot = (expert_ids[:, :, None] == jnp.arange(expert_count, dtype=jnp.int32)).astype(jnp.int32)
    per_row = jnp.sum(onehot, axis=1)
    before = jnp.cumsum(per_row, axis=0) - per_row
    slot_index = jnp.sum(onehot * before[:, None, :], axis=2)
    position = (expert_ids * capacity + slot_index).reshape(-1)
    token_number = jnp.repeat(jnp.arange(token_count, dtype=jnp.int32), top_count)
    token_of = jnp.full((total_rows,), token_count, jnp.int32).at[position].set(token_number)
    gate_of = jnp.zeros((total_rows,), jnp.bfloat16).at[position].set(gate_values.reshape(-1))
    zero_row = jnp.zeros((1, quarter), jnp.bfloat16)
    send_x = jnp.concatenate([tokens, zero_row], axis=0)[token_of].reshape(
        expert_count, capacity, quarter
    )
    send_dy = jnp.concatenate([cotangent, zero_row], axis=0)[token_of].reshape(
        expert_count, capacity, quarter
    )
    send_gate = gate_of.reshape(expert_count, capacity)
    recv_x, recv_dy, recv_gate = (
        lax.all_to_all(send_x, "expert", split_axis=0, concat_axis=0, tiled=True),
        lax.all_to_all(send_dy, "expert", split_axis=0, concat_axis=0, tiled=True),
        lax.all_to_all(send_gate, "expert", split_axis=0, concat_axis=0, tiled=True),
    )
    flat_x = recv_x.reshape(total_rows, quarter)
    flat_dy = recv_dy.reshape(total_rows, quarter)
    flat_gate = recv_gate.reshape(total_rows)
    w_gate = gate_weight[0]
    w_up = up_weight[0]
    w_down = down_weight[0]
    contract_last = (((1,), (1,)), ((), ()))
    contract_rows = (((0,), (0,)), ((), ()))
    share_count = total_rows // seq_count
    gate_part = jnp.dot(flat_x, w_gate, preferred_element_type=jnp.float32)
    up_part = jnp.dot(flat_x, w_up, preferred_element_type=jnp.float32)
    down_part = lax.dot_general(flat_dy, w_down, contract_last, preferred_element_type=jnp.float32)
    share_sum = lax.psum_scatter(
        jnp.concatenate([gate_part, up_part, down_part], axis=1).astype(jnp.bfloat16),
        "seq",
        scatter_dimension=0,
        tiled=True,
    ).astype(jnp.float32)
    share_start = lax.axis_index("seq") * share_count
    share_gates = lax.dynamic_slice_in_dim(flat_gate, share_start, share_count, 0)
    part_act, part_gate, part_up, part_slot = pointwise(share_sum, share_gates, hidden)
    activation, pre_gate_grad, pre_up_grad, slot_grad = (
        lax.all_gather(part_act, "seq", axis=0, tiled=True),
        lax.all_gather(part_gate, "seq", axis=0, tiled=True),
        lax.all_gather(part_up, "seq", axis=0, tiled=True),
        lax.all_gather(part_slot, "seq", axis=0, tiled=True),
    )
    row_grad = (
        lax.dot_general(pre_gate_grad, w_gate, contract_last, preferred_element_type=jnp.float32)
        + lax.dot_general(pre_up_grad, w_up, contract_last, preferred_element_type=jnp.float32)
    ).astype(jnp.bfloat16)
    returned_dx, returned_gate = (
        lax.all_to_all(
            row_grad.reshape(expert_count, capacity, quarter),
            "expert",
            split_axis=0,
            concat_axis=0,
            tiled=True,
        ),
        lax.all_to_all(
            slot_grad.reshape(expert_count, capacity),
            "expert",
            split_axis=0,
            concat_axis=0,
            tiled=True,
        ),
    )
    scaled_dy = (flat_gate.astype(jnp.float32)[:, None] * flat_dy.astype(jnp.float32)).astype(
        jnp.bfloat16
    )
    down_grad = lax.dot_general(
        activation, scaled_dy, contract_rows, preferred_element_type=jnp.float32
    )
    gate_w_grad = lax.dot_general(
        flat_x, pre_gate_grad, contract_rows, preferred_element_type=jnp.float32
    )
    up_w_grad = lax.dot_general(
        flat_x, pre_up_grad, contract_rows, preferred_element_type=jnp.float32
    )
    picked = returned_dx.reshape(total_rows, quarter)[position].reshape(
        token_count, top_count, quarter
    )
    input_grad = jnp.sum(picked.astype(jnp.float32), axis=1).astype(jnp.bfloat16)
    gate_grad = returned_gate.reshape(total_rows)[position].reshape(token_count, top_count)
    return (
        input_grad,
        gate_grad,
        gate_w_grad.astype(jnp.bfloat16)[None],
        up_w_grad.astype(jnp.bfloat16)[None],
        down_grad.astype(jnp.bfloat16)[None],
    )


def solution(mesh):
    in_specs = (
        P("expert", "seq"),
        P("expert", "seq"),
        P("expert", None),
        P("expert", None),
        P("expert", "seq", None),
        P("expert", "seq", None),
        P("expert", None, "seq"),
    )
    out_specs = (
        P("expert", "seq"),
        P("expert", None),
        P("expert", "seq", None),
        P("expert", "seq", None),
        P("expert", None, "seq"),
    )
    return jax.shard_map(local, mesh=mesh, in_specs=in_specs, out_specs=out_specs, check_vma=False)
```

profile of v0, /device:TPU:13, one launch (start us, length us, event | category | flops | bytes accessed | tf_op | source)
XLA Modules:
  0.0 451.3 jit_solution(2343226892257264247)
XLA Ops:
  7.2 0.9 convert_reduce_fusion
  8.0 0.1 copy.23
  8.1 0.1 reduce_window_sum.11
  8.3 0.1 copy.25
  8.3 0.7 select_reduce_fusion
  9.1 0.7 multiply_add_fusion
  9.8 0.1 copy.26
  9.8 0.1 reshape.104
  10.0 0.1 reshape.161
  10.1 3.4 scatter_custom_fusion.1
  13.5 1.8 concatenate.10
  15.3 9.8 %gather_fusion = bf16[864,2048]{1,0:T(8,128)(2,1)} fusion(bf16[97,2048]{1,0:T(8,128)(2,1)} %concatenate.10, s32[1024]{0:T(1024)S(1)} %pad_clamp_fusion.1), kind=kCustom, calls=%fused_computation | custom fusion | bytes 7081344 | tf_op jit(solution)/shard_map/gather | solution.py:46
  25.1 4.8 %reshape.108 = bf16[16,54,2048]{2,1,0:T(8,128)(2,1)} reshape(bf16[864,2048]{1,0:T(8,128)(2,1)} %gather_fusion) | data formatting | bytes 7077888 | tf_op jit(solution)/shard_map/reshape | solution.py:46
  29.8 6.7 %all-to-all-start.1 = ((bf16[16,54,2048]{2,1,0:T(8,128)(2,1)}), bf16[16,54,2048]{2,1,0:T(8,128)(2,1)}, u32[]{:S(2)}, u32[]{:S(2)}) async-start(bf16[16,54,2048]{2,1,0:T(8,128)(2,1)} %reshape.108), calls=%async_computation.1 | async-start | bytes 7340032 | tf_op jit(solution)/shard_map/all_to_all | solution.py:54
  36.5 0.8 concatenate.11
  37.3 9.8 %gather_fusion.1 = bf16[864,2048]{1,0:T(8,128)(2,1)} fusion(bf16[97,2048]{1,0:T(8,128)(2,1)} %concatenate.11, s32[1024]{0:T(1024)S(1)} %pad_clamp_fusion.1), kind=kCustom, calls=%fused_computation.1 | custom fusion | bytes 7081344 | tf_op jit(solution)/shard_map/gather | solution.py:49
  47.1 4.8 %reshape.110 = bf16[16,54,2048]{2,1,0:T(8,128)(2,1)} reshape(bf16[864,2048]{1,0:T(8,128)(2,1)} %gather_fusion.1) | data formatting | bytes 7077888 | tf_op jit(solution)/shard_map/reshape | solution.py:49
  51.9 65.9 %all-to-all-done.1 = bf16[16,54,2048]{2,1,0:T(8,128)(2,1)} async-done(((bf16[16,54,2048]{2,1,0:T(8,128)(2,1)}), bf16[16,54,2048]{2,1,0:T(8,128)(2,1)}, u32[]{:S(2)}, u32[]{:S(2)}) %all-to-all-start.1) | async-done | bytes 3538976 | tf_op jit(solution)/shard_map/all_to_all | solution.py:54
  117.8 4.9 %all-to-all-start.2 = ((bf16[16,54,2048]{2,1,0:T(8,128)(2,1)}), bf16[16,54,2048]{2,1,0:T(8,128)(2,1)}, u32[]{:S(2)}, u32[]{:S(2)}) async-start(bf16[16,54,2048]{2,1,0:T(8,128)(2,1)} %reshape.110), calls=%async_computation.2 | async-start | bytes 7340032 | tf_op jit(solution)/shard_map/all_to_all | solution.py:55
  122.7 0.3 reduce-scatter.2.cloned.1.call-start
  123.0 4.8 %reshape.109 = bf16[864,2048]{1,0:T(8,128)(2,1)} reshape(bf16[16,54,2048]{2,1,0:T(8,128)(2,1)} %all-to-all-done.1) | data formatting | bytes 7077888 | tf_op jit(solution)/shard_map/reshape | solution.py:58
  127.7 6.1 %fusion.15 = bf16[864,768]{1,0:T(8,128)(2,1)} fusion(bf16[864,2048]{1,0:T(8,128)(2,1)} %reshape.109, bf16[1,2048,768]{2,1,0:T(8,128)(2,1)S(1)} %copy-done), kind=kOutput, calls=%fused_computation.27 | convolution fusion | flops 2718572544 | bytes 8011776 | tf_op jit(solution)/shard_map/dot_general | solution.py:67
  133.9 4.0 fusion.18
  137.8 66.1 %all-to-all-done.2 = bf16[16,54,2048]{2,1,0:T(8,128)(2,1)} async-done(((bf16[16,54,2048]{2,1,0:T(8,128)(2,1)}), bf16[16,54,2048]{2,1,0:T(8,128)(2,1)}, u32[]{:S(2)}, u32[]{:S(2)}) %all-to-all-start.2) | async-done | bytes 3538976 | tf_op jit(solution)/shard_map/all_to_all | solution.py:55
  203.9 4.8 %reshape.111 = bf16[864,2048]{1,0:T(8,128)(2,1)} reshape(bf16[16,54,2048]{2,1,0:T(8,128)(2,1)} %all-to-all-done.2) | data formatting | bytes 7077888 | tf_op jit(solution)/shard_map/reshape | solution.py:59
  208.7 6.0 %fusion.21 = bf16[864,768]{1,0:T(8,128)(2,1)S(1)} fusion(bf16[864,2048]{1,0:T(8,128)(2,1)} %reshape.111, bf16[1,768,2048]{2,1,0:T(8,128)(2,1)} %param.13), kind=kOutput, calls=%fused_computation.29 | convolution fusion | flops 2718572544 | bytes 8011776 | tf_op jit(solution)/shard_map/dot_general | solution.py:69
  214.7 2.0 pad_maximum_fusion
  216.8 0.7 copy-done.7
  217.4 0.1 copy.27
  217.6 0.1 reshape.153
  217.7 8.6 %scatter_custom_fusion = bf16[864]{0:T(1024)(128)(2,1)S(1)} fusion(s32[768]{0:T(1024)S(1)} %fusion.26, bf16[768]{0:T(1024)(128)(2,1)S(1)} %reshape.153, bf16[]{:T(256)} %constant.10.clone.1), kind=kCustom, calls=%fused_computation.50 | custom fusion | bytes 1730 | tf_op jit(solution)/shard_map/scatter | solution.py:44
  226.3 0.7 all_to_all.28
  227.0 4.9 %all-to-all-start = ((bf16[16,1,54]{2,1,0:T(2,128)(2,1)}), bf16[16,1,54]{2,1,0:T(2,128)(2,1)S(1)}, u32[]{:S(2)}, u32[]{:S(2)}) async-start(bf16[16,1,54]{2,1,0:T(2,128)(2,1)} %all_to_all.28), calls=%async_computation | async-start | bytes 16384 | tf_op jit(solution)/shard_map/all_to_all | solution.py:56
  231.9 13.7 %all-gather.4.cloned.1.call-start = ((), (), s32[]{:S(2)}) async-start(), calls=%async_computation.7 | async-start | bytes 1990656 | tf_op jit(solution)/shard_map/all_gather | solution.py:81
  245.6 0.1 reshape.106
  245.7 0.1 dynamic-slice_convert_fusion
  245.8 22.6 %reduce-scatter.2.cloned.1.call-done = bf16[432,2304]{1,0:T(8,128)(2,1)} async-done(((bf16[864,2304]{1,0:T(8,128)(2,1)}), bf16[432,2304]{1,0:T(8,128)(2,1)}) %reduce-scatter.2.cloned.1.call-update) | async-done | bytes 1990672 | tf_op jit(solution)/shard_map/reduce_scatter | solution.py:70
  268.4 1.8 convert_element_type.51
  270.2 2.1 fusion.25
  272.5 0.7 all-gather.6.cloned.1.call-update
  273.2 0.6 dynamic-slice
  274.4 0.2 dynamic-update-slice
  274.7 3.8 all-reduce.2
  278.4 0.7 all_to_all.29
  279.1 7.5 %all-to-all-start.4 = ((bf16[16,1,54]{2,1,0:T(2,128)(2,1)}), bf16[16,1,54]{2,1,0:T(2,128)(2,1)S(1)}, u32[]{:S(2)}, u32[]{:S(2)}) async-start(bf16[16,1,54]{2,1,0:T(2,128)(2,1)} %all_to_all.29), calls=%async_computation.5 | async-start | bytes 16384 | tf_op jit(solution)/shard_map/all_to_all | solution.py:97
  286.6 10.4 %all-gather.4.cloned.1.call-done = bf16[864,768]{1,0:T(8,128)(2,1)} async-done(((bf16[432,768]{1,0:T(8,128)(2,1)}), bf16[864,768]{1,0:T(8,128)(2,1)}) %all-gather.4.cloned.1.call-update) | async-done | bytes 1327120 | tf_op jit(solution)/shard_map/all_gather | solution.py:81
  297.0 6.2 %fusion.8 = f32[864,2048]{1,0:T(8,128)} fusion(bf16[864,768]{1,0:T(8,128)(2,1)} %all-gather.4.cloned.1.call-done, bf16[1,2048,768]{2,1,0:T(8,128)(2,1)S(1)} %copy-done), kind=kOutput, calls=%fused_computation.20 | convolution fusion | flops 2717908992 | bytes 11550720 | tf_op jit(solution)/shard_map/dot_general | solution.py:86
  303.2 20.4 %all-gather.6.cloned.1.call-done = bf16[864,768]{1,0:T(8,128)(2,1)} async-done(((bf16[432,768]{1,0:T(8,128)(2,1)}), bf16[864,768]{1,0:T(8,128)(2,1)}) %all-gather.6.cloned.1.call-update) | async-done | bytes 1327120 | tf_op jit(solution)/shard_map/all_gather | solution.py:82
  323.6 9.2 %add_convert_fusion = bf16[864,2048]{1,0:T(8,128)(2,1)} fusion(f32[864,2048]{1,0:T(8,128)} %fusion.8, bf16[864,768]{1,0:T(8,128)(2,1)} %all-gather.6.cloned.1.call-done, bf16[1,2048,768]{2,1,0:T(8,128)(2,1)} %param.12), kind=kOutput, calls=%fused_computation.7 | convolution fusion | flops 2721447936 | bytes 15089664 | tf_op jit(solution)/shard_map/dot_general | solution.py:87
  332.8 4.8 %reshape.112 = bf16[16,54,2048]{2,1,0:T(8,128)(2,1)} reshape(bf16[864,2048]{1,0:T(8,128)(2,1)} %add_convert_fusion) | data formatting | bytes 7077888 | tf_op jit(solution)/shard_map/reshape | solution.py:91
  337.6 6.5 %all-to-all-start.3 = ((bf16[16,54,2048]{2,1,0:T(8,128)(2,1)}), bf16[16,54,2048]{2,1,0:T(8,128)(2,1)}, u32[]{:S(2)}, u32[]{:S(2)}) async-start(bf16[16,54,2048]{2,1,0:T(8,128)(2,1)} %reshape.112), calls=%async_computation.4 | async-start | bytes 7340032 | tf_op jit(solution)/shard_map/all_to_all | solution.py:90
  344.1 0.5 all-gather.8.cloned.1.call-update
  344.7 0.1 reshape.115
  344.8 5.0 %gather_fusion.3 = bf16[768]{0:T(1024)(128)(2,1)S(1)} fusion(bf16[864]{0:T(1024)(128)(2,1)S(1)} %reshape.115, s32[1024]{0:T(1024)S(1)} %pad_clamp_fusion), kind=kCustom, calls=%fused_computation.3 | custom fusion | bytes 6144 | tf_op jit(solution)/shard_map/gather | solution.py:121
  349.8 0.1 reshape.116
  349.9 0.7 copy.30
  350.5 7.3 %fusion.12 = bf16[1,2048,768]{2,1,0:T(8,128)(2,1)} fusion(bf16[864,2048]{1,0:T(8,128)(2,1)} %reshape.109, bf16[864,768]{1,0:T(8,128)(2,1)S(1)} %copy-done.9), kind=kOutput, calls=%fused_computation.24 | convolution fusion | flops 2719481856 | bytes 8011776 | tf_op jit(solution)/shard_map/dot_general | solution.py:111
  357.9 4.9 %fusion.13 = bf16[1,2048,768]{2,1,0:T(8,128)(2,1)} fusion(bf16[864,2048]{1,0:T(8,128)(2,1)S(1)} %copy-done.3, bf16[864,768]{1,0:T(8,128)(2,1)S(1)} %copy-done.10), kind=kOutput, calls=%fused_computation.25 | convolution fusion | flops 2719481856 | bytes 8011776 | tf_op jit(solution)/shard_map/dot_general | solution.py:114
  362.8 8.0 %all-gather.8.cloned.1.call-done = bf16[864,768]{1,0:T(8,128)(2,1)} async-done(((bf16[432,768]{1,0:T(8,128)(2,1)}), bf16[864,768]{1,0:T(8,128)(2,1)}) %all-gather.8.cloned.1.call-update) | async-done | bytes 1327120 | tf_op jit(solution)/shard_map/all_gather | solution.py:80
  370.8 7.7 %fusion.14 = bf16[1,768,2048]{2,1,0:T(8,128)(2,1)} fusion(bf16[864,768]{1,0:T(8,128)(2,1)} %all-gather.8.cloned.1.call-done, bf16[864,2048]{1,0:T(8,128)(2,1)} %reshape.111, f32[864]{0:T(1024)S(1)} %convert_element_type.59), kind=kOutput, calls=%fused_computation.26 | convolution fusion | flops 2724790272 | bytes 8015232 | tf_op jit(solution)/shard_map/dot_general | solution.py:108
  378.5 46.8 %all-to-all-done.3 = bf16[16,54,2048]{2,1,0:T(8,128)(2,1)} async-done(((bf16[16,54,2048]{2,1,0:T(8,128)(2,1)}), bf16[16,54,2048]{2,1,0:T(8,128)(2,1)}, u32[]{:S(2)}, u32[]{:S(2)}) %all-to-all-start.3) | async-done | bytes 3538976 | tf_op jit(solution)/shard_map/all_to_all | solution.py:90
  425.3 4.7 %reshape.113 = bf16[864,2048]{1,0:T(8,128)(2,1)} reshape(bf16[16,54,2048]{2,1,0:T(8,128)(2,1)} %all-to-all-done.3) | data formatting | bytes 7077888 | tf_op jit(solution)/shard_map/reshape | solution.py:117
  430.0 9.7 %gather_fusion.2 = bf16[768,2048]{1,0:T(8,128)(2,1)} fusion(bf16[864,2048]{1,0:T(8,128)(2,1)} %reshape.113, s32[1024]{0:T(1024)S(1)} %pad_clamp_fusion), kind=kCustom, calls=%fused_computation.2 | custom fusion | bytes 6294528 | tf_op jit(solution)/shard_map/gather | solution.py:117
  439.8 4.8 %bitcast_reduce_fusion = bf16[96,2048]{1,0:T(8,128)(2,1)} fusion(bf16[768,2048]{1,0:T(8,128)(2,1)} %gather_fusion.2), kind=kLoop, calls=%fused_computation.14 | loop fusion | flops 1376256 | bytes 3538944 | tf_op jit(solution)/shard_map/reduce_sum | solution.py:120
  (39 shorter events, 0.3 us)
Async XLA Ops:
  7.2 120.6 %copy-start = (bf16[1,2048,768]{2,1,0:T(8,128)(2,1)S(1)}, bf16[1,2048,768]{2,1,0:T(8,128)(2,1)}, u32[]{:S(2)}) copy-start(bf16[1,2048,768]{2,1,0:T(8,128)(2,1)} %param.11) | copy-start | bytes 9437188
  29.8 6.7 %copy-start.6 = (bf16[96,2048]{1,0:T(8,128)(2,1)S(1)}, bf16[96,2048]{1,0:T(8,128)(2,1)}, u32[]{:S(2)}) copy-start(bf16[96,2048]{1,0:T(8,128)(2,1)} %param.8) | copy-start | bytes 1179652
  29.8 87.9 %all-to-all-start.1 = ((bf16[16,54,2048]{2,1,0:T(8,128)(2,1)}), bf16[16,54,2048]{2,1,0:T(8,128)(2,1)}, u32[]{:S(2)}, u32[]{:S(2)}) async-start(bf16[16,54,2048]{2,1,0:T(8,128)(2,1)} %reshape.108), calls=%async_computation.1 | async-start | bytes 7340032 | tf_op jit(solution)/shard_map/all_to_all | solution.py:54
  117.8 86.1 %all-to-all-start.2 = ((bf16[16,54,2048]{2,1,0:T(8,128)(2,1)}), bf16[16,54,2048]{2,1,0:T(8,128)(2,1)}, u32[]{:S(2)}, u32[]{:S(2)}) async-start(bf16[16,54,2048]{2,1,0:T(8,128)(2,1)} %reshape.110), calls=%async_computation.2 | async-start | bytes 7340032 | tf_op jit(solution)/shard_map/all_to_all | solution.py:55
  122.7 145.7 %reduce-scatter.2.cloned.1.call-start = ((), (), s32[]{:S(2)}) async-start(), calls=%async_computation.6 | async-start | bytes 5971968 | tf_op jit(solution)/shard_map/reduce_scatter | solution.py:70
  127.7 6.1 %copy-start.2 = (bf16[864,2048]{1,0:T(8,128)(2,1)S(1)}, bf16[864,2048]{1,0:T(8,128)(2,1)}, u32[]{:S(2)}) copy-start(bf16[864,2048]{1,0:T(8,128)(2,1)} %reshape.109) | copy-start | bytes 10616836
  127.7 6.1 %copy-start.8 = (bf16[1,2048,768]{2,1,0:T(8,128)(2,1)S(1)}, bf16[1,2048,768]{2,1,0:T(8,128)(2,1)}, u32[]{:S(2)}) copy-start(bf16[1,2048,768]{2,1,0:T(8,128)(2,1)} %param.12) | copy-start | bytes 9437188
  208.7 6.1 %copy-start.4 = (bf16[864,768]{1,0:T(8,128)(2,1)S(1)}, bf16[864,768]{1,0:T(8,128)(2,1)}, u32[]{:S(2)}) copy-start(bf16[864,768]{1,0:T(8,128)(2,1)} %fusion.15) | copy-start | bytes 3981316
  208.7 6.1 %copy-start.5 = (bf16[864,768]{1,0:T(8,128)(2,1)S(1)}, bf16[864,768]{1,0:T(8,128)(2,1)}, u32[]{:S(2)}) copy-start(bf16[864,768]{1,0:T(8,128)(2,1)} %fusion.18) | copy-start | bytes 3981316
  216.8 0.7 copy-start.7
  227.0 18.6 %all-to-all-start = ((bf16[16,1,54]{2,1,0:T(2,128)(2,1)}), bf16[16,1,54]{2,1,0:T(2,128)(2,1)S(1)}, u32[]{:S(2)}, u32[]{:S(2)}) async-start(bf16[16,1,54]{2,1,0:T(2,128)(2,1)} %all_to_all.28), calls=%async_computation | async-start | bytes 16384 | tf_op jit(solution)/shard_map/all_to_all | solution.py:56
  231.9 65.1 %all-gather.4.cloned.1.call-start = ((), (), s32[]{:S(2)}) async-start(), calls=%async_computation.7 | async-start | bytes 1990656 | tf_op jit(solution)/shard_map/all_gather | solution.py:81
  270.2 2.9 copy-start.11
  272.4 51.2 %all-gather.6.cloned.1.call-start = ((), (), s32[]{:S(2)}) async-start(), calls=%async_computation.8 | async-start | bytes 1990656 | tf_op jit(solution)/shard_map/all_gather | solution.py:82
  279.1 58.4 %all-to-all-start.4 = ((bf16[16,1,54]{2,1,0:T(2,128)(2,1)}), bf16[16,1,54]{2,1,0:T(2,128)(2,1)S(1)}, u32[]{:S(2)}, u32[]{:S(2)}) async-start(bf16[16,1,54]{2,1,0:T(2,128)(2,1)} %all_to_all.29), calls=%async_computation.5 | async-start | bytes 16384 | tf_op jit(solution)/shard_map/all_to_all | solution.py:97
  337.6 13.0 %copy-start.9 = (bf16[864,768]{1,0:T(8,128)(2,1)S(1)}, bf16[864,768]{1,0:T(8,128)(2,1)}, u32[]{:S(2)}) copy-start(bf16[864,768]{1,0:T(8,128)(2,1)} %all-gather.4.cloned.1.call-done) | copy-start | bytes 3981316
  337.6 87.7 %all-to-all-start.3 = ((bf16[16,54,2048]{2,1,0:T(8,128)(2,1)}), bf16[16,54,2048]{2,1,0:T(8,128)(2,1)}, u32[]{:S(2)}, u32[]{:S(2)}) async-start(bf16[16,54,2048]{2,1,0:T(8,128)(2,1)} %reshape.112), calls=%async_computation.4 | async-start | bytes 7340032 | tf_op jit(solution)/shard_map/all_to_all | solution.py:90
  344.1 26.8 %all-gather.8.cloned.1.call-start = ((), (), s32[]{:S(2)}) async-start(), calls=%async_computation.9 | async-start | bytes 1990656 | tf_op jit(solution)/shard_map/all_gather | solution.py:80
  350.5 7.3 %copy-start.3 = (bf16[864,2048]{1,0:T(8,128)(2,1)S(1)}, bf16[864,2048]{1,0:T(8,128)(2,1)}, u32[]{:S(2)}) copy-start(bf16[864,2048]{1,0:T(8,128)(2,1)} %reshape.109) | copy-start | bytes 10616836
  350.5 7.3 %copy-start.10 = (bf16[864,768]{1,0:T(8,128)(2,1)S(1)}, bf16[864,768]{1,0:T(8,128)(2,1)}, u32[]{:S(2)}) copy-start(bf16[864,768]{1,0:T(8,128)(2,1)} %all-gather.6.cloned.1.call-done) | copy-start | bytes 3981316
  430.0 14.5 %copy-start.1 = (bf16[1,2048,768]{2,1,0:T(8,128)(2,1)S(1)}, bf16[1,2048,768]{2,1,0:T(8,128)(2,1)}, u32[]{:S(2)}) copy-start(bf16[1,2048,768]{2,1,0:T(8,128)(2,1)} %param.11) | copy-start | bytes 9437188
Sparse Core Ops, SparseCore 0:
  216.9 51.4 reduce-scatter.1
  272.5 24.4 all-gather.3
  299.1 24.4 all-gather.5
  346.7 24.0 all-gather.7
where the time goes:
time: 458 us; the launch traced here: 451 us
  waiting for transfers between devices  241 us (53%)
  local copies, waits for them, and re-layouts  82 us (18%)
  matrix products  51.4 us (11%)
  starting transfers between devices  44.6 us (10%)
  between operations  14.8 us (3%)
  other arithmetic  13.4 us (3%)
    all_to_all x1, waiting for transfers between devices, local(): lax.all_to_all(send_dy, 'expert', split_axis=0, concat_axis=0, tiled=True)  66.1 us
    all_to_all x1, waiting for transfers between devices, local(): lax.all_to_all(send_x, 'expert', split_axis=0, concat_axis=0, tiled=True)  65.9 us
    all_to_all x1, waiting for transfers between devices, local(): lax.all_to_all(row_grad.reshape(expert_count, capacity, quarter), 'expert...  46.8 us
    reduce_scatter x1, waiting for transfers between devices, local(): lax.psum_scatter(jnp.concatenate([gate_part, up_part, down_part], axis=1)...  22.6 us
    all_gather x1, waiting for transfers between devices, local(): lax.all_gather(part_up, 'seq', axis=0, tiled=True)  20.4 us
    all_gather x1, starting transfers between devices, local(): lax.all_gather(part_gate, 'seq', axis=0, tiled=True)  13.7 us
    all_gather x1, waiting for transfers between devices, local(): lax.all_gather(part_gate, 'seq', axis=0, tiled=True)  10.4 us
    gather x1, local copies, waits for them, and re-layouts, local(): jnp.concatenate([tokens, zero_row], axis=0)[token_of]  9.8 us
  transfers between devices with their start and end apart: 9, of which 7 were waited for; matrix products, arithmetic and copies ran while one was open for 19% of the time, Pallas kernels for 0%

commit v1 on v0

v1 whole, which is shorter than its diff:
```python
import functools

import jax
import jax.numpy as jnp
from jax import lax
from jax.experimental import pallas as pl
from jax.experimental.pallas import tpu as pltpu
from jax.sharding import PartitionSpec as P

BF = jnp.bfloat16
F32 = jnp.float32
LANES = 128
LAST = (((1,), (1,)), ((), ()))


def dot(a, b):
    return jnp.dot(a, b, preferred_element_type=F32)


def round_up(n, m):
    return -(-n // m) * m


def forward_kernel(inner, cap, tok, feat, hid, tile, *refs):
    blocks = refs[:inner]
    wg, wu, wd = refs[inner : inner + 3]
    parts, x_all, sd_all, st_out, grow_out = refs[-9:-4]
    cat, x_s, dy_s, lower = refs[-4:]
    rows = inner * cap
    pad = x_s.shape[0]
    step = pl.program_id(0)

    @pl.when(step == 0)
    def _():
        me = lax.axis_index("expert")
        mine = (lax.broadcasted_iota(jnp.int32, (tok, LANES), 1) == me).astype(F32)
        r = lax.broadcasted_iota(jnp.int32, (tok, tok), 0)
        c = lax.broadcasted_iota(jnp.int32, (tok, tok), 1)
        lower[...] = (c < r).astype(F32).astype(BF)
        slot_of = lax.broadcasted_iota(jnp.int32, (tok, pad), 1)
        st = []
        gates = []
        for b in range(inner):
            cat[b * tok : (b + 1) * tok, :] = blocks[b][:, : 2 * feat]
            table = blocks[b][:, 2 * feat :].astype(F32)
            gate = jnp.sum(table * mine, axis=1, keepdims=True)
            chosen = gate >= 0.0
            flag = jnp.broadcast_to(chosen.astype(F32), (tok, LANES))
            before = dot(lower[...], flag.astype(BF))[:, :1]
            place = jnp.where(chosen, before.astype(jnp.int32) + b * cap, -1)
            st.append((slot_of == place).astype(F32))
            gates.append(jnp.broadcast_to(gate, (tok, LANES)).astype(BF))
        st = jnp.concatenate(st, axis=0)
        gates = jnp.concatenate(gates, axis=0)
        st_out[...] = st.astype(BF)
        pick = st.T.astype(BF)
        grow = dot(pick, gates)
        grow_out[...] = grow.astype(BF)
        x = dot(pick, cat[:, :feat]).astype(BF)
        x_s[...] = x
        x_all[...] = x
        dy = dot(pick, cat[:, feat:])
        dy_s[...] = dy.astype(BF)
        sd_all[...] = (grow[:, :1] * dy).astype(BF)

    off = pl.multiple_of(step * tile, tile)
    parts[:, pl.ds(off, tile)] = dot(x_s[...], wg[...])[:rows].astype(BF)
    parts[:, pl.ds(hid + off, tile)] = dot(x_s[...], wu[...])[:rows].astype(BF)
    back = lax.dot_general(dy_s[...], wd[...], LAST, preferred_element_type=F32)
    parts[:, pl.ds(2 * hid + off, tile)] = back[:rows].astype(BF)


def forward_call(index, count, blocks, wg, wu, wd, cap, slabs):
    inner = len(blocks)
    tok = blocks[0].shape[0]
    feat, hid = wg.shape
    tile = 256 if hid % 256 == 0 else hid
    rows = inner * cap
    pad = round_up(rows, 16)
    whole = lambda shape: pl.BlockSpec(shape, lambda i: (0,) * len(shape))
    slab = lambda width: pl.BlockSpec((pad, width), lambda i: (index, 0))
    in_specs = [whole(b.shape) for b in blocks] + [
        pl.BlockSpec((feat, tile), lambda i: (0, i)),
        pl.BlockSpec((feat, tile), lambda i: (0, i)),
        pl.BlockSpec((tile, feat), lambda i: (i, 0)),
    ]
    args = list(blocks) + [wg, wu, wd]
    aliases = {}
    if slabs is not None:
        aliases = {len(args): 1, len(args) + 1: 2}
        args += list(slabs)
        in_specs += [pl.BlockSpec(memory_space=pl.ANY)] * 2
    return pl.pallas_call(
        functools.partial(forward_kernel, inner, cap, tok, feat, hid, tile),
        grid=(hid // tile,),
        in_specs=in_specs,
        out_specs=[
            whole((rows, 3 * hid)),
            slab(feat),
            slab(feat),
            whole((inner * tok, pad)),
            whole((pad, LANES)),
        ],
        out_shape=[
            jax.ShapeDtypeStruct((rows, 3 * hid), BF),
            jax.ShapeDtypeStruct((count * pad, feat), BF),
            jax.ShapeDtypeStruct((count * pad, feat), BF),
            jax.ShapeDtypeStruct((inner * tok, pad), BF),
            jax.ShapeDtypeStruct((pad, LANES), BF),
        ],
        scratch_shapes=[
            pltpu.VMEM((inner * tok, 2 * feat), BF),
            pltpu.VMEM((pad, feat), BF),
            pltpu.VMEM((pad, feat), BF),
            pltpu.VMEM((tok, tok), BF),
        ],
        input_output_aliases=aliases,
        compiler_params=pltpu.CompilerParams(vmem_limit_bytes=40 * 1024 * 1024),
        cost_estimate=pl.CostEstimate(
            flops=6 * pad * feat * hid + 4 * pad * inner * tok * feat,
            bytes_accessed=2 * (3 * feat * hid + 2 * inner * tok * feat + 2 * pad * feat + 3 * pad * hid),
            transcendentals=0,
        ),
    )(*args)


def backward_kernel(inner, tok, feat, hid, tile, n_parts, *refs):
    parts = refs[:n_parts]
    st, grow, wg, wu = refs[n_parts : n_parts + 4]
    keep, send, act_all, pg_all, pu_all = refs[-7:-2]
    pg_s, pu_s = refs[-2:]
    rows = parts[0].shape[0]
    pad = pg_s.shape[0]
    half = inner // 2
    step = pl.program_id(0)

    def spread(value, column, width):
        for b in range(inner):
            piece = value[b * tok : (b + 1) * tok]
            target = keep if b % 2 == 0 else send
            target[b // 2, :, pl.ds(column, width)] = piece

    @pl.when(step == 0)
    def _():
        def total(at):
            out = parts[0][:, at * hid : (at + 1) * hid].astype(F32)
            for part in parts[1:]:
                out = out + part[:, at * hid : (at + 1) * hid].astype(F32)
            return out

        def full(value):
            if pad > rows:
                value = jnp.concatenate([value, jnp.zeros((pad - rows, value.shape[1]), F32)], axis=0)
            return value

        gate_pre = total(0)
        sig = 1.0 / (1.0 + jnp.exp(-gate_pre))
        silu = gate_pre * sig
        up = total(1)
        act = silu * up
        back = total(2)
        slot = jnp.sum(act * back, axis=1, keepdims=True)
        act_grad = grow[:rows, :1].astype(F32) * back
        pre_gate = act_grad * up * sig * (1.0 + gate_pre * (1.0 - sig))
        pre_up = act_grad * silu
        act_all[...] = full(act).astype(BF)
        pg = full(pre_gate).astype(BF)
        pu = full(pre_up).astype(BF)
        pg_all[...] = pg
        pu_all[...] = pu
        pg_s[...] = pg
        pu_s[...] = pu
        me = lax.axis_index("expert")
        mine = (lax.broadcasted_iota(jnp.int32, (rows, LANES), 1) == me).astype(F32)
        slots = full(slot * mine).astype(BF)
        spread(dot(st[...], slots).astype(BF), feat, LANES)

    off = pl.multiple_of(step * tile, tile)
    grad = lax.dot_general(pg_s[...], wg[...], LAST, preferred_element_type=F32)
    grad = grad + lax.dot_general(pu_s[...], wu[...], LAST, preferred_element_type=F32)
    spread(dot(st[...], grad.astype(BF)).astype(BF), off, tile)


def backward_call(index, count, parts, st, grow, wg, wu, tok, slabs):
    feat, hid = wg.shape
    tile = 512 if feat % 512 == 0 else feat
    inner = st.shape[0] // tok
    pad = st.shape[1]
    rows = parts[0].shape[0]
    wide = feat + LANES
    whole = lambda shape: pl.BlockSpec(shape, lambda i: (0,) * len(shape))
    slab = pl.BlockSpec((pad, hid), lambda i: (index, 0))
    weight = pl.BlockSpec((tile, hid), lambda i: (i, 0))
    args = list(parts) + [st, grow, wg, wu]
    in_specs = [whole(a.shape) for a in args[:-2]] + [weight, weight]
    aliases = {}
    if slabs is not None:
        aliases = {len(args) + i: 2 + i for i in range(3)}
        args += list(slabs)
        in_specs += [pl.BlockSpec(memory_space=pl.ANY)] * 3
    half = jax.ShapeDtypeStruct((inner // 2, tok, wide), BF)
    saved = jax.ShapeDtypeStruct((count * pad, hid), BF)
    return pl.pallas_call(
        functools.partial(backward_kernel, inner, tok, feat, hid, tile, len(parts)),
        grid=(feat // tile,),
        in_specs=in_specs,
        out_specs=[whole(half.shape), whole(half.shape), slab, slab, slab],
        out_shape=[half, half, saved, saved, saved],
        scratch_shapes=[pltpu.VMEM((pad, hid), BF), pltpu.VMEM((pad, hid), BF)],
        input_output_aliases=aliases,
        compiler_params=pltpu.CompilerParams(vmem_limit_bytes=40 * 1024 * 1024),
        cost_estimate=pl.CostEstimate(
            flops=4 * pad * feat * hid + 2 * pad * inner * tok * feat,
            bytes_accessed=2 * (2 * feat * hid + inner * tok * feat + 9 * pad * hid),
            transcendentals=pad * hid,
        ),
    )(*args)


def local(tokens, cotangent, expert_ids, gate_values, gate_weight, up_weight, down_weight):
    experts = lax.axis_size("expert")
    seqs = lax.axis_size("seq")
    tok, feat = tokens.shape
    top = expert_ids.shape[1]
    cap = min(tok, tok * top // experts + tok * top // (8 * experts))
    inner = 2 * seqs if experts % (2 * seqs) == 0 else 2
    columns = inner // 2
    planes = experts // inner

    def split(i):
        return i // inner, (i % inner) // 2, i % 2

    def join(z, y, c):
        return (z % planes) * inner + (y % columns) * 2 + c

    def shift(dz=0, dy=0, dc=0):
        out = []
        for i in range(experts):
            z, y, c = split(i)
            out.append((i, join(z + dz, y + dy, c ^ dc)))
        return out

    def move(x, **by):
        return lax.ppermute(x, "expert", shift(**by))

    wg, wu, wd = gate_weight[0], up_weight[0], down_weight[0]
    lanes = jnp.arange(LANES, dtype=jnp.int32)
    hit = expert_ids[:, :, None] == lanes
    chosen = jnp.any(hit, axis=1)
    table = jnp.sum(jnp.where(hit, gate_values[:, :, None].astype(F32), 0.0), axis=1)
    table = jnp.where(chosen, table, -1.0).astype(BF)
    block = jnp.concatenate([tokens, cotangent, table], axis=1)

    planes_in = [block] + [move(block, dz=k) for k in range(1, planes)]
    x_slab = act_slab = None
    totals = None
    for k in range(planes):
        mine = [planes_in[k]] + [move(planes_in[k], dy=j) for j in range(1, columns)]
        theirs = [move(b, dc=1) for b in mine]
        blocks = [b for pair in zip(mine, theirs) for b in pair]
        part, xs, sds, st, grow = forward_call(k, planes, blocks, wg, wu, wd, cap, x_slab)
        x_slab = (xs, sds)
        if seqs == 2:
            parts = [part, lax.ppermute(part, "seq", [(0, 1), (1, 0)])]
        else:
            gathered = lax.all_gather(part, "seq", axis=0)
            parts = [gathered[i] for i in range(seqs)]
        keep, send, *act_slab = backward_call(k, planes, parts, st, grow, wg, wu, tok, act_slab)
        got = move(send, dc=1)
        both = (keep.astype(F32) + got.astype(F32)).astype(BF)
        summed = both[0].astype(F32)
        for j in range(1, columns):
            summed = summed + move(both[j], dy=-j).astype(F32)
        if k:
            summed = move(summed.astype(BF), dz=-k).astype(F32)
        totals = summed if totals is None else totals + summed

    input_grad = totals[:, :feat].astype(BF)
    slots = totals[:, feat:]
    gate_grad = jnp.sum(jnp.where(hit, slots[:, None, :], 0.0), axis=2).astype(BF)
    contract_rows = (((0,), (0,)), ((), ()))
    wgrad = lambda a, b: lax.dot_general(a, b, contract_rows, preferred_element_type=F32).astype(BF)[None]
    x_all, sd_all = x_slab
    act_all, pg_all, pu_all = act_slab
    return (
        input_grad,
        gate_grad,
        wgrad(x_all, pg_all),
        wgrad(x_all, pu_all),
        wgrad(act_all, sd_all),
    )


def solution(mesh):
    in_specs = (
        P("expert", "seq"),
        P("expert", "seq"),
        P("expert", None),
        P("expert", None),
        P("expert", "seq", None),
        P("expert", "seq", None),
        P("expert", None, "seq"),
    )
    out_specs = (
        P("expert", "seq"),
        P("expert", None),
        P("expert", "seq", None),
        P("expert", "seq", None),
        P("expert", None, "seq"),
    )
    return jax.shard_map(local, mesh=mesh, in_specs=in_specs, out_specs=out_specs, check_vma=False)
```

time: 458 us -> 285 us (0.62)
  the two profiles are of different devices: /device:TPU:13 before, /device:TPU:0 now
where the time goes in v1:
time: 285 us; the launch traced here: 284 us
  waiting for transfers between devices  164 us (58%)
  Pallas kernels  47.8 us (17%)
  starting transfers between devices  26.9 us (9%)
  local copies, waits for them, and re-layouts  24.6 us (9%)
  matrix products  17.1 us (6%)
  other arithmetic  3.37 us (1%)
    ppermute x26, waiting for transfers between devices, move(): return lax.ppermute(x, 'expert', shift(**by))  125 us
    ppermute x4, waiting for transfers between devices, local(): parts = [part, lax.ppermute(part, 'seq', [(0, 1), (1, 0)])]  39.2 us
    pallas_call x4, Pallas kernels, forward_call(): pl.pallas_call(functools.partial(forward_kernel, inner, cap, tok, feat, h...  28.3 us
    unnamed x58, local copies, waits for them, and re-layouts  22.9 us
    ppermute x26, starting transfers between devices, move(): return lax.ppermute(x, 'expert', shift(**by))  22.8 us
    pallas_call x4, Pallas kernels, backward_call(): pl.pallas_call(functools.partial(backward_kernel, inner, tok, feat, hid,...  19.5 us
    dot_general x3, matrix products, local(): lax.dot_general(a, b, contract_rows, preferred_element_type=F32).astype(BF)  17.1 us
  transfers between devices with their start and end apart: 30, of which 12 were waited for; matrix products, arithmetic and copies ran while one was open for 6% of the time, Pallas kernels for 17%

profile of v1, /device:TPU:0, one launch (start us, length us, event | category | flops | bytes accessed | tf_op | source)
XLA Modules:
  0.0 284.4 jit_solution(11530989496472691579)
XLA Ops:
  0.6 0.8 copy.29
  1.6 0.8 copy.30
  2.7 1.2 pad_maximum_fusion.refs_0_
  3.9 3.1 %collective-permute-start.6 = (bf16[96,4224]{1,0:T(8,128)(2,1)S(1)}, bf16[96,4224]{1,0:T(8,128)(2,1)S(1)}, u32[]{:S(2)}, u32[]{:S(2)}) collective-permute-start(bf16[96,4224]{1,0:T(8,128)(2,1)S(1)} %pad_maximum_fusion.refs_0_), channel_id=1, source_target_pairs={{0,8},{2,10},{4,12},{6,14},{8,16},{10,18},{12,20},{14,22},{16,24},... | collective-permute-start | bytes 2433032 | tf_op jit(solution)/shard_map/ppermute | solution.py:244
  7.0 2.1 collective-permute-start.22
  9.1 0.9 collective-permute-start.14
  10.0 1.5 collective-permute-start.1
  11.5 16.4 %collective-permute-done.6.refs_0_ = bf16[96,4224]{1,0:T(8,128)(2,1)S(1)} collective-permute-done((bf16[96,4224]{1,0:T(8,128)(2,1)S(1)}, bf16[96,4224]{1,0:T(8,128)(2,1)S(1)}, u32[]{:S(2)}, u32[]{:S(2)}) %collective-permute-start.6) | collective-permute-done | bytes 811040 | tf_op jit(solution)/shard_map/ppermute | solution.py:244
  27.9 1.8 collective-permute-start.8
  29.7 14.2 %collective-permute-done.22.refs_0_ = bf16[96,4224]{1,0:T(8,128)(2,1)S(1)} collective-permute-done((bf16[96,4224]{1,0:T(8,128)(2,1)S(1)}, bf16[96,4224]{1,0:T(8,128)(2,1)S(1)}, u32[]{:S(2)}, u32[]{:S(2)}) %collective-permute-start.22) | collective-permute-done | bytes 811040 | tf_op jit(solution)/shard_map/ppermute | solution.py:244
  43.9 1.5 collective-permute-start.24
  45.4 33.9 %collective-permute-done.14.refs_0_ = bf16[96,4224]{1,0:T(8,128)(2,1)} collective-permute-done((bf16[96,4224]{1,0:T(8,128)(2,1)S(1)}, bf16[96,4224]{1,0:T(8,128)(2,1)}, u32[]{:S(2)}, u32[]{:S(2)}) %collective-permute-start.14) | collective-permute-done | bytes 811040 | tf_op jit(solution)/shard_map/ppermute | solution.py:244
  79.3 1.5 collective-permute-start.16
  80.8 0.9 copy-done.14
  81.7 0.9 copy-done.10
  83.1 0.9 copy-done.16
  84.5 15.1 %collective-permute-done.16.refs_2_ = bf16[96,4224]{1,0:T(8,128)(2,1)} collective-permute-done((bf16[96,4224]{1,0:T(8,128)(2,1)}, bf16[96,4224]{1,0:T(8,128)(2,1)}, u32[]{:S(2)}, u32[]{:S(2)}) %collective-permute-start.16) | collective-permute-done | bytes 811040 | tf_op jit(solution)/shard_map/ppermute | solution.py:244
  99.6 0.9 copy-done.12
  101.0 0.9 copy-done.18
  101.9 1.9 copy-done
  103.8 1.9 copy-done.2
  105.7 1.9 copy-done.4
  107.6 1.1 copy-done.15
  108.7 1.1 copy-done.17
  109.9 1.1 copy-done.19
  111.0 6.2 %shard_map.110 = (bf16[216,2304]{1,0:T(8,128)(2,1)}, bf16[896,2048]{1,0:T(8,128)(2,1)}, bf16[896,2048]{1,0:T(8,128)(2,1)}, bf16[384,224]{1,0:T(8,128)(2,1)S(1)}, bf16[224,128]{1,0:T(8,128)(2,1)S(1)}) custom-call(bf16[96,4224]{1,0:T(8,128)(2,1)S(1)} %pad_maximum_fusion.refs_0_, bf16[96,4224]{1,0:T(8,128)(2,1)S(1)} %copy-done.15, ...), custom_call_target="tpu_custom_call" | custom-call | flops 2818572288 | bytes 15450112 | tf_op jit(solution)/shard_map/pallas_call | solution.py:93
  117.3 1.5 collective-permute-start.3
  118.8 1.1 copy-done.11
  119.9 1.1 copy-done.13
  121.0 7.1 %shard_map.112 = (bf16[216,2304]{1,0:T(8,128)(2,1)S(1)}, bf16[896,2048]{1,0:T(8,128)(2,1)}, bf16[896,2048]{1,0:T(8,128)(2,1)}, bf16[384,224]{1,0:T(8,128)(2,1)S(1)}, bf16[224,128]{1,0:T(8,128)(2,1)S(1)}) custom-call(bf16[96,4224]{1,0:T(8,128)(2,1)S(1)} %copy-done.11, bf16[96,4224]{1,0:T(8,128)(2,1)S(1)} %copy-done.13, ...), custom_call_target="tpu_custom_call", output_to_operand_aliasing={{1}: (7, {}), {2}: (8, {})} | custom-call | flops 2818572288 | bytes 15450112 | tf_op jit(solution)/shard_map/pallas_call | solution.py:93
  128.1 0.5 collective-permute-start.10
  128.7 7.6 %shard_map.114 = (bf16[216,2304]{1,0:T(8,128)(2,1)S(1)}, bf16[896,2048]{1,0:T(8,128)(2,1)}, bf16[896,2048]{1,0:T(8,128)(2,1)}, bf16[384,224]{1,0:T(8,128)(2,1)S(1)}, bf16[224,128]{1,0:T(8,128)(2,1)S(1)}) custom-call(bf16[96,4224]{1,0:T(8,128)(2,1)} %collective-permute-done.14.refs_0_, ...), custom_call_target="tpu_custom_call", output_to_operand_aliasing={{1}: (7, {}), {2}: (8, {})} | custom-call | flops 2818572288 | bytes 15450112 | tf_op jit(solution)/shard_map/pallas_call | solution.py:93
  136.3 1.5 collective-permute-start.18
  137.8 7.4 %shard_map.116 = (bf16[216,2304]{1,0:T(8,128)(2,1)S(1)}, bf16[896,2048]{1,0:T(8,128)(2,1)}, bf16[896,2048]{1,0:T(8,128)(2,1)}, bf16[384,224]{1,0:T(8,128)(2,1)S(1)}, bf16[224,128]{1,0:T(8,128)(2,1)S(1)}) custom-call(bf16[96,4224]{1,0:T(8,128)(2,1)S(1)} %collective-permute-done.22.refs_0_, ...), custom_call_target="tpu_custom_call", output_to_operand_aliasing={{1}: (7, {}), {2}: (8, {})} | custom-call | flops 2818572288 | bytes 15450112 | tf_op jit(solution)/shard_map/pallas_call | solution.py:93
  145.2 0.7 copy-done.20
  145.9 0.6 copy-done.22
  147.0 0.9 copy-done.8
  148.0 1.2 copy-done.9
  149.2 5.5 %shard_map.111 = (bf16[2,96,2176]{2,1,0:T(8,128)(2,1)S(1)}, bf16[2,96,2176]{2,1,0:T(8,128)(2,1)S(1)}, bf16[896,768]{1,0:T(8,128)(2,1)S(1)}, bf16[896,768]{1,0:T(8,128)(2,1)S(1)}, bf16[896,768]{1,0:T(8,128)(2,1)S(1)}) custom-call(bf16[216,2304]{1,0:T(8,128)(2,1)} %get-tuple-element.45.refs_0_, bf16[216,2304]{1,0:T(8,128)(2,1)S(1)} %copy-done.9, ...), custom_call_target="tpu_custom_call" | custom-call | flops 1761607680 | bytes 10960896 | tf_op jit(solution)/shard_map/pallas_call | solution.py:203
  154.7 8.9 %collective-permute-done.10.refs_1_ = bf16[216,2304]{1,0:T(8,128)(2,1)S(1)} collective-permute-done((bf16[216,2304]{1,0:T(8,128)(2,1)S(1)}, bf16[216,2304]{1,0:T(8,128)(2,1)S(1)}, u32[]{:S(2)}, u32[]{:S(2)}) %collective-permute-start.10) | collective-permute-done | bytes 995360 | tf_op jit(solution)/shard_map/ppermute | solution.py:264
  163.6 0.9 copy-done.6
  164.6 1.2 copy-done.7
  165.8 4.3 %shard_map.113 = (bf16[2,96,2176]{2,1,0:T(8,128)(2,1)S(1)}, bf16[2,96,2176]{2,1,0:T(8,128)(2,1)S(1)}, bf16[896,768]{1,0:T(8,128)(2,1)S(1)}, bf16[896,768]{1,0:T(8,128)(2,1)S(1)}, bf16[896,768]{1,0:T(8,128)(2,1)S(1)}) custom-call(bf16[216,2304]{1,0:T(8,128)(2,1)S(1)} %get-tuple-element.52.refs_0_, ...), custom_call_target="tpu_custom_call", output_to_operand_aliasing={{2}: (6, {}), {3}: (7, {}), {4}: (8, {})} | custom-call | flops 1761607680 | bytes 10960896 | tf_op jit(solution)/shard_map/pallas_call | solution.py:203
  170.1 15.0 %collective-permute-done.18.refs_1_ = bf16[216,2304]{1,0:T(8,128)(2,1)} collective-permute-done((bf16[216,2304]{1,0:T(8,128)(2,1)S(1)}, bf16[216,2304]{1,0:T(8,128)(2,1)}, u32[]{:S(2)}, u32[]{:S(2)}) %collective-permute-start.18) | collective-permute-done | bytes 995360 | tf_op jit(solution)/shard_map/ppermute | solution.py:264
  185.1 5.5 %shard_map.115 = (bf16[2,96,2176]{2,1,0:T(8,128)(2,1)S(1)}, bf16[2,96,2176]{2,1,0:T(8,128)(2,1)S(1)}, bf16[896,768]{1,0:T(8,128)(2,1)S(1)}, bf16[896,768]{1,0:T(8,128)(2,1)S(1)}, bf16[896,768]{1,0:T(8,128)(2,1)S(1)}) custom-call(bf16[216,2304]{1,0:T(8,128)(2,1)S(1)} %get-tuple-element.62.refs_0_, ...), custom_call_target="tpu_custom_call", output_to_operand_aliasing={{2}: (6, {}), {3}: (7, {}), {4}: (8, {})} | custom-call | flops 1761607680 | bytes 10960896 | tf_op jit(solution)/shard_map/pallas_call | solution.py:203
  190.6 15.3 %collective-permute-done.26.refs_1_ = bf16[216,2304]{1,0:T(8,128)(2,1)S(1)} collective-permute-done((bf16[216,2304]{1,0:T(8,128)(2,1)S(1)}, bf16[216,2304]{1,0:T(8,128)(2,1)S(1)}, u32[]{:S(2)}, u32[]{:S(2)}) %collective-permute-start.26) | collective-permute-done | bytes 995360 | tf_op jit(solution)/shard_map/ppermute | solution.py:264
  205.9 4.2 %shard_map.117 = (bf16[2,96,2176]{2,1,0:T(8,128)(2,1)S(1)}, bf16[2,96,2176]{2,1,0:T(8,128)(2,1)S(1)}, bf16[896,768]{1,0:T(8,128)(2,1)S(1)}, bf16[896,768]{1,0:T(8,128)(2,1)S(1)}, bf16[896,768]{1,0:T(8,128)(2,1)S(1)}) custom-call(bf16[216,2304]{1,0:T(8,128)(2,1)S(1)} %get-tuple-element.72.refs_0_, ...), custom_call_target="tpu_custom_call", output_to_operand_aliasing={{2}: (6, {}), {3}: (7, {}), {4}: (8, {})} | custom-call | flops 1761607680 | bytes 10960896 | tf_op jit(solution)/shard_map/pallas_call | solution.py:203
  210.8 7.4 %fusion = bf16[1,2048,768]{2,1,0:T(8,128)(2,1)} fusion(bf16[896,2048]{1,0:T(8,128)(2,1)} %get-tuple-element.80, bf16[896,768]{1,0:T(8,128)(2,1)S(1)} %get-tuple-element.81), kind=kOutput, calls=%fused_computation.3 | convolution fusion | flops 2820145152 | bytes 8192000 | tf_op jit(solution)/shard_map/dot_general | solution.py:282
  218.2 4.9 %fusion.1 = bf16[1,2048,768]{2,1,0:T(8,128)(2,1)} fusion(bf16[896,2048]{1,0:T(8,128)(2,1)S(1)} %copy-done.24, bf16[896,768]{1,0:T(8,128)(2,1)S(1)} %get-tuple-element.82), kind=kOutput, calls=%fused_computation.4 | convolution fusion | flops 2820145152 | bytes 8192000 | tf_op jit(solution)/shard_map/dot_general | solution.py:282
  223.3 1.6 collective-permute-start.5
  225.1 0.6 collective-permute-start.28
  225.9 1.6 collective-permute-start.20
  227.8 0.6 collective-permute-start.12
  228.4 16.4 %collective-permute-done.28 = bf16[96,2176]{1,0:T(8,128)(2,1)S(1)} collective-permute-done((bf16[96,2176]{1,0:T(8,128)(2,1)S(1)}, bf16[96,2176]{1,0:T(8,128)(2,1)S(1)}, u32[]{:S(2)}, u32[]{:S(2)}) %collective-permute-start.28) | collective-permute-done | bytes 417824 | tf_op jit(solution)/shard_map/ppermute | solution.py:244
  244.9 0.6 collective-permute-start.29
  245.5 8.2 %collective-permute-done.20 = bf16[96,2176]{1,0:T(8,128)(2,1)S(1)} collective-permute-done((bf16[96,2176]{1,0:T(8,128)(2,1)S(1)}, bf16[96,2176]{1,0:T(8,128)(2,1)S(1)}, u32[]{:S(2)}, u32[]{:S(2)}) %collective-permute-start.20) | collective-permute-done | bytes 417824 | tf_op jit(solution)/shard_map/ppermute | solution.py:244
  253.8 2.6 collective-permute-start.21
  256.4 5.8 %collective-permute-done.12 = bf16[96,2176]{1,0:T(8,128)(2,1)S(1)} collective-permute-done((bf16[96,2176]{1,0:T(8,128)(2,1)S(1)}, bf16[96,2176]{1,0:T(8,128)(2,1)S(1)}, u32[]{:S(2)}, u32[]{:S(2)}) %collective-permute-start.12) | collective-permute-done | bytes 417824 | tf_op jit(solution)/shard_map/ppermute | solution.py:244
  262.3 0.6 collective-permute-start.13
  262.9 4.8 %fusion.2 = bf16[1,768,2048]{2,1,0:T(8,128)(2,1)} fusion(bf16[896,768]{1,0:T(8,128)(2,1)S(1)} %get-tuple-element.83, bf16[896,2048]{1,0:T(8,128)(2,1)S(1)} %copy-done.25), kind=kOutput, calls=%fused_computation.5 | convolution fusion | flops 2820145152 | bytes 8192000 | tf_op jit(solution)/shard_map/dot_general | solution.py:282
  267.8 7.7 %collective-permute-done.21 = bf16[96,2176]{1,0:T(8,128)(2,1)S(1)} collective-permute-done((bf16[96,2176]{1,0:T(8,128)(2,1)S(1)}, bf16[96,2176]{1,0:T(8,128)(2,1)S(1)}, u32[]{:S(2)}, u32[]{:S(2)}) %collective-permute-start.21) | collective-permute-done | bytes 417824 | tf_op jit(solution)/shard_map/ppermute | solution.py:244
  275.5 6.9 %collective-permute-done.13 = bf16[96,2176]{1,0:T(8,128)(2,1)S(1)} collective-permute-done((bf16[96,2176]{1,0:T(8,128)(2,1)S(1)}, bf16[96,2176]{1,0:T(8,128)(2,1)S(1)}, u32[]{:S(2)}, u32[]{:S(2)}) %collective-permute-start.13) | collective-permute-done | bytes 417824 | tf_op jit(solution)/shard_map/ppermute | solution.py:244
  282.7 0.8 slice.68
  283.8 0.7 copy.31
  (85 shorter events, 5.2 us)
Async XLA Ops:
  1.4 100.5 %copy-start.26 = (s32[96,8]{1,0:T(8,128)}, s32[96,8]{1,0:T(8,128)S(1)}, u32[]{:S(2)}) copy-start(s32[96,8]{1,0:T(8,128)S(1)} %copy.29) | copy-start | bytes 9220
  3.9 24.0 %collective-permute-start.6 = (bf16[96,4224]{1,0:T(8,128)(2,1)S(1)}, bf16[96,4224]{1,0:T(8,128)(2,1)S(1)}, u32[]{:S(2)}, u32[]{:S(2)}) collective-permute-start(bf16[96,4224]{1,0:T(8,128)(2,1)S(1)} %pad_maximum_fusion.refs_0_), channel_id=1, source_target_pairs={{0,8},{2,10},{4,12},{6,14},{8,16},{10,18},{12,20},{14,22},{16,24},... | collective-permute-start | bytes 2433032 | tf_op jit(solution)/shard_map/ppermute | solution.py:244
  7.0 36.9 %collective-permute-start.22 = (bf16[96,4224]{1,0:T(8,128)(2,1)S(1)}, bf16[96,4224]{1,0:T(8,128)(2,1)S(1)}, u32[]{:S(2)}, u32[]{:S(2)}) collective-permute-start(bf16[96,4224]{1,0:T(8,128)(2,1)S(1)} %pad_maximum_fusion.refs_0_), channel_id=1, source_target_pairs={{0,24},{2,26},{4,28},{6,30},{8,0},{10,2},{12,4},{14,6},{16,8},{18,... | collective-permute-start | bytes 2433032 | tf_op jit(solution)/shard_map/ppermute | solution.py:244
  9.1 70.2 %collective-permute-start.14 = (bf16[96,4224]{1,0:T(8,128)(2,1)S(1)}, bf16[96,4224]{1,0:T(8,128)(2,1)}, u32[]{:S(2)}, u32[]{:S(2)}) collective-permute-start(bf16[96,4224]{1,0:T(8,128)(2,1)S(1)} %pad_maximum_fusion.refs_0_), channel_id=1, source_target_pairs={{0,16},{2,18},{4,20},{6,22},{8,24},{10,26},{12,28},{14,30},{16,0},... | collective-permute-start | bytes 2433032 | tf_op jit(solution)/shard_map/ppermute | solution.py:244
  10.0 70.8 %collective-permute-start = (bf16[96,4224]{1,0:T(8,128)(2,1)S(1)}, bf16[96,4224]{1,0:T(8,128)(2,1)S(1)}, u32[]{:S(2)}, u32[]{:S(2)}) collective-permute-start(bf16[96,4224]{1,0:T(8,128)(2,1)S(1)} %pad_maximum_fusion.refs_0_), channel_id=1, source_target_pairs={{0,2},{2,0},{4,6},{6,4},{8,10},{10,8},{12,14},{14,12},{16,18},{18,... | collective-permute-start | bytes 2433032 | tf_op jit(solution)/shard_map/ppermute | solution.py:244
  10.0 72.6 %collective-permute-start.1 = (bf16[96,4224]{1,0:T(8,128)(2,1)S(1)}, bf16[96,4224]{1,0:T(8,128)(2,1)S(1)}, u32[]{:S(2)}, u32[]{:S(2)}) collective-permute-start(bf16[96,4224]{1,0:T(8,128)(2,1)S(1)} %pad_maximum_fusion.refs_0_), channel_id=1, source_target_pairs={{0,4},{2,6},{4,0},{6,2},{8,12},{10,14},{12,8},{14,10},{16,20},{18,... | collective-permute-start | bytes 2433032 | tf_op jit(solution)/shard_map/ppermute | solution.py:244
  27.9 56.1 %collective-permute-start.8 = (bf16[96,4224]{1,0:T(8,128)(2,1)S(1)}, bf16[96,4224]{1,0:T(8,128)(2,1)}, u32[]{:S(2)}, u32[]{:S(2)}) collective-permute-start(bf16[96,4224]{1,0:T(8,128)(2,1)S(1)} %collective-permute-done.6.refs_0_), channel_id=1, source_target_pairs={{0,4},{2,6},{4,0},{6,2},{8,12},{10,14},{12,8},{14,10},{16,20},{18,... | collective-permute-start | bytes 2433032 | tf_op jit(solution)/shard_map/ppermute | solution.py:244
  43.9 40.2 %collective-permute-start.24 = (bf16[96,4224]{1,0:T(8,128)(2,1)S(1)}, bf16[96,4224]{1,0:T(8,128)(2,1)}, u32[]{:S(2)}, u32[]{:S(2)}) collective-permute-start(bf16[96,4224]{1,0:T(8,128)(2,1)S(1)} %collective-permute-done.22.refs_0_), channel_id=1, source_target_pairs={{0,4},{2,6},{4,0},{6,2},{8,12},{10,14},{12,8},{14,10},{16,20},{18,... | collective-permute-start | bytes 2433032 | tf_op jit(solution)/shard_map/ppermute | solution.py:244
  79.3 20.3 %collective-permute-start.16 = (bf16[96,4224]{1,0:T(8,128)(2,1)}, bf16[96,4224]{1,0:T(8,128)(2,1)}, u32[]{:S(2)}, u32[]{:S(2)}) collective-permute-start(bf16[96,4224]{1,0:T(8,128)(2,1)} %collective-permute-done.14.refs_0_), channel_id=1, source_target_pairs={{0,4},{2,6},{4,0},{6,2},{8,12},{10,14},{12,8},{14,10},{16,20},{18,... | collective-permute-start | bytes 2433032 | tf_op jit(solution)/shard_map/ppermute | solution.py:244
  80.8 0.9 copy-start.14
  81.7 17.9 %collective-permute-start.7 = (bf16[96,4224]{1,0:T(8,128)(2,1)S(1)}, bf16[96,4224]{1,0:T(8,128)(2,1)S(1)}, u32[]{:S(2)}, u32[]{:S(2)}) collective-permute-start(bf16[96,4224]{1,0:T(8,128)(2,1)S(1)} %collective-permute-done.6.refs_0_), channel_id=1, source_target_pairs={{0,2},{2,0},{4,6},{6,4},{8,10},{10,8},{12,14},{14,12},{16,18},{18,... | collective-permute-start | bytes 2433032 | tf_op jit(solution)/shard_map/ppermute | solution.py:244
  81.7 0.9 copy-start.10
  82.6 18.4 %collective-permute-start.2 = (bf16[96,4224]{1,0:T(8,128)(2,1)S(1)}, bf16[96,4224]{1,0:T(8,128)(2,1)S(1)}, u32[]{:S(2)}, u32[]{:S(2)}) collective-permute-start(bf16[96,4224]{1,0:T(8,128)(2,1)S(1)} %collective-permute-done.1.refs_2_), channel_id=1, source_target_pairs={{0,2},{2,0},{4,6},{6,4},{8,10},{10,8},{12,14},{14,12},{16,18},{18,... | collective-permute-start | bytes 2433032 | tf_op jit(solution)/shard_map/ppermute | solution.py:244
  83.1 0.9 copy-start.16
  84.0 33.2 %collective-permute-start.9 = (bf16[96,4224]{1,0:T(8,128)(2,1)}, bf16[96,4224]{1,0:T(8,128)(2,1)}, u32[]{:S(2)}, u32[]{:S(2)}) collective-permute-start(bf16[96,4224]{1,0:T(8,128)(2,1)} %collective-permute-done.8.refs_2_), channel_id=1, source_target_pairs={{0,2},{2,0},{4,6},{6,4},{8,10},{10,8},{12,14},{14,12},{16,18},{18,... | collective-permute-start | bytes 2433032 | tf_op jit(solution)/shard_map/ppermute | solution.py:244
  84.0 44.1 %collective-permute-start.15 = (bf16[96,4224]{1,0:T(8,128)(2,1)}, bf16[96,4224]{1,0:T(8,128)(2,1)}, u32[]{:S(2)}, u32[]{:S(2)}) collective-permute-start(bf16[96,4224]{1,0:T(8,128)(2,1)} %collective-permute-done.14.refs_0_), channel_id=1, source_target_pairs={{0,2},{2,0},{4,6},{6,4},{8,10},{10,8},{12,14},{14,12},{16,18},{18,... | collective-permute-start | bytes 2433032 | tf_op jit(solution)/shard_map/ppermute | solution.py:244
  99.6 29.1 %collective-permute-start.17 = (bf16[96,4224]{1,0:T(8,128)(2,1)}, bf16[96,4224]{1,0:T(8,128)(2,1)}, u32[]{:S(2)}, u32[]{:S(2)}) collective-permute-start(bf16[96,4224]{1,0:T(8,128)(2,1)} %collective-permute-done.16.refs_2_), channel_id=1, source_target_pairs={{0,2},{2,0},{4,6},{6,4},{8,10},{10,8},{12,14},{14,12},{16,18},{18,... | collective-permute-start | bytes 2433032 | tf_op jit(solution)/shard_map/ppermute | solution.py:244
  99.6 0.9 copy-start.12
  100.5 37.2 %collective-permute-start.23 = (bf16[96,4224]{1,0:T(8,128)(2,1)S(1)}, bf16[96,4224]{1,0:T(8,128)(2,1)}, u32[]{:S(2)}, u32[]{:S(2)}) collective-permute-start(bf16[96,4224]{1,0:T(8,128)(2,1)S(1)} %collective-permute-done.22.refs_0_), channel_id=1, source_target_pairs={{0,2},{2,0},{4,6},{6,4},{8,10},{10,8},{12,14},{14,12},{16,18},{18,... | collective-permute-start | bytes 2433032 | tf_op jit(solution)/shard_map/ppermute | solution.py:244
  101.0 0.9 copy-start.18
  101.9 35.8 %collective-permute-start.25 = (bf16[96,4224]{1,0:T(8,128)(2,1)}, bf16[96,4224]{1,0:T(8,128)(2,1)}, u32[]{:S(2)}, u32[]{:S(2)}) collective-permute-start(bf16[96,4224]{1,0:T(8,128)(2,1)} %collective-permute-done.24.refs_2_), channel_id=1, source_target_pairs={{0,2},{2,0},{4,6},{6,4},{8,10},{10,8},{12,14},{14,12},{16,18},{18,... | collective-permute-start | bytes 2433032 | tf_op jit(solution)/shard_map/ppermute | solution.py:244
  101.9 1.9 copy-start
  103.8 1.9 copy-start.2
  105.7 1.9 copy-start.4
  107.6 1.1 copy-start.15
  108.7 1.1 copy-start.17
  109.9 1.1 copy-start.19
  111.0 7.7 %copy-start.1 = (bf16[1,2048,768]{2,1,0:T(8,128)(2,1)S(1)}, bf16[1,2048,768]{2,1,0:T(8,128)(2,1)}, u32[]{:S(2)}) copy-start(bf16[1,2048,768]{2,1,0:T(8,128)(2,1)} %param.11) | copy-start | bytes 9437188
  111.0 7.7 %copy-start.3 = (bf16[1,2048,768]{2,1,0:T(8,128)(2,1)S(1)}, bf16[1,2048,768]{2,1,0:T(8,128)(2,1)}, u32[]{:S(2)}) copy-start(bf16[1,2048,768]{2,1,0:T(8,128)(2,1)} %param.12) | copy-start | bytes 9437188
  111.0 7.7 %copy-start.5 = (bf16[1,768,2048]{2,1,0:T(8,128)(2,1)S(1)}, bf16[1,768,2048]{2,1,0:T(8,128)(2,1)}, u32[]{:S(2)}) copy-start(bf16[1,768,2048]{2,1,0:T(8,128)(2,1)} %param.13) | copy-start | bytes 9437188
  117.3 29.8 %collective-permute-start.3 = (bf16[216,2304]{1,0:T(8,128)(2,1)}, bf16[216,2304]{1,0:T(8,128)(2,1)S(1)}, u32[]{:S(2)}, u32[]{:S(2)}) collective-permute-start(bf16[216,2304]{1,0:T(8,128)(2,1)} %get-tuple-element.45.refs_0_), channel_id=1, source_target_pairs={{0,1},{1,0},{2,3},{3,2},{4,5},{5,4},{6,7},{7,6},{8,9},{9,8},{10,11... | collective-permute-start | bytes 2985992 | tf_op jit(solution)/shard_map/ppermute | solution.py:264
  118.8 1.1 copy-start.11
  119.9 1.1 copy-start.13
  128.1 35.5 %collective-permute-start.10 = (bf16[216,2304]{1,0:T(8,128)(2,1)S(1)}, bf16[216,2304]{1,0:T(8,128)(2,1)S(1)}, u32[]{:S(2)}, u32[]{:S(2)}) collective-permute-start(bf16[216,2304]{1,0:T(8,128)(2,1)S(1)} %get-tuple-element.52.refs_0_), channel_id=1, source_target_pairs={{0,1},{1,0},{2,3},{3,2},{4,5},{5,4},{6,7},{7,6},{8,9},{9,8},{10,11... | collective-permute-start | bytes 2985992 | tf_op jit(solution)/shard_map/ppermute | solution.py:264
  136.3 48.8 %collective-permute-start.18 = (bf16[216,2304]{1,0:T(8,128)(2,1)S(1)}, bf16[216,2304]{1,0:T(8,128)(2,1)}, u32[]{:S(2)}, u32[]{:S(2)}) collective-permute-start(bf16[216,2304]{1,0:T(8,128)(2,1)S(1)} %get-tuple-element.62.refs_0_), channel_id=1, source_target_pairs={{0,1},{1,0},{2,3},{3,2},{4,5},{5,4},{6,7},{7,6},{8,9},{9,8},{10,11... | collective-permute-start | bytes 2985992 | tf_op jit(solution)/shard_map/ppermute | solution.py:264
  145.2 0.7 copy-start.20
  145.9 0.6 copy-start.22
  146.5 59.4 %collective-permute-start.26 = (bf16[216,2304]{1,0:T(8,128)(2,1)S(1)}, bf16[216,2304]{1,0:T(8,128)(2,1)S(1)}, u32[]{:S(2)}, u32[]{:S(2)}) collective-permute-start(bf16[216,2304]{1,0:T(8,128)(2,1)S(1)} %get-tuple-element.72.refs_0_), channel_id=1, source_target_pairs={{0,1},{1,0},{2,3},{3,2},{4,5},{5,4},{6,7},{7,6},{8,9},{9,8},{10,11... | collective-permute-start | bytes 2985992 | tf_op jit(solution)/shard_map/ppermute | solution.py:264
  147.0 0.9 copy-start.8
  148.0 1.2 copy-start.9
  154.6 68.4 %collective-permute-start.4 = (bf16[2,96,2176]{2,1,0:T(8,128)(2,1)S(1)}, bf16[2,96,2176]{2,1,0:T(8,128)(2,1)S(1)}, u32[]{:S(2)}, u32[]{:S(2)}) collective-permute-start(bf16[2,96,2176]{2,1,0:T(8,128)(2,1)S(1)} %get-tuple-element.49), channel_id=1, source_target_pairs={{0,2},{2,0},{4,6},{6,4},{8,10},{10,8},{12,14},{14,12},{16,18},{18,... | collective-permute-start | bytes 2506760 | tf_op jit(solution)/shard_map/ppermute | solution.py:244
  163.6 0.9 copy-start.6
  164.6 1.2 copy-start.7
  185.1 20.8 %copy-start.21 = (bf16[384,224]{1,0:T(8,128)(2,1)S(1)}, bf16[384,224]{1,0:T(8,128)(2,1)}, u32[]{:S(2)}) copy-start(bf16[384,224]{1,0:T(8,128)(2,1)} %copy-done.20) | copy-start | bytes 516100
  185.1 20.8 %copy-start.23 = (bf16[224,128]{1,0:T(8,128)(2,1)S(1)}, bf16[224,128]{1,0:T(8,128)(2,1)}, u32[]{:S(2)}) copy-start(bf16[224,128]{1,0:T(8,128)(2,1)} %copy-done.22) | copy-start | bytes 172036
  210.1 14.7 %collective-permute-start.27 = (bf16[2,96,2176]{2,1,0:T(8,128)(2,1)S(1)}, bf16[2,96,2176]{2,1,0:T(8,128)(2,1)S(1)}, u32[]{:S(2)}, u32[]{:S(2)}) collective-permute-start(bf16[2,96,2176]{2,1,0:T(8,128)(2,1)S(1)} %get-tuple-element.79), channel_id=1, source_target_pairs={{0,2},{2,0},{4,6},{6,4},{8,10},{10,8},{12,14},{14,12},{16,18},{18,... | collective-permute-start | bytes 2506760 | tf_op jit(solution)/shard_map/ppermute | solution.py:244
  210.2 15.5 %collective-permute-start.19 = (bf16[2,96,2176]{2,1,0:T(8,128)(2,1)S(1)}, bf16[2,96,2176]{2,1,0:T(8,128)(2,1)S(1)}, u32[]{:S(2)}, u32[]{:S(2)}) collective-permute-start(bf16[2,96,2176]{2,1,0:T(8,128)(2,1)S(1)} %get-tuple-element.69), channel_id=1, source_target_pairs={{0,2},{2,0},{4,6},{6,4},{8,10},{10,8},{12,14},{14,12},{16,18},{18,... | collective-permute-start | bytes 2506760 | tf_op jit(solution)/shard_map/ppermute | solution.py:244
  210.7 16.8 %collective-permute-start.11 = (bf16[2,96,2176]{2,1,0:T(8,128)(2,1)S(1)}, bf16[2,96,2176]{2,1,0:T(8,128)(2,1)S(1)}, u32[]{:S(2)}, u32[]{:S(2)}) collective-permute-start(bf16[2,96,2176]{2,1,0:T(8,128)(2,1)S(1)} %get-tuple-element.59), channel_id=1, source_target_pairs={{0,2},{2,0},{4,6},{6,4},{8,10},{10,8},{12,14},{14,12},{16,18},{18,... | collective-permute-start | bytes 2506760 | tf_op jit(solution)/shard_map/ppermute | solution.py:244
  210.8 7.4 %copy-start.24 = (bf16[896,2048]{1,0:T(8,128)(2,1)S(1)}, bf16[896,2048]{1,0:T(8,128)(2,1)}, u32[]{:S(2)}) copy-start(bf16[896,2048]{1,0:T(8,128)(2,1)} %get-tuple-element.80) | copy-start | bytes 11010052
  223.3 44.5 %collective-permute-start.5 = (bf16[96,2176]{1,0:T(8,128)(2,1)S(1)}, bf16[96,2176]{1,0:T(8,128)(2,1)S(1)}, u32[]{:S(2)}, u32[]{:S(2)}) collective-permute-start(bf16[96,2176]{1,0:T(8,128)(2,1)S(1)} %slice_bitcast_fusion.6), channel_id=1, source_target_pairs={{0,4},{2,6},{4,0},{6,2},{8,12},{10,14},{12,8},{14,10},{16,20},{18,... | collective-permute-start | bytes 1253384 | tf_op jit(solution)/shard_map/ppermute | solution.py:244
  225.1 19.6 %collective-permute-start.28 = (bf16[96,2176]{1,0:T(8,128)(2,1)S(1)}, bf16[96,2176]{1,0:T(8,128)(2,1)S(1)}, u32[]{:S(2)}, u32[]{:S(2)}) collective-permute-start(bf16[96,2176]{1,0:T(8,128)(2,1)S(1)} %slice_bitcast_fusion), channel_id=1, source_target_pairs={{0,4},{2,6},{4,0},{6,2},{8,12},{10,14},{12,8},{14,10},{16,20},{18,... | collective-permute-start | bytes 1253384 | tf_op jit(solution)/shard_map/ppermute | solution.py:244
  225.9 27.8 %collective-permute-start.20 = (bf16[96,2176]{1,0:T(8,128)(2,1)S(1)}, bf16[96,2176]{1,0:T(8,128)(2,1)S(1)}, u32[]{:S(2)}, u32[]{:S(2)}) collective-permute-start(bf16[96,2176]{1,0:T(8,128)(2,1)S(1)} %slice_bitcast_fusion.2), channel_id=1, source_target_pairs={{0,4},{2,6},{4,0},{6,2},{8,12},{10,14},{12,8},{14,10},{16,20},{18,... | collective-permute-start | bytes 1253384 | tf_op jit(solution)/shard_map/ppermute | solution.py:244
  227.8 35.1 %copy-start.25 = (bf16[896,2048]{1,0:T(8,128)(2,1)S(1)}, bf16[896,2048]{1,0:T(8,128)(2,1)}, u32[]{:S(2)}) copy-start(bf16[896,2048]{1,0:T(8,128)(2,1)} %get-tuple-element.84) | copy-start | bytes 11010052
  227.8 34.4 %collective-permute-start.12 = (bf16[96,2176]{1,0:T(8,128)(2,1)S(1)}, bf16[96,2176]{1,0:T(8,128)(2,1)S(1)}, u32[]{:S(2)}, u32[]{:S(2)}) collective-permute-start(bf16[96,2176]{1,0:T(8,128)(2,1)S(1)} %slice_bitcast_fusion.4), channel_id=1, source_target_pairs={{0,4},{2,6},{4,0},{6,2},{8,12},{10,14},{12,8},{14,10},{16,20},{18,... | collective-permute-start | bytes 1253384 | tf_op jit(solution)/shard_map/ppermute | solution.py:244
  244.9 22.9 %collective-permute-start.29 = (bf16[96,2176]{1,0:T(8,128)(2,1)S(1)}, bf16[96,2176]{1,0:T(8,128)(2,1)S(1)}, u32[]{:S(2)}, u32[]{:S(2)}) collective-permute-start(bf16[96,2176]{1,0:T(8,128)(2,1)S(1)} %fusion.3), channel_id=1, source_target_pairs={{0,8},{2,10},{4,12},{6,14},{8,16},{10,18},{12,20},{14,22},{16,24},... | collective-permute-start | bytes 1253384 | tf_op jit(solution)/shard_map/ppermute | solution.py:244
  253.8 21.7 %collective-permute-start.21 = (bf16[96,2176]{1,0:T(8,128)(2,1)S(1)}, bf16[96,2176]{1,0:T(8,128)(2,1)S(1)}, u32[]{:S(2)}, u32[]{:S(2)}) collective-permute-start(bf16[96,2176]{1,0:T(8,128)(2,1)S(1)} %fusion.4), channel_id=1, source_target_pairs={{0,16},{2,18},{4,20},{6,22},{8,24},{10,26},{12,28},{14,30},{16,0},... | collective-permute-start | bytes 1253384 | tf_op jit(solution)/shard_map/ppermute | solution.py:244
  262.3 20.1 %collective-permute-start.13 = (bf16[96,2176]{1,0:T(8,128)(2,1)S(1)}, bf16[96,2176]{1,0:T(8,128)(2,1)S(1)}, u32[]{:S(2)}, u32[]{:S(2)}) collective-permute-start(bf16[96,2176]{1,0:T(8,128)(2,1)S(1)} %fusion.5), channel_id=1, source_target_pairs={{0,24},{2,26},{4,28},{6,30},{8,0},{10,2},{12,4},{14,6},{16,8},{18,... | collective-permute-start | bytes 1253384 | tf_op jit(solution)/shard_map/ppermute | solution.py:244
  267.8 15.7 %copy-start.27 = (s32[96,8]{1,0:T(8,128)S(1)}, s32[96,8]{1,0:T(8,128)}, u32[]{:S(2)}) copy-start(s32[96,8]{1,0:T(8,128)} %copy-done.26) | copy-start | bytes 9220

commit v2 on v1

v2 whole, which is shorter than its diff:
```python
import functools

import jax
import jax.numpy as jnp
from jax import lax
from jax.experimental import pallas as pl
from jax.experimental.pallas import tpu as pltpu
from jax.sharding import PartitionSpec as P

BF = jnp.bfloat16
F32 = jnp.float32
LANES = 128
VMEM_LIMIT = 30 * 1024 * 1024
LAST = (((1,), (1,)), ((), ()))


def dot(a, b):
    return jnp.dot(a, b, preferred_element_type=F32)


def round_up(n, m):
    return -(-n // m) * m


def forward_kernel(inner, cap, tok, feat, hid, tile, *refs):
    blocks = refs[:inner]
    wg, wu, wd = refs[inner : inner + 3]
    parts, x_all, sd_all, st_out, grow_out = refs[-9:-4]
    cat, x_s, dy_s, lower = refs[-4:]
    rows = inner * cap
    pad = x_s.shape[0]
    step = pl.program_id(0)

    @pl.when(step == 0)
    def _():
        me = lax.axis_index("expert")
        mine = (lax.broadcasted_iota(jnp.int32, (tok, LANES), 1) == me).astype(F32)
        r = lax.broadcasted_iota(jnp.int32, (tok, tok), 0)
        c = lax.broadcasted_iota(jnp.int32, (tok, tok), 1)
        lower[...] = (c < r).astype(F32).astype(BF)
        slot_of = lax.broadcasted_iota(jnp.int32, (tok, pad), 1)
        st = []
        gates = []
        for b in range(inner):
            cat[b * tok : (b + 1) * tok, :] = blocks[b][:, : 2 * feat]
            table = blocks[b][:, 2 * feat :].astype(F32)
            gate = jnp.sum(table * mine, axis=1, keepdims=True)
            chosen = gate >= 0.0
            flag = jnp.broadcast_to(chosen.astype(F32), (tok, LANES))
            before = dot(lower[...], flag.astype(BF))[:, :1]
            place = jnp.where(chosen, before.astype(jnp.int32) + b * cap, -1)
            st.append((slot_of == place).astype(F32))
            gates.append(jnp.broadcast_to(gate, (tok, LANES)).astype(BF))
        st = jnp.concatenate(st, axis=0)
        gates = jnp.concatenate(gates, axis=0)
        st_out[...] = st.astype(BF)
        pick = st.T.astype(BF)
        grow = dot(pick, gates)
        grow_out[...] = grow.astype(BF)
        x = dot(pick, cat[:, :feat]).astype(BF)
        x_s[...] = x
        x_all[...] = x
        dy = dot(pick, cat[:, feat:])
        dy_s[...] = dy.astype(BF)
        sd_all[...] = (grow[:, :1] * dy).astype(BF)

    off = pl.multiple_of(step * tile, tile)
    cols = pl.ds(off, tile)
    parts[:, cols] = dot(x_s[...], wg[:, cols])[:rows].astype(BF)
    parts[:, pl.ds(hid + off, tile)] = dot(x_s[...], wu[:, cols])[:rows].astype(BF)
    back = lax.dot_general(dy_s[...], wd[cols, :], LAST, preferred_element_type=F32)
    parts[:, pl.ds(2 * hid + off, tile)] = back[:rows].astype(BF)


COST = pl.CostEstimate(flops=1000, bytes_accessed=1000, transcendentals=0)
ANY = pl.BlockSpec(memory_space=pl.ANY)
VMEM = pl.BlockSpec(memory_space=pltpu.VMEM)


def in_hbm(arrays):
    return [pltpu.with_memory_space_constraint(x, pltpu.HBM) for x in arrays]


def in_vmem(arrays):
    return [pltpu.with_memory_space_constraint(x, pltpu.VMEM) for x in arrays]


def tie(x, *after):
    return pl.pallas_call(
        lambda *refs: None,
        in_specs=[ANY] * (1 + len(after)),
        out_specs=ANY,
        out_shape=jax.ShapeDtypeStruct(x.shape, x.dtype),
        input_output_aliases={0: 0},
        compiler_params=pltpu.CompilerParams(vmem_limit_bytes=1024 * 1024),
        cost_estimate=COST,
    )(x, *in_hbm(after))


def block_kernel(tokens, cotangent, ids, gates, out):
    tok, feat = tokens.shape
    out[:, :feat] = tokens[...]
    out[:, feat : 2 * feat] = cotangent[...]
    expert = lax.broadcasted_iota(jnp.int32, (LANES, tok), 0)
    table = jnp.full((LANES, tok), -1.0, F32)
    for k in range(ids.shape[0]):
        table = jnp.where(expert == ids[k : k + 1, :], gates[k : k + 1, :].astype(F32), table)
    out[:, 2 * feat :] = table.T.astype(BF)


def make_block(tokens, cotangent, ids, gates):
    tok, feat = tokens.shape
    return pl.pallas_call(
        block_kernel,
        out_shape=jax.ShapeDtypeStruct((tok, 2 * feat + LANES), BF),
        compiler_params=pltpu.CompilerParams(vmem_limit_bytes=VMEM_LIMIT),
        cost_estimate=COST,
    )(*in_hbm([tokens, cotangent, ids.T, gates.T]))


def forward_kernel(cfg, *refs):
    inner, cap, tok, feat, hid, tile, fresh, n_after, n_slabs, n_add = cfg
    refs = list(refs)

    def take(n):
        out = refs[:n]
        del refs[:n]
        return out

    blocks = take(inner)
    weights = take(3)
    take(n_after + n_slabs)
    added = take(2 if n_add else 0)
    parts, x_all, sd_all, st_out, grow_out, token = take(6)
    sums = take(n_add)
    held = take(3 if fresh else 0)
    cat, x_s, dy_s, lower, *sems = refs
    rows = inner * cap
    pad = x_s.shape[0]
    step = pl.program_id(0)
    off = pl.multiple_of(step * tile, tile)
    cols = pl.ds(off, tile)

    def fetch(i, at):
        cut = (at, slice(None)) if i == 2 else (slice(None), at)
        return pltpu.make_async_copy(weights[i].at[cut], held[i].at[cut], sems[0].at[i])

    @pl.when(step == 0)
    def _():
        if fresh:
            for i in range(3):
                fetch(i, pl.ds(0, tile)).start()
        me = lax.axis_index("expert")
        mine = (lax.broadcasted_iota(jnp.int32, (tok, LANES), 1) == me).astype(F32)
        r = lax.broadcasted_iota(jnp.int32, (tok, tok), 0)
        c = lax.broadcasted_iota(jnp.int32, (tok, tok), 1)
        lower[...] = (c < r).astype(F32).astype(BF)
        slot_of = lax.broadcasted_iota(jnp.int32, (tok, pad), 1)
        st = []
        gates = []
        for b in range(inner):
            cat[b * tok : (b + 1) * tok, :] = blocks[b][:, : 2 * feat]
            table = blocks[b][:, 2 * feat :].astype(F32)
            gate = jnp.sum(table * mine, axis=1, keepdims=True)
            chosen = gate >= 0.0
            flag = jnp.broadcast_to(chosen.astype(F32), (tok, LANES))
            before = dot(lower[...], flag.astype(BF))[:, :1]
            place = jnp.where(chosen, before.astype(jnp.int32) + b * cap, -1)
            st.append((slot_of == place).astype(F32))
            gates.append(jnp.broadcast_to(gate, (tok, LANES)).astype(BF))
        st = jnp.concatenate(st, axis=0)
        gates = jnp.concatenate(gates, axis=0)
        st_out[...] = st.astype(BF)
        pick = st.T.astype(BF)
        grow = dot(pick, gates)
        grow_out[...] = grow.astype(BF)
        x = dot(pick, cat[:, :feat]).astype(BF)
        x_s[...] = x
        x_all[...] = x
        dy = dot(pick, cat[:, feat:])
        dy_s[...] = dy.astype(BF)
        sd_all[...] = (grow[:, :1] * dy).astype(BF)
        token[...] = jnp.zeros_like(token)
        for i in range(n_add):
            sums[i][...] = (added[0][i].astype(F32) + added[1][i].astype(F32)).astype(BF)

    if fresh:
        for i in range(3):
            fetch(i, cols).wait()

        @pl.when(step + 1 < hid // tile)
        def _():
            for i in range(3):
                fetch(i, pl.ds(pl.multiple_of((step + 1) * tile, tile), tile)).start()

        weights = held
    wg, wu, wd = weights
    parts[:, cols] = dot(x_s[...], wg[:, cols])[:rows].astype(BF)
    parts[:, pl.ds(hid + off, tile)] = dot(x_s[...], wu[:, cols])[:rows].astype(BF)
    back = lax.dot_general(dy_s[...], wd[cols, :], LAST, preferred_element_type=F32)
    parts[:, pl.ds(2 * hid + off, tile)] = back[:rows].astype(BF)


def forward_call(start, total, pad, blocks, weights, fresh, cap, slabs, after, added):
    inner = len(blocks)
    tok = blocks[0].shape[0]
    feat, hid = weights[0].shape
    tile = 256 if hid % 256 == 0 else hid
    rows = inner * cap
    index = start // (inner // 2)
    whole = lambda shape: pl.BlockSpec(shape, lambda i: (0,) * len(shape))
    slab = lambda width: pl.BlockSpec((pad, width), lambda i: (index, 0))
    n_add = added[0].shape[0] if added else 0
    in_specs = [whole(b.shape) for b in blocks] + [ANY if fresh else VMEM] * 3 + [ANY] * (len(after) + len(slabs))
    args = list(blocks) + (in_hbm(weights) if fresh else in_vmem(weights)) + in_hbm(after)
    aliases = {len(args) + i: 1 + i for i in range(len(slabs))}
    args += [*slabs, *in_hbm(added[:1]), *added[1:]]
    in_specs += [whole(a.shape) for a in added]
    out_specs = [
        whole((rows, 3 * hid)),
        slab(feat),
        slab(feat),
        whole((inner * tok, pad)),
        whole((pad, LANES)),
        whole((8, LANES)),
    ]
    out_shape = [
        pltpu.HBM((rows, 3 * hid), BF),
        pltpu.HBM((total, feat), BF),
        pltpu.HBM((total, feat), BF),
        pltpu.HBM((inner * tok, pad), BF),
        pltpu.HBM((pad, LANES), BF),
        pltpu.HBM((8, LANES), F32),
    ]
    for i in range(n_add):
        out_specs.append(whole(added[0].shape[1:]))
        out_shape.append(pltpu.HBM(added[0].shape[1:], BF))
    scratch = [
        pltpu.VMEM((inner * tok, 2 * feat), BF),
        pltpu.VMEM((pad, feat), BF),
        pltpu.VMEM((pad, feat), BF),
        pltpu.VMEM((tok, tok), BF),
    ]
    if fresh:
        out_specs += [VMEM] * 3
        out_shape += [pltpu.VMEM(w.shape, w.dtype) for w in weights]
        scratch.append(pltpu.SemaphoreType.DMA((3,)))
    cfg = (inner, cap, tok, feat, hid, tile, fresh, len(after), len(slabs), n_add)
    out = pl.pallas_call(
        functools.partial(forward_kernel, cfg),
        grid=(hid // tile,),
        in_specs=in_specs,
        out_specs=out_specs,
        out_shape=out_shape,
        scratch_shapes=scratch,
        input_output_aliases=aliases,
        compiler_params=pltpu.CompilerParams(vmem_limit_bytes=VMEM_LIMIT),
        cost_estimate=COST,
    )(*args)
    return out[:6], out[6 : 6 + n_add], out[6 + n_add :]


def backward_kernel(inner, tok, feat, hid, tile, n_parts, *refs):
    parts = refs[:n_parts]
    st, grow, wg, wu = refs[n_parts : n_parts + 4]
    keep, send, act_all, pg_all, pu_all, token = refs[-8:-2]
    pg_s, pu_s = refs[-2:]
    rows = parts[0].shape[0]
    pad = pg_s.shape[0]
    half = inner // 2
    step = pl.program_id(0)

    def spread(value, column, width):
        for b in range(inner):
            piece = value[b * tok : (b + 1) * tok]
            target = keep if b % 2 == 0 else send
            target[b // 2, :, pl.ds(column, width)] = piece

    @pl.when(step == 0)
    def _():
        def total(at):
            out = parts[0][:, at * hid : (at + 1) * hid].astype(F32)
            for part in parts[1:]:
                out = out + part[:, at * hid : (at + 1) * hid].astype(F32)
            return out

        def full(value):
            if pad > rows:
                value = jnp.concatenate([value, jnp.zeros((pad - rows, value.shape[1]), F32)], axis=0)
            return value

        gate_pre = total(0)
        sig = 1.0 / (1.0 + jnp.exp(-gate_pre))
        silu = gate_pre * sig
        up = total(1)
        act = silu * up
        back = total(2)
        slot = jnp.sum(act * back, axis=1, keepdims=True)
        act_grad = grow[:rows, :1].astype(F32) * back
        pre_gate = act_grad * up * sig * (1.0 + gate_pre * (1.0 - sig))
        pre_up = act_grad * silu
        token[...] = jnp.zeros_like(token)
        act_all[...] = full(act).astype(BF)
        pg = full(pre_gate).astype(BF)
        pu = full(pre_up).astype(BF)
        pg_all[...] = pg
        pu_all[...] = pu
        pg_s[...] = pg
        pu_s[...] = pu
        me = lax.axis_index("expert")
        mine = (lax.broadcasted_iota(jnp.int32, (rows, LANES), 1) == me).astype(F32)
        slots = full(slot * mine).astype(BF)
        spread(dot(st[...], slots).astype(BF), feat, LANES)

    off = pl.multiple_of(step * tile, tile)
    cut = pl.ds(off, tile)
    grad = lax.dot_general(pg_s[...], wg[cut, :], LAST, preferred_element_type=F32)
    grad = grad + lax.dot_general(pu_s[...], wu[cut, :], LAST, preferred_element_type=F32)
    spread(dot(st[...], grad.astype(BF)).astype(BF), off, tile)


def backward_call(start, total, pad, parts, st, grow, wg, wu, tok, slabs, after):
    feat, hid = wg.shape
    tile = 512 if feat % 512 == 0 else feat
    inner = st.shape[0] // tok
    rows = parts[0].shape[0]
    index = start // (inner // 2)
    wide = feat + LANES
    whole = lambda shape: pl.BlockSpec(shape, lambda i: (0,) * len(shape))
    slab = pl.BlockSpec((pad, hid), lambda i: (index, 0))
    args = in_hbm(parts[:1]) + list(parts[1:]) + in_hbm([st, grow]) + in_vmem([wg, wu]) + in_hbm(after)
    in_specs = [whole(a.shape) for a in args[: len(parts) + 2]] + [VMEM] * 2 + [ANY] * len(after)
    aliases = {}
    if slabs:
        aliases = {len(args) + i: 2 + i for i in range(3)}
        args += list(slabs)
        in_specs += [ANY] * 3
    half = pltpu.HBM((inner // 2, tok, wide), BF)
    saved = pltpu.HBM((total, hid), BF)
    return pl.pallas_call(
        functools.partial(backward_kernel, inner, tok, feat, hid, tile, len(parts)),
        grid=(feat // tile,),
        in_specs=in_specs,
        out_specs=[whole(half.shape), whole(half.shape), slab, slab, slab, whole((8, LANES))],
        out_shape=[half, half, saved, saved, saved, pltpu.HBM((8, LANES), F32)],
        scratch_shapes=[pltpu.VMEM((pad, hid), BF), pltpu.VMEM((pad, hid), BF)],
        input_output_aliases=aliases,
        compiler_params=pltpu.CompilerParams(vmem_limit_bytes=VMEM_LIMIT),
        cost_estimate=COST,
    )(*args)


def local(tokens, cotangent, expert_ids, gate_values, gate_weight, up_weight, down_weight):
    experts = lax.axis_size("expert")
    seqs = lax.axis_size("seq")
    tok, feat = tokens.shape
    top = expert_ids.shape[1]
    cap = min(tok, tok * top // experts + tok * top // (8 * experts))
    inner = 2 * seqs if experts % (2 * seqs) == 0 else 2
    columns = inner // 2
    planes = experts // inner

    def split(i):
        return i // inner, (i % inner) // 2, i % 2

    def join(z, y, c):
        return (z % planes) * inner + (y % columns) * 2 + c

    def shift(dz=0, dy=0, dc=0):
        out = []
        for i in range(experts):
            z, y, c = split(i)
            out.append((i, join(z + dz, y + dy, c ^ dc)))
        return out

    def move(x, **by):
        return lax.ppermute(x, "expert", shift(**by))

    wg, wu, wd = gate_weight[0], up_weight[0], down_weight[0]
    hit = expert_ids[:, :, None] == jnp.arange(LANES, dtype=jnp.int32)
    block = make_block(tokens, cotangent, expert_ids, gate_values)

    def swap(part):
        if seqs == 2:
            return [part, lax.ppermute(part, "seq", [(0, 1), (1, 0)])]
        gathered = lax.all_gather(part, "seq", axis=0)
        return [gathered[i] for i in range(seqs)]

    order = list(range(planes // 2 + 1)) + list(range(planes - 1, planes // 2, -1))
    pieces = [(k, j) for k in order for j in range(columns)]
    ends = [1 + columns * i for i in range(planes)]
    ends += [ends[-1] + i for i in range(1, columns)]
    chunks = [pieces[lo:hi] for lo, hi in zip([0] + ends, ends)]
    unit = round_up(2 * cap, 16)
    total_rows = planes * columns * unit
    starts, at = [0] * len(chunks), 0
    for size in sorted({len(c) for c in chunks}, reverse=True):
        for n, chunk in enumerate(chunks):
            if len(chunk) == size:
                starts[n], at = at, at + size

    arrived = {(0, 0): block}
    pending = {}

    def send_on(k):
        own = arrived[k, 0]
        for j in range(1, columns):
            pending[k, j] = move(own, dy=j)
        if k < planes - k and k + 1 <= planes // 2:
            pending[k + 1, 0] = move(own, dz=1)
        if k == 0 and planes > 2:
            pending[planes - 1, 0] = move(own, dz=-1)
        elif planes - k < k and planes - k + 1 < (planes + 1) // 2:
            pending[k - 1, 0] = move(own, dz=-1)

    send_on(0)
    x_slab = act_slab = ()
    returned = {}
    outgoing = {}
    totals = []

    def finish(entry, after):
        nonlocal act_slab
        start, chunk, parts, st, grow = entry
        keep, send, *act_slab, token = backward_call(
            start, total_rows, len(chunk) * unit, parts, st, grow, *held[:2], tok, act_slab, after
        )
        return token, (keep, move(send, dc=1))

    def add(keep, got):
        return [(keep[i].astype(F32) + got[i].astype(F32)).astype(BF) for i in range(keep.shape[0])]

    def give_back(chunk, sums):
        for (k, j), value in zip(chunk, sums):
            returned[k, j] = move(value, dy=-j) if j else value
        for k in {k: None for k, _ in chunk}:
            if all((k, j) in returned for j in range(columns)):
                summed = sum(returned[k, j].astype(F32) for j in range(columns))
                if k:
                    outgoing[k] = summed.astype(BF)
                    summed = move(outgoing[k], dz=-k).astype(F32)
                totals.append(summed)

    held = (wg, wu, wd)
    entries, unsent = [], []
    sent = token = None
    for n, chunk in enumerate(chunks):
        blocks = []
        for piece in chunk:
            if piece not in arrived:
                arrived[piece] = tie(pending.pop(piece), token)
                if piece[1] == 0:
                    send_on(piece[0])
            blocks += [arrived[piece], move(arrived[piece], dc=1)]
        added = unsent.pop(0) if unsent else None
        (part, *x_slab, st, grow, sent), sums, loaded = forward_call(
            starts[n], total_rows, len(chunk) * unit, blocks, held, n == 0, cap, x_slab,
            [] if token is None else [token], added[1] if added else ()
        )
        held = loaded or held
        if added:
            give_back(added[0], sums)
        entries.append((starts[n], chunk, swap(part), st, grow))
        if n != 1:
            done = entries.pop(0)
            token, halves = finish(done, [sent])
            unsent.append((done[1], halves))
    for last_chunk, halves in unsent:
        sums = add(*halves)
        give_back(last_chunk, sums)
    done = entries.pop(0)
    token, halves = finish(done, [token, *sums])
    sums = add(*halves)
    give_back(done[1], sums)

    totals = sum(totals[1:], totals[0])
    input_grad = totals[:, :feat].astype(BF)
    slots = totals[:, feat:]
    gate_grad = jnp.sum(jnp.where(hit, slots[:, None, :], 0.0), axis=2).astype(BF)
    contract_rows = (((0,), (0,)), ((), ()))
    wgrad = lambda a, b: lax.dot_general(a, b, contract_rows, preferred_element_type=F32).astype(BF)[None]
    x_all, sd_all = x_slab
    act_all, pg_all, pu_all = act_slab
    leaving = list(outgoing.values())
    down = wgrad(act_all, tie(sd_all, *sums, *leaving[:-1]))
    x_all = tie(x_all, *leaving)
    return (
        input_grad,
        gate_grad,
        wgrad(x_all, pg_all),
        wgrad(x_all, pu_all),
        down,
    )


def solution(mesh):
    in_specs = (
        P("expert", "seq"),
        P("expert", "seq"),
        P("expert", None),
        P("expert", None),
        P("expert", "seq", None),
        P("expert", "seq", None),
        P("expert", None, "seq"),
    )
    out_specs = (
        P("expert", "seq"),
        P("expert", None),
        P("expert", "seq", None),
        P("expert", "seq", None),
        P("expert", None, "seq"),
    )
    return jax.shard_map(local, mesh=mesh, in_specs=in_specs, out_specs=out_specs, check_vma=False)
```

time: 285 us -> 191 us (0.67)
  waiting for transfers between devices: 164 us -> 68.6 us
  Pallas kernels: 47.8 us -> 66.4 us
  local copies, waits for them, and re-layouts: 24.6 us -> 6.39 us
    ppermute x26 -> x27, waiting for transfers between devices: 125 us -> 36.1 us  [move(): return lax.ppermute(x, 'expert', shift(**by))]
    unnamed x58 -> x38, local copies, waits for them, and re-layouts: 22.9 us -> 5.58 us
    pallas_call x4 -> x5, Pallas kernels: 19.5 us -> 32.1 us  [backward_call(): pl.pallas_call(functools.partial(backward_kernel, inner, tok, feat, hid,...]
    ppermute x4 -> x5, waiting for transfers between devices: 39.2 us -> 32.5 us  [swap(): return [part, lax.ppermute(part, 'seq', [(0, 1), (1, 0)])]]
    pallas_call x4 -> x15, Pallas kernels: 28.3 us -> 34.3 us  [the longest x5 33.1 us: forward_call(): pl.pallas_call(functools.partial(forward_kernel, cfg), grid=(hid // tile,...]
    ppermute x4 -> x5, starting transfers between devices: 4.06 us -> 7.66 us  [swap(): return [part, lax.ppermute(part, 'seq', [(0, 1), (1, 0)])]]
    ppermute x26 -> x27, starting transfers between devices: 22.8 us -> 20.9 us  [move(): return lax.ppermute(x, 'expert', shift(**by))]
  transfers between devices with their start and end apart: 30 -> 32, of which waited for: 12 -> 14; matrix products, arithmetic and copies ran while one was open for 6% -> 10% of each run, Pallas kernels for 17% -> 31%
where the time goes in v2:
time: 191 us; the launch traced here: 190 us
  waiting for transfers between devices  68.6 us (36%)
  Pallas kernels  66.4 us (35%)
  starting transfers between devices  28.5 us (15%)
  matrix products  14.7 us (8%)
  local copies, waits for them, and re-layouts  6.39 us (3%)
  other arithmetic  4.44 us (2%)
    ppermute x27, waiting for transfers between devices, move(): return lax.ppermute(x, 'expert', shift(**by))  36.1 us
    pallas_call x5, Pallas kernels, forward_call(): pl.pallas_call(functools.partial(forward_kernel, cfg), grid=(hid // tile,...  33.1 us
    ppermute x5, waiting for transfers between devices, swap(): return [part, lax.ppermute(part, 'seq', [(0, 1), (1, 0)])]  32.5 us
    pallas_call x5, Pallas kernels, backward_call(): pl.pallas_call(functools.partial(backward_kernel, inner, tok, feat, hid,...  32.1 us
    ppermute x27, starting transfers between devices, move(): return lax.ppermute(x, 'expert', shift(**by))  20.9 us
    dot_general x3, matrix products, local(): lax.dot_general(a, b, contract_rows, preferred_element_type=F32).astype(BF)  14.7 us
    ppermute x5, starting transfers between devices, swap(): return [part, lax.ppermute(part, 'seq', [(0, 1), (1, 0)])]  7.66 us
    unnamed x38, local copies, waits for them, and re-layouts  5.58 us
  transfers between devices with their start and end apart: 32, of which 14 were waited for; matrix products, arithmetic and copies ran while one was open for 10% of the time, Pallas kernels for 31%

profile of v2, /device:TPU:0, one launch (start us, length us, event | category | flops | bytes accessed | tf_op | source)
XLA Modules:
  0.0 189.9 jit_solution(4253808248001388494)
XLA Ops:
  0.6 1.3 shard_map.110.refs_0_
  1.9 0.5 collective-permute-start.1
  2.4 2.6 %collective-permute-start.4 = (bf16[96,4224]{1,0:T(8,128)(2,1)S(1)}, bf16[96,4224]{1,0:T(8,128)(2,1)S(1)}, u32[]{:S(2)}, u32[]{:S(2)}) collective-permute-start(bf16[96,4224]{1,0:T(8,128)(2,1)S(1)} %shard_map.110.refs_0_), channel_id=1, source_target_pairs={{0,8},{2,10},{4,12},{6,14},{8,16},{10,18},{12,20},{14,22},{16,24},... | collective-permute-start | bytes 2433032 | tf_op jit(solution)/shard_map/ppermute | solution.py:377
  5.1 1.5 collective-permute-start
  6.6 7.4 %shard_map.111 = (bf16[108,2304]{1,0:T(8,128)(2,1)}, bf16[896,2048]{1,0:T(8,128)(2,1)}, bf16[896,2048]{1,0:T(8,128)(2,1)}, bf16[192,112]{1,0:T(8,128)(2,1)}, bf1...) custom-call(bf16[96,4224]{1,0:T(8,128)(2,1)S(1)} %shard_map.110.refs, ...), custom_call_target="tpu_custom_call" | custom-call | flops 1000 | bytes 1000 | tf_op jit(solution)/shard_map/pallas_call | solution.py:249
  14.0 1.6 collective-permute-start.2
  15.6 12.3 %collective-permute-done.2.refs_1_ = bf16[108,2304]{1,0:T(8,128)(2,1)S(1)} collective-permute-done((bf16[108,2304]{1,0:T(8,128)(2,1)}, bf16[108,2304]{1,0:T(8,128)(2,1)S(1)}, u32[]{:S(2)}, u32[]{:S(2)}) %collective-permute-start.2) | collective-permute-done | bytes 497696 | tf_op jit(solution)/shard_map/ppermute | solution.py:385
  27.8 5.7 %shard_map.112 = (bf16[1,96,2176]{2,1,0:T(8,128)(2,1)}, bf16[1,96,2176]{2,1,0:T(8,128)(2,1)}, bf16[896,768]{1,0:T(8,128)(2,1)}, bf16[896,768]{1,0:T(8,128)(2,1)}...) custom-call(bf16[108,2304]{1,0:T(8,128)(2,1)} %get-tuple-element.71.refs_0_, ...), custom_call_target="tpu_custom_call" | custom-call | flops 1000 | bytes 1000 | tf_op jit(solution)/shard_map/pallas_call | solution.py:340
  33.6 0.5 collective-permute-start.3
  34.1 1.6 collective-permute-start.7
  35.7 0.9 collective-permute-start.10
  36.6 1.8 collective-permute-done.6.refs_11_
  38.4 6.8 %shard_map.115 = (bf16[216,2304]{1,0:T(8,128)(2,1)}, bf16[896,2048]{1,0:T(8,128)(2,1)}, bf16[896,2048]{1,0:T(8,128)(2,1)}, bf16[384,224]{1,0:T(8,128)(2,1)}, bf1...) custom-call(bf16[96,4224]{1,0:T(8,128)(2,1)S(1)} %shard_map.113.refs, ...), custom_call_target="tpu_custom_call", output_to_operand_aliasing={{1}: (8, {}), {2}: (9, {})} | custom-call | flops 1000 | bytes 1000 | tf_op jit(solution)/shard_map/pallas_call | solution.py:249
  45.2 1.6 collective-permute-start.9
  46.8 9.2 %collective-permute-done.7.refs_0_ = bf16[96,4224]{1,0:T(8,128)(2,1)S(1)} collective-permute-done((bf16[96,4224]{1,0:T(8,128)(2,1)S(1)}, bf16[96,4224]{1,0:T(8,128)(2,1)S(1)}, u32[]{:S(2)}, u32[]{:S(2)}) %collective-permute-start.7) | collective-permute-done | bytes 811040 | tf_op jit(solution)/shard_map/ppermute | solution.py:377
  56.0 0.5 collective-permute-start.11
  56.5 1.0 collective-permute-start.8
  57.5 1.7 collective-permute-start.14
  59.2 0.2 collective-permute-done.11.refs_1_
  59.5 5.6 %shard_map.118 = (bf16[216,2304]{1,0:T(8,128)(2,1)}, bf16[896,2048]{1,0:T(8,128)(2,1)}, bf16[896,2048]{1,0:T(8,128)(2,1)}, bf16[384,224]{1,0:T(8,128)(2,1)}, bf16[224,128]{1,0:T(8,128)(2,1)}, /*index=5*/f32[8,128]{1,0:T(8,128)}) custom-call(bf16[96,4224]{1,0:T(8,128)(2,1)S(1)} %shard_map.117.refs_0_, ...), custom_call_target="tpu_custom_call", output_to_operand_aliasing={{1}: (8, {}), {2}: (9, {})} | custom-call | flops 1000 | bytes 1000 | tf_op jit(solution)/shard_map/pallas_call | solution.py:249
  65.1 1.5 collective-permute-start.19
  66.6 3.8 %collective-permute-done.9.refs_1_ = bf16[216,2304]{1,0:T(8,128)(2,1)S(1)} collective-permute-done((bf16[216,2304]{1,0:T(8,128)(2,1)}, bf16[216,2304]{1,0:T(8,128)(2,1)S(1)}, u32[]{:S(2)}, u32[]{:S(2)}) %collective-permute-start.9) | collective-permute-done | bytes 995360 | tf_op jit(solution)/shard_map/ppermute | solution.py:385
  70.4 6.9 %shard_map.119 = (bf16[2,96,2176]{2,1,0:T(8,128)(2,1)}, bf16[2,96,2176]{2,1,0:T(8,128)(2,1)}, bf16[896,768]{1,0:T(8,128)(2,1)}, bf16[896,768]{1,0:T(8,128)(2,1)}...) custom-call(bf16[216,2304]{1,0:T(8,128)(2,1)} %get-tuple-element.84.refs_, ...), custom_call_target="tpu_custom_call", output_to_operand_aliasing={{2}: (7, {}), {3}: (8, {}), {4}: (9, {})} | custom-call | flops 1000 | bytes 1000 | tf_op jit(solution)/shard_map/pallas_call | solution.py:340
  77.3 0.5 collective-permute-start.13
  77.8 1.1 collective-permute-start.18
  78.9 1.8 collective-permute-done.13.refs_1_
  80.7 1.2 collective-permute-done.15.refs_3_
  81.9 7.5 %shard_map.122 = (bf16[216,2304]{1,0:T(8,128)(2,1)}, bf16[896,2048]{1,0:T(8,128)(2,1)}, bf16[896,2048]{1,0:T(8,128)(2,1)}, bf16[384,224]{1,0:T(8,128)(2,1)}, bf1...) custom-call(bf16[96,4224]{1,0:T(8,128)(2,1)S(1)} %shard_map.120.refs, ...), custom_call_target="tpu_custom_call", output_to_operand_aliasing={{1}: (8, {}), {2}: (9, {})} | custom-call | flops 1000 | bytes 1000 | tf_op jit(solution)/shard_map/pallas_call | solution.py:249
  89.4 1.6 collective-permute-start.24
  90.9 6.9 %shard_map.123 = (bf16[2,96,2176]{2,1,0:T(8,128)(2,1)}, bf16[2,96,2176]{2,1,0:T(8,128)(2,1)}, bf16[896,768]{1,0:T(8,128)(2,1)}, bf16[896,768]{1,0:T(8,128)(2,1)}...) custom-call(bf16[216,2304]{1,0:T(8,128)(2,1)} %get-tuple-element.100.refs, ...), custom_call_target="tpu_custom_call", output_to_operand_aliasing={{2}: (7, {}), {3}: (8, {}), {4}: (9, {})} | custom-call | flops 1000 | bytes 1000 | tf_op jit(solution)/shard_map/pallas_call | solution.py:340
  97.8 0.5 collective-permute-done.18.refs_0_
  98.3 3.0 %collective-permute-done.20.refs_1_ = bf16[96,4224]{1,0:T(8,128)(2,1)S(1)} collective-permute-done((bf16[96,4224]{1,0:T(8,128)(2,1)S(1)}, bf16[96,4224]{1,0:T(8,128)(2,1)S(1)}, u32[]{:S(2)}, u32[]{:S(2)}) %collective-permute-start.20) | collective-permute-done | bytes 811040 | tf_op jit(solution)/shard_map/ppermute | solution.py:377
  101.3 5.7 %shard_map.125 = (bf16[108,2304]{1,0:T(8,128)(2,1)}, bf16[896,2048]{1,0:T(8,128)(2,1)}, bf16[896,2048]{1,0:T(8,128)(2,1)}, bf16[192,112]{1,0:T(8,128)(2,1)}, bf1...) custom-call(bf16[96,4224]{1,0:T(8,128)(2,1)S(1)} %shard_map.124.refs, ...), custom_call_target="tpu_custom_call", output_to_operand_aliasing={{1}: (6, {}), {2}: (7, {})} | custom-call | flops 1000 | bytes 1000 | tf_op jit(solution)/shard_map/pallas_call | solution.py:249
  107.0 6.7 %collective-permute-done.24.refs_1_ = bf16[216,2304]{1,0:T(8,128)(2,1)S(1)} collective-permute-done((bf16[216,2304]{1,0:T(8,128)(2,1)}, bf16[216,2304]{1,0:T(8,128)(2,1)S(1)}, u32[]{:S(2)}, u32[]{:S(2)}) %collective-permute-start.24) | collective-permute-done | bytes 995360 | tf_op jit(solution)/shard_map/ppermute | solution.py:385
  113.7 6.9 %shard_map.126 = (bf16[2,96,2176]{2,1,0:T(8,128)(2,1)}, bf16[2,96,2176]{2,1,0:T(8,128)(2,1)}, bf16[896,768]{1,0:T(8,128)(2,1)}, bf16[896,768]{1,0:T(8,128)(2,1)}...) custom-call(bf16[216,2304]{1,0:T(8,128)(2,1)} %get-tuple-element.114.refs, ...), custom_call_target="tpu_custom_call", output_to_operand_aliasing={{2}: (7, {}), {3}: (8, {}), {4}: (9, {})} | custom-call | flops 1000 | bytes 1000 | tf_op jit(solution)/shard_map/pallas_call | solution.py:340
  120.7 1.1 collective-permute-start.17
  121.8 0.9 collective-permute-start.22
  122.8 1.5 collective-permute-start.28
  124.3 2.5 %fusion.4 = (bf16[96,2176]{1,0:T(8,128)(2,1)}, bf16[96,2176]{1,0:T(8,128)(2,1)}) fusion(bf16[2,96,2176]{2,1,0:T(8,128)(2,1)} %collective-permute-done.25, bf16[2,96,2176]{2,1,0:T(8,128)(2,1)} %get-tuple-element.121), kind=kLoop, calls=%fused_computation.15 | loop fusion | flops 1671168 | bytes 2506752 | tf_op jit(solution)/shard_map/convert_element_type | solution.py:431
  126.8 9.8 %collective-permute-done.28.refs_1_ = bf16[108,2304]{1,0:T(8,128)(2,1)S(1)} collective-permute-done((bf16[108,2304]{1,0:T(8,128)(2,1)}, bf16[108,2304]{1,0:T(8,128)(2,1)S(1)}, u32[]{:S(2)}, u32[]{:S(2)}) %collective-permute-start.28) | collective-permute-done | bytes 497696 | tf_op jit(solution)/shard_map/ppermute | solution.py:385
  136.6 1.9 copy-done.1
  138.5 5.8 %shard_map.127 = (bf16[1,96,2176]{2,1,0:T(8,128)(2,1)}, bf16[1,96,2176]{2,1,0:T(8,128)(2,1)}, bf16[896,768]{1,0:T(8,128)(2,1)}, bf16[896,768]{1,0:T(8,128)(2,1)}...) custom-call(bf16[108,2304]{1,0:T(8,128)(2,1)} %get-tuple-element.123.re, ...), custom_call_target="tpu_custom_call", output_to_operand_aliasing={{2}: (9, {}), {3}: (10, {}), {4}: (11, {})} | custom-call | flops 1000 | bytes 1000 | tf_op jit(solution)/shard_map/pallas_call | solution.py:340
  144.4 0.1 add_convert_fusion.5.refs_1_.refs_2_
  144.5 2.6 %collective-permute-start.23 = (bf16[96,2176]{1,0:T(8,128)(2,1)S(1)}, bf16[96,2176]{1,0:T(8,128)(2,1)S(1)}, u32[]{:S(2)}, u32[]{:S(2)}) collective-permute-start(bf16[96,2176]{1,0:T(8,128)(2,1)S(1)} %add_convert_fusion.5.refs_1_.refs_2_), channel_id=1, source_target_pairs={{0,24},{2,26},{4,28},{6,30},{8,0},{10,2},{12,4},{14,6},{16,8},{18,... | collective-permute-start | bytes 1253384 | tf_op jit(solution)/shard_map/ppermute | solution.py:377
  147.1 1.5 collective-permute-start.26
  148.6 1.1 fusion.5.refs_1_
  149.7 0.6 collective-permute-start.30
  150.3 9.3 %collective-permute-done.26 = bf16[96,2176]{1,0:T(8,128)(2,1)S(1)} collective-permute-done((bf16[96,2176]{1,0:T(8,128)(2,1)S(1)}, bf16[96,2176]{1,0:T(8,128)(2,1)S(1)}, u32[]{:S(2)}, u32[]{:S(2)}) %collective-permute-start.26) | collective-permute-done | bytes 417824 | tf_op jit(solution)/shard_map/ppermute | solution.py:377
  159.6 0.1 add_convert_fusion.3.refs_2_.refs_3_
  159.7 0.8 collective-permute-start.27
  160.5 1.3 copy-done.4
  161.8 4.8 %fusion.2 = bf16[1,768,2048]{2,1,0:T(8,128)(2,1)} fusion(bf16[896,768]{1,0:T(8,128)(2,1)S(1)} %copy-done.4, bf16[896,2048]{1,0:T(8,128)(2,1)S(1)} %shard_map.129), kind=kOutput, calls=%fused_computation.5 | convolution fusion | flops 2820145152 | bytes 8192000 | tf_op jit(solution)/shard_map/dot_general | solution.py:481
  166.7 1.1 collective-permute-done.30
  167.8 0.1 add_convert_fusion.refs_3_
  167.9 0.5 collective-permute-start.31
  168.4 0.2 copy-done.10
  168.6 1.3 copy-done.6
  170.0 4.9 %fusion.1 = bf16[1,2048,768]{2,1,0:T(8,128)(2,1)} fusion(bf16[896,2048]{1,0:T(8,128)(2,1)S(1)} %shard_map.128, bf16[896,768]{1,0:T(8,128)(2,1)S(1)} %copy-done.6), kind=kOutput, calls=%fused_computation.4 | convolution fusion | flops 2820145152 | bytes 8192000 | tf_op jit(solution)/shard_map/dot_general | solution.py:481
  174.9 4.9 %fusion = bf16[1,2048,768]{2,1,0:T(8,128)(2,1)} fusion(bf16[896,2048]{1,0:T(8,128)(2,1)S(1)} %shard_map.128, bf16[896,768]{1,0:T(8,128)(2,1)S(1)} %copy-done.5), kind=kOutput, calls=%fused_computation.3 | convolution fusion | flops 2820145152 | bytes 8192000 | tf_op jit(solution)/shard_map/dot_general | solution.py:481
  179.8 8.1 %collective-permute-done.27 = bf16[96,2176]{1,0:T(8,128)(2,1)S(1)} collective-permute-done((bf16[96,2176]{1,0:T(8,128)(2,1)S(1)}, bf16[96,2176]{1,0:T(8,128)(2,1)S(1)}, u32[]{:S(2)}, u32[]{:S(2)}) %collective-permute-start.27) | collective-permute-done | bytes 417824 | tf_op jit(solution)/shard_map/ppermute | solution.py:377
  187.9 0.2 convert_add_fusion
  188.2 0.8 slice.34
  189.0 0.3 select_reduce_fusion
  189.3 0.7 copy.43
  (70 shorter events, 0.5 us)
Async XLA Ops:
  1.9 4.7 %collective-permute-start.1 = (bf16[96,4224]{1,0:T(8,128)(2,1)S(1)}, bf16[96,4224]{1,0:T(8,128)(2,1)S(1)}, u32[]{:S(2)}, u32[]{:S(2)}) collective-permute-start(bf16[96,4224]{1,0:T(8,128)(2,1)S(1)} %shard_map.110.refs_0_), channel_id=1, source_target_pairs={{0,2},{2,0},{4,6},{6,4},{8,10},{10,8},{12,14},{14,12},{16,18},{18,... | collective-permute-start | bytes 2433032 | tf_op jit(solution)/shard_map/ppermute | solution.py:377
  2.4 31.1 %collective-permute-start.4 = (bf16[96,4224]{1,0:T(8,128)(2,1)S(1)}, bf16[96,4224]{1,0:T(8,128)(2,1)S(1)}, u32[]{:S(2)}, u32[]{:S(2)}) collective-permute-start(bf16[96,4224]{1,0:T(8,128)(2,1)S(1)} %shard_map.110.refs_0_), channel_id=1, source_target_pairs={{0,8},{2,10},{4,12},{6,14},{8,16},{10,18},{12,20},{14,22},{16,24},... | collective-permute-start | bytes 2433032 | tf_op jit(solution)/shard_map/ppermute | solution.py:377
  5.1 28.5 %collective-permute-start = (bf16[96,4224]{1,0:T(8,128)(2,1)S(1)}, bf16[96,4224]{1,0:T(8,128)(2,1)S(1)}, u32[]{:S(2)}, u32[]{:S(2)}) collective-permute-start(bf16[96,4224]{1,0:T(8,128)(2,1)S(1)} %shard_map.110.refs_0_), channel_id=1, source_target_pairs={{0,4},{2,6},{4,0},{6,2},{8,12},{10,14},{12,8},{14,10},{16,20},{18,... | collective-permute-start | bytes 2433032 | tf_op jit(solution)/shard_map/ppermute | solution.py:377
  14.0 99.7 %copy-start = (bf16[2048,768]{1,0:T(8,128)(2,1)}, bf16[2048,768]{1,0:T(8,128)(2,1)S(1)}, u32[]{:S(2)}) copy-start(bf16[2048,768]{1,0:T(8,128)(2,1)S(1)} %get-tuple-element.75.refs_5_.refs_3_) | copy-start | bytes 9437188
  14.0 13.8 %collective-permute-start.2 = (bf16[108,2304]{1,0:T(8,128)(2,1)}, bf16[108,2304]{1,0:T(8,128)(2,1)S(1)}, u32[]{:S(2)}, u32[]{:S(2)}) collective-permute-start(bf16[108,2304]{1,0:T(8,128)(2,1)} %get-tuple-element.71.refs_0_), channel_id=1, source_target_pairs={{0,1},{1,0},{2,3},{3,2},{4,5},{5,4},{6,7},{7,6},{8,9},{9,8},{10,11... | collective-permute-start | bytes 1493000 | tf_op jit(solution)/shard_map/ppermute | solution.py:385
  33.5 3.1 %copy-start.17 = (bf16[1,96,2176]{2,1,0:T(8,128)(2,1)S(1)}, bf16[1,96,2176]{2,1,0:T(8,128)(2,1)}, u32[]{:S(2)}) copy-start(bf16[1,96,2176]{2,1,0:T(8,128)(2,1)} %get-tuple-element.82) | copy-start | bytes 1253380
  33.5 4.9 %collective-permute-start.5 = (bf16[96,4224]{1,0:T(8,128)(2,1)S(1)}, bf16[96,4224]{1,0:T(8,128)(2,1)S(1)}, u32[]{:S(2)}, u32[]{:S(2)}) collective-permute-start(bf16[96,4224]{1,0:T(8,128)(2,1)S(1)} %shard_map.114.refs_2_), channel_id=1, source_target_pairs={{0,2},{2,0},{4,6},{6,4},{8,10},{10,8},{12,14},{14,12},{16,18},{18,... | collective-permute-start | bytes 2433032 | tf_op jit(solution)/shard_map/ppermute | solution.py:377
  33.6 4.8 %collective-permute-start.3 = (bf16[96,4224]{1,0:T(8,128)(2,1)S(1)}, bf16[96,4224]{1,0:T(8,128)(2,1)S(1)}, u32[]{:S(2)}, u32[]{:S(2)}) collective-permute-start(bf16[96,4224]{1,0:T(8,128)(2,1)S(1)} %shard_map.113.refs_0_), channel_id=1, source_target_pairs={{0,2},{2,0},{4,6},{6,4},{8,10},{10,8},{12,14},{14,12},{16,18},{18,... | collective-permute-start | bytes 2433032 | tf_op jit(solution)/shard_map/ppermute | solution.py:377
  34.1 21.9 %collective-permute-start.7 = (bf16[96,4224]{1,0:T(8,128)(2,1)S(1)}, bf16[96,4224]{1,0:T(8,128)(2,1)S(1)}, u32[]{:S(2)}, u32[]{:S(2)}) collective-permute-start(bf16[96,4224]{1,0:T(8,128)(2,1)S(1)} %shard_map.114.refs_2_), channel_id=1, source_target_pairs={{0,8},{2,10},{4,12},{6,14},{8,16},{10,18},{12,20},{14,22},{16,24},... | collective-permute-start | bytes 2433032 | tf_op jit(solution)/shard_map/ppermute | solution.py:377
  35.7 20.3 %collective-permute-start.10 = (bf16[96,4224]{1,0:T(8,128)(2,1)S(1)}, bf16[96,4224]{1,0:T(8,128)(2,1)S(1)}, u32[]{:S(2)}, u32[]{:S(2)}) collective-permute-start(bf16[96,4224]{1,0:T(8,128)(2,1)S(1)} %shard_map.114.refs_2_), channel_id=1, source_target_pairs={{0,4},{2,6},{4,0},{6,2},{8,12},{10,14},{12,8},{14,10},{16,20},{18,... | collective-permute-start | bytes 2433032 | tf_op jit(solution)/shard_map/ppermute | solution.py:377
  36.6 1.8 collective-permute-start.6
  45.2 25.1 %collective-permute-start.9 = (bf16[216,2304]{1,0:T(8,128)(2,1)}, bf16[216,2304]{1,0:T(8,128)(2,1)S(1)}, u32[]{:S(2)}, u32[]{:S(2)}) collective-permute-start(bf16[216,2304]{1,0:T(8,128)(2,1)} %get-tuple-element.84.refs_0_), channel_id=1, source_target_pairs={{0,1},{1,0},{2,3},{3,2},{4,5},{5,4},{6,7},{7,6},{8,9},{9,8},{10,11... | collective-permute-start | bytes 2985992 | tf_op jit(solution)/shard_map/ppermute | solution.py:385
  56.0 3.3 %collective-permute-start.12 = (bf16[96,4224]{1,0:T(8,128)(2,1)S(1)}, bf16[96,4224]{1,0:T(8,128)(2,1)S(1)}, u32[]{:S(2)}, u32[]{:S(2)}) collective-permute-start(bf16[96,4224]{1,0:T(8,128)(2,1)S(1)} %shard_map.116.refs_2_), channel_id=1, source_target_pairs={{0,2},{2,0},{4,6},{6,4},{8,10},{10,8},{12,14},{14,12},{16,18},{18,... | collective-permute-start | bytes 2433032 | tf_op jit(solution)/shard_map/ppermute | solution.py:377
  56.0 3.5 %collective-permute-start.11 = (bf16[96,4224]{1,0:T(8,128)(2,1)S(1)}, bf16[96,4224]{1,0:T(8,128)(2,1)S(1)}, u32[]{:S(2)}, u32[]{:S(2)}) collective-permute-start(bf16[96,4224]{1,0:T(8,128)(2,1)S(1)} %shard_map.117.refs_0_), channel_id=1, source_target_pairs={{0,2},{2,0},{4,6},{6,4},{8,10},{10,8},{12,14},{14,12},{16,18},{18,... | collective-permute-start | bytes 2433032 | tf_op jit(solution)/shard_map/ppermute | solution.py:377
  56.5 20.7 %collective-permute-start.8 = (bf16[96,4224]{1,0:T(8,128)(2,1)S(1)}, bf16[96,4224]{1,0:T(8,128)(2,1)S(1)}, u32[]{:S(2)}, u32[]{:S(2)}) collective-permute-start(bf16[96,4224]{1,0:T(8,128)(2,1)S(1)} %shard_map.116.refs_2_), channel_id=1, source_target_pairs={{0,4},{2,6},{4,0},{6,2},{8,12},{10,14},{12,8},{14,10},{16,20},{18,... | collective-permute-start | bytes 2433032 | tf_op jit(solution)/shard_map/ppermute | solution.py:377
  57.5 20.3 %collective-permute-start.14 = (bf16[96,4224]{1,0:T(8,128)(2,1)S(1)}, bf16[96,4224]{1,0:T(8,128)(2,1)S(1)}, u32[]{:S(2)}, u32[]{:S(2)}) collective-permute-start(bf16[96,4224]{1,0:T(8,128)(2,1)S(1)} %shard_map.110.refs_0_), channel_id=1, source_target_pairs={{0,24},{2,26},{4,28},{6,30},{8,0},{10,2},{12,4},{14,6},{16,8},{18,... | collective-permute-start | bytes 2433032 | tf_op jit(solution)/shard_map/ppermute | solution.py:377
  65.1 25.8 %collective-permute-start.19 = (bf16[216,2304]{1,0:T(8,128)(2,1)}, bf16[216,2304]{1,0:T(8,128)(2,1)S(1)}, u32[]{:S(2)}, u32[]{:S(2)}) collective-permute-start(bf16[216,2304]{1,0:T(8,128)(2,1)} %get-tuple-element.100.refs_0_), channel_id=1, source_target_pairs={{0,1},{1,0},{2,3},{3,2},{4,5},{5,4},{6,7},{7,6},{8,9},{9,8},{10,11... | collective-permute-start | bytes 2985992 | tf_op jit(solution)/shard_map/ppermute | solution.py:385
  77.2 4.7 %collective-permute-start.16 = (bf16[2,96,2176]{2,1,0:T(8,128)(2,1)}, bf16[2,96,2176]{2,1,0:T(8,128)(2,1)S(1)}, u32[]{:S(2)}, u32[]{:S(2)}) collective-permute-start(bf16[2,96,2176]{2,1,0:T(8,128)(2,1)} %get-tuple-element.97), channel_id=1, source_target_pairs={{0,2},{2,0},{4,6},{6,4},{8,10},{10,8},{12,14},{14,12},{16,18},{18,... | collective-permute-start | bytes 2506760 | tf_op jit(solution)/shard_map/ppermute | solution.py:377
  77.3 3.5 %collective-permute-start.13 = (bf16[96,4224]{1,0:T(8,128)(2,1)S(1)}, bf16[96,4224]{1,0:T(8,128)(2,1)S(1)}, u32[]{:S(2)}, u32[]{:S(2)}) collective-permute-start(bf16[96,4224]{1,0:T(8,128)(2,1)S(1)} %shard_map.120.refs_0_), channel_id=1, source_target_pairs={{0,2},{2,0},{4,6},{6,4},{8,10},{10,8},{12,14},{14,12},{16,18},{18,... | collective-permute-start | bytes 2433032 | tf_op jit(solution)/shard_map/ppermute | solution.py:377
  77.7 4.2 %collective-permute-start.15 = (bf16[96,4224]{1,0:T(8,128)(2,1)S(1)}, bf16[96,4224]{1,0:T(8,128)(2,1)S(1)}, u32[]{:S(2)}, u32[]{:S(2)}) collective-permute-start(bf16[96,4224]{1,0:T(8,128)(2,1)S(1)} %shard_map.121.refs_2_), channel_id=1, source_target_pairs={{0,2},{2,0},{4,6},{6,4},{8,10},{10,8},{12,14},{14,12},{16,18},{18,... | collective-permute-start | bytes 2433032 | tf_op jit(solution)/shard_map/ppermute | solution.py:377
  77.8 20.4 %collective-permute-start.18 = (bf16[96,4224]{1,0:T(8,128)(2,1)S(1)}, bf16[96,4224]{1,0:T(8,128)(2,1)S(1)}, u32[]{:S(2)}, u32[]{:S(2)}) collective-permute-start(bf16[96,4224]{1,0:T(8,128)(2,1)S(1)} %shard_map.121.refs_2_), channel_id=1, source_target_pairs={{0,4},{2,6},{4,0},{6,2},{8,12},{10,14},{12,8},{14,10},{16,20},{18,... | collective-permute-start | bytes 2433032 | tf_op jit(solution)/shard_map/ppermute | solution.py:377
  89.4 24.3 %collective-permute-start.24 = (bf16[216,2304]{1,0:T(8,128)(2,1)}, bf16[216,2304]{1,0:T(8,128)(2,1)S(1)}, u32[]{:S(2)}, u32[]{:S(2)}) collective-permute-start(bf16[216,2304]{1,0:T(8,128)(2,1)} %get-tuple-element.114.refs_0_), channel_id=1, source_target_pairs={{0,1},{1,0},{2,3},{3,2},{4,5},{5,4},{6,7},{7,6},{8,9},{9,8},{10,11... | collective-permute-start | bytes 2985992 | tf_op jit(solution)/shard_map/ppermute | solution.py:385
  97.8 3.5 %collective-permute-start.21 = (bf16[2,96,2176]{2,1,0:T(8,128)(2,1)}, bf16[2,96,2176]{2,1,0:T(8,128)(2,1)S(1)}, u32[]{:S(2)}, u32[]{:S(2)}) collective-permute-start(bf16[2,96,2176]{2,1,0:T(8,128)(2,1)} %get-tuple-element.111), channel_id=1, source_target_pairs={{0,2},{2,0},{4,6},{6,4},{8,10},{10,8},{12,14},{14,12},{16,18},{18,... | collective-permute-start | bytes 2506760 | tf_op jit(solution)/shard_map/ppermute | solution.py:377
  98.2 3.0 %collective-permute-start.20 = (bf16[96,4224]{1,0:T(8,128)(2,1)S(1)}, bf16[96,4224]{1,0:T(8,128)(2,1)S(1)}, u32[]{:S(2)}, u32[]{:S(2)}) collective-permute-start(bf16[96,4224]{1,0:T(8,128)(2,1)S(1)} %shard_map.124.refs_0_), channel_id=1, source_target_pairs={{0,2},{2,0},{4,6},{6,4},{8,10},{10,8},{12,14},{14,12},{16,18},{18,... | collective-permute-start | bytes 2433032 | tf_op jit(solution)/shard_map/ppermute | solution.py:377
  113.7 6.9 %copy-start.16 = (s32[96,8]{0,1:T(8,128)S(1)}, s32[96,8]{0,1:T(8,128)}, u32[]{:S(2)}) copy-start(s32[96,8]{0,1:T(8,128)} %param.9) | copy-start | bytes 9220
  120.6 3.7 %collective-permute-start.25 = (bf16[2,96,2176]{2,1,0:T(8,128)(2,1)}, bf16[2,96,2176]{2,1,0:T(8,128)(2,1)}, u32[]{:S(2)}, u32[]{:S(2)}) collective-permute-start(bf16[2,96,2176]{2,1,0:T(8,128)(2,1)} %get-tuple-element.122), channel_id=1, source_target_pairs={{0,2},{2,0},{4,6},{6,4},{8,10},{10,8},{12,14},{14,12},{16,18},{18,... | collective-permute-start | bytes 2506760 | tf_op jit(solution)/shard_map/ppermute | solution.py:377
  120.7 59.1 %collective-permute-start.17 = (bf16[96,2176]{1,0:T(8,128)(2,1)}, bf16[96,2176]{1,0:T(8,128)(2,1)S(1)}, u32[]{:S(2)}, u32[]{:S(2)}) collective-permute-start(bf16[96,2176]{1,0:T(8,128)(2,1)} %get-tuple-element.98), channel_id=1, source_target_pairs={{0,4},{2,6},{4,0},{6,2},{8,12},{10,14},{12,8},{14,10},{16,20},{18,... | collective-permute-start | bytes 1253384 | tf_op jit(solution)/shard_map/ppermute | solution.py:377
  121.8 22.5 %collective-permute-start.22 = (bf16[96,2176]{1,0:T(8,128)(2,1)}, bf16[96,2176]{1,0:T(8,128)(2,1)S(1)}, u32[]{:S(2)}, u32[]{:S(2)}) collective-permute-start(bf16[96,2176]{1,0:T(8,128)(2,1)} %get-tuple-element.112), channel_id=1, source_target_pairs={{0,4},{2,6},{4,0},{6,2},{8,12},{10,14},{12,8},{14,10},{16,20},{18,... | collective-permute-start | bytes 1253384 | tf_op jit(solution)/shard_map/ppermute | solution.py:377
  122.8 13.8 %collective-permute-start.28 = (bf16[108,2304]{1,0:T(8,128)(2,1)}, bf16[108,2304]{1,0:T(8,128)(2,1)S(1)}, u32[]{:S(2)}, u32[]{:S(2)}) collective-permute-start(bf16[108,2304]{1,0:T(8,128)(2,1)} %get-tuple-element.123.refs_0_), channel_id=1, source_target_pairs={{0,1},{1,0},{2,3},{3,2},{4,5},{5,4},{6,7},{7,6},{8,9},{9,8},{10,11... | collective-permute-start | bytes 1493000 | tf_op jit(solution)/shard_map/ppermute | solution.py:385
  136.6 1.9 copy-start.1
  138.5 5.9 %copy-start.13 = (bf16[96,2176]{1,0:T(8,128)(2,1)S(1)}, bf16[96,2176]{1,0:T(8,128)(2,1)}, u32[]{:S(2)}) copy-start(bf16[96,2176]{1,0:T(8,128)(2,1)} %get-tuple-element.99) | copy-start | bytes 1253380
  138.5 8.6 %copy-start.12 = (bf16[96,2176]{1,0:T(8,128)(2,1)S(1)}, bf16[96,2176]{1,0:T(8,128)(2,1)}, u32[]{:S(2)}) copy-start(bf16[96,2176]{1,0:T(8,128)(2,1)} %get-tuple-element.143.refs_7_) | copy-start | bytes 1253380
  138.5 21.1 %copy-start.14 = (bf16[96,2176]{1,0:T(8,128)(2,1)S(1)}, bf16[96,2176]{1,0:T(8,128)(2,1)}, u32[]{:S(2)}) copy-start(bf16[96,2176]{1,0:T(8,128)(2,1)} %get-tuple-element.113) | copy-start | bytes 1253380
  144.3 16.2 %copy-start.3 = (bf16[896,2048]{1,0:T(8,128)(2,1)S(1)}, bf16[896,2048]{1,0:T(8,128)(2,1)}, u32[]{:S(2)}) copy-start(bf16[896,2048]{1,0:T(8,128)(2,1)} %get-tuple-element.136.refs_0_) | copy-start | bytes 11010052
  144.3 4.3 %collective-permute-start.29 = (bf16[1,96,2176]{2,1,0:T(8,128)(2,1)}, bf16[1,96,2176]{2,1,0:T(8,128)(2,1)S(1)}, u32[]{:S(2)}, u32[]{:S(2)}) collective-permute-start(bf16[1,96,2176]{2,1,0:T(8,128)(2,1)} %get-tuple-element.131), channel_id=1, source_target_pairs={{0,2},{2,0},{4,6},{6,4},{8,10},{10,8},{12,14},{14,12},{16,18},{18,... | collective-permute-start | bytes 1253384 | tf_op jit(solution)/shard_map/ppermute | solution.py:377
  144.5 16.0 %copy-start.7 = (bf16[96,2176]{1,0:T(8,128)(2,1)}, bf16[96,2176]{1,0:T(8,128)(2,1)S(1)}, u32[]{:S(2)}) copy-start(bf16[96,2176]{1,0:T(8,128)(2,1)S(1)} %add_convert_fusion.5.refs_1_.refs_2_) | copy-start | bytes 1253380
  144.5 35.3 %collective-permute-start.23 = (bf16[96,2176]{1,0:T(8,128)(2,1)S(1)}, bf16[96,2176]{1,0:T(8,128)(2,1)S(1)}, u32[]{:S(2)}, u32[]{:S(2)}) collective-permute-start(bf16[96,2176]{1,0:T(8,128)(2,1)S(1)} %add_convert_fusion.5.refs_1_.refs_2_), channel_id=1, source_target_pairs={{0,24},{2,26},{4,28},{6,30},{8,0},{10,2},{12,4},{14,6},{16,8},{18,... | collective-permute-start | bytes 1253384 | tf_op jit(solution)/shard_map/ppermute | solution.py:377
  147.1 12.5 %collective-permute-start.26 = (bf16[96,2176]{1,0:T(8,128)(2,1)S(1)}, bf16[96,2176]{1,0:T(8,128)(2,1)S(1)}, u32[]{:S(2)}, u32[]{:S(2)}) collective-permute-start(bf16[96,2176]{1,0:T(8,128)(2,1)S(1)} %copy-done.12), channel_id=1, source_target_pairs={{0,4},{2,6},{4,0},{6,2},{8,12},{10,14},{12,8},{14,10},{16,20},{18,... | collective-permute-start | bytes 1253384 | tf_op jit(solution)/shard_map/ppermute | solution.py:377
  149.7 10.8 %copy-start.11 = (bf16[96,2176]{1,0:T(8,128)(2,1)}, bf16[96,2176]{1,0:T(8,128)(2,1)S(1)}, u32[]{:S(2)}) copy-start(bf16[96,2176]{1,0:T(8,128)(2,1)S(1)} %fusion.5.refs_1_) | copy-start | bytes 1253380
  149.7 18.0 %collective-permute-start.30 = (bf16[96,2176]{1,0:T(8,128)(2,1)S(1)}, bf16[96,2176]{1,0:T(8,128)(2,1)S(1)}, u32[]{:S(2)}, u32[]{:S(2)}) collective-permute-start(bf16[96,2176]{1,0:T(8,128)(2,1)S(1)} %fusion.5.refs_1_), channel_id=1, source_target_pairs={{0,4},{2,6},{4,0},{6,2},{8,12},{10,14},{12,8},{14,10},{16,20},{18,... | collective-permute-start | bytes 1253384 | tf_op jit(solution)/shard_map/ppermute | solution.py:377
  159.7 0.8 copy-start.8
  159.7 28.2 %collective-permute-start.27 = (bf16[96,2176]{1,0:T(8,128)(2,1)S(1)}, bf16[96,2176]{1,0:T(8,128)(2,1)S(1)}, u32[]{:S(2)}, u32[]{:S(2)}) collective-permute-start(bf16[96,2176]{1,0:T(8,128)(2,1)S(1)} %add_convert_fusion.3.refs_2_.refs_3_), channel_id=1, source_target_pairs={{0,16},{2,18},{4,20},{6,22},{8,24},{10,26},{12,28},{14,30},{16,0},... | collective-permute-start | bytes 1253384 | tf_op jit(solution)/shard_map/ppermute | solution.py:377
  160.5 1.3 copy-start.4
  161.8 5.9 %copy-start.9 = (bf16[96,2176]{1,0:T(8,128)(2,1)S(1)}, bf16[96,2176]{1,0:T(8,128)(2,1)}, u32[]{:S(2)}) copy-start(bf16[96,2176]{1,0:T(8,128)(2,1)} %get-tuple-element.142.refs_8_) | copy-start | bytes 1253380
  161.8 6.8 %copy-start.2 = (bf16[896,2048]{1,0:T(8,128)(2,1)S(1)}, bf16[896,2048]{1,0:T(8,128)(2,1)}, u32[]{:S(2)}) copy-start(bf16[896,2048]{1,0:T(8,128)(2,1)} %get-tuple-element.132.refs_0_) | copy-start | bytes 11010052
  167.9 0.8 copy-start.10
  167.9 20.0 %collective-permute-start.31 = (bf16[96,2176]{1,0:T(8,128)(2,1)S(1)}, bf16[96,2176]{1,0:T(8,128)(2,1)S(1)}, u32[]{:S(2)}, u32[]{:S(2)}) collective-permute-start(bf16[96,2176]{1,0:T(8,128)(2,1)S(1)} %add_convert_fusion.refs_3_), channel_id=1, source_target_pairs={{0,8},{2,10},{4,12},{6,14},{8,16},{10,18},{12,20},{14,22},{16,24},... | collective-permute-start | bytes 1253384 | tf_op jit(solution)/shard_map/ppermute | solution.py:377
  168.6 1.3 copy-start.6
  170.0 4.9 %copy-start.5 = (bf16[896,768]{1,0:T(8,128)(2,1)S(1)}, bf16[896,768]{1,0:T(8,128)(2,1)}, u32[]{:S(2)}) copy-start(bf16[896,768]{1,0:T(8,128)(2,1)} %get-tuple-element.133) | copy-start | bytes 4128772
  174.9 13.0 %copy-start.15 = (bf16[96,2176]{1,0:T(8,128)(2,1)S(1)}, bf16[96,2176]{1,0:T(8,128)(2,1)}, u32[]{:S(2)}) copy-start(bf16[96,2176]{1,0:T(8,128)(2,1)} %get-tuple-element.83) | copy-start | bytes 1253380

commit v3 on v2

--- a/solution.py
+++ b/solution.py
@@ -94,7 +94,7 @@
         input_output_aliases={0: 0},
         compiler_params=pltpu.CompilerParams(vmem_limit_bytes=1024 * 1024),
         cost_estimate=COST,
-    )(x, *in_hbm(after))
+    )(x, *after)
 
 
 def block_kernel(tokens, cotangent, ids, gates, out):
@@ -212,7 +212,7 @@
     slab = lambda width: pl.BlockSpec((pad, width), lambda i: (index, 0))
     n_add = added[0].shape[0] if added else 0
     in_specs = [whole(b.shape) for b in blocks] + [ANY if fresh else VMEM] * 3 + [ANY] * (len(after) + len(slabs))
-    args = list(blocks) + (in_hbm(weights) if fresh else in_vmem(weights)) + in_hbm(after)
+    args = list(blocks) + (in_hbm(weights) if fresh else in_vmem(weights)) + in_hbm(after[:1]) + list(after[1:])
     aliases = {len(args) + i: 1 + i for i in range(len(slabs))}
     args += [*slabs, *in_hbm(added[:1]), *added[1:]]
     in_specs += [whole(a.shape) for a in added]
@@ -328,7 +328,7 @@
     wide = feat + LANES
     whole = lambda shape: pl.BlockSpec(shape, lambda i: (0,) * len(shape))
     slab = pl.BlockSpec((pad, hid), lambda i: (index, 0))
-    args = in_hbm(parts[:1]) + list(parts[1:]) + in_hbm([st, grow]) + in_vmem([wg, wu]) + in_hbm(after)
+    args = in_hbm(parts[:1]) + list(parts[1:]) + in_hbm([st, grow]) + in_vmem([wg, wu]) + in_hbm(after[:1]) + list(after[1:])
     in_specs = [whole(a.shape) for a in args[: len(parts) + 2]] + [VMEM] * 2 + [ANY] * len(after)
     aliases = {}
     if slabs:
@@ -416,8 +416,6 @@
     send_on(0)
     x_slab = act_slab = ()
     returned = {}
-    outgoing = {}
-    totals = []
 
     def finish(entry, after):
         nonlocal act_slab
@@ -433,47 +431,69 @@
     def give_back(chunk, sums):
         for (k, j), value in zip(chunk, sums):
             returned[k, j] = move(value, dy=-j) if j else value
-        for k in {k: None for k, _ in chunk}:
-            if all((k, j) in returned for j in range(columns)):
-                summed = sum(returned[k, j].astype(F32) for j in range(columns))
-                if k:
-                    outgoing[k] = summed.astype(BF)
-                    summed = move(outgoing[k], dz=-k).astype(F32)
-                totals.append(summed)
+
+    def gather_plane(k):
+        return [returned[k, j] for j in range(columns)]
+
+    def total(values):
+        return sum(v.astype(F32) for v in values[1:]) + values[0].astype(F32)
 
     held = (wg, wu, wd)
-    entries, unsent = [], []
-    sent = token = None
-    for n, chunk in enumerate(chunks):
+    entries, unsent = {}, {}
+    mark = None
+
+    def arrive(piece, after):
+        if piece not in arrived:
+            arrived[piece] = tie(pending.pop(piece), *after)
+            if piece[1] == 0:
+                send_on(piece[0])
+
+    def go_forward(n, after, added, more=()):
+        nonlocal x_slab, held
         blocks = []
-        for piece in chunk:
-            if piece not in arrived:
-                arrived[piece] = tie(pending.pop(piece), token)
-                if piece[1] == 0:
-                    send_on(piece[0])
+        for piece in chunks[n]:
+            arrive(piece, after)
             blocks += [arrived[piece], move(arrived[piece], dc=1)]
-        added = unsent.pop(0) if unsent else None
+        halves = unsent.pop(added, ())
         (part, *x_slab, st, grow, sent), sums, loaded = forward_call(
-            starts[n], total_rows, len(chunk) * unit, blocks, held, n == 0, cap, x_slab,
-            [] if token is None else [token], added[1] if added else ()
+            starts[n], total_rows, len(chunks[n]) * unit, blocks, held, n == 0, cap, x_slab,
+            [x for x in [mark, *more] if x is not None], halves
         )
         held = loaded or held
-        if added:
-            give_back(added[0], sums)
-        entries.append((starts[n], chunk, swap(part), st, grow))
-        if n != 1:
-            done = entries.pop(0)
-            token, halves = finish(done, [sent])
-            unsent.append((done[1], halves))
-    for last_chunk, halves in unsent:
-        sums = add(*halves)
-        give_back(last_chunk, sums)
-    done = entries.pop(0)
-    token, halves = finish(done, [token, *sums])
-    sums = add(*halves)
-    give_back(done[1], sums)
-
-    totals = sum(totals[1:], totals[0])
+        if halves:
+            give_back(chunks[added], sums)
+        entries[n] = (starts[n], chunks[n], swap(part), st, grow)
+        return sent
+
+    def go_back(n, after):
+        token, unsent[n] = finish(entries.pop(n), after)
+        return token
+
+    count = len(chunks)
+    mark = go_forward(0, [], None)
+    first = entries[0][2][1:]
+    mark = go_back(0, [mark])
+    mark = go_forward(1, first, None)
+    for n in range(2, count):
+        mark = go_forward(n, [mark], n - 2, ())
+        mark = go_back(n - 1, [mark] + ([v for p, v in returned.items() if p[1]][:columns - 1] if n == count - 1 else []))
+    sent_back = [v for p, v in returned.items() if p[1]]
+    for n in list(unsent):
+        sums = add(*unsent.pop(n))
+        give_back(chunks[n], sums)
+    mark = go_back(count - 1, [mark, *sums, *sent_back])
+    sums = add(*unsent.pop(count - 1))
+    give_back(chunks[-1], sums)
+
+    up, down, leaving = [], [], []
+    for k in range(planes // 2, 0, -1):
+        leaving.append(total(gather_plane(k) + up).astype(BF))
+        up = [move(leaving[-1], dz=-1)]
+    for k in range(planes // 2 + 1, planes):
+        leaving.append(total(gather_plane(k) + down).astype(BF))
+        down = [move(leaving[-1], dz=1)]
+    totals = total(gather_plane(0) + up + down)
+
     input_grad = totals[:, :feat].astype(BF)
     slots = totals[:, feat:]
     gate_grad = jnp.sum(jnp.where(hit, slots[:, None, :], 0.0), axis=2).astype(BF)
@@ -481,15 +501,16 @@
     wgrad = lambda a, b: lax.dot_general(a, b, contract_rows, preferred_element_type=F32).astype(BF)[None]
     x_all, sd_all = x_slab
     act_all, pg_all, pu_all = act_slab
-    leaving = list(outgoing.values())
-    down = wgrad(act_all, tie(sd_all, *sums, *leaving[:-1]))
+    down_grad = wgrad(act_all, tie(sd_all, leaving[0]))
     x_all = tie(x_all, *leaving)
+    gate_w_grad = wgrad(x_all, pg_all)
+    up_w_grad = wgrad(x_all, pu_all)
     return (
         input_grad,
         gate_grad,
-        wgrad(x_all, pg_all),
-        wgrad(x_all, pu_all),
-        down,
+        gate_w_grad,
+        up_w_grad,
+        down_grad,
     )
 
 

time: 191 us -> 182 us (0.953)
  waiting for transfers between devices: 68.6 us -> 52.7 us
  local copies, waits for them, and re-layouts: 6.39 us -> 9.84 us
  starting transfers between devices: 28.5 us -> 31.4 us
    ppermute x5, waiting for transfers between devices: 32.5 us -> 9.26 us  [swap(): return [part, lax.ppermute(part, 'seq', [(0, 1), (1, 0)])]]
    ppermute x27, waiting for transfers between devices: 36.1 us -> 43.4 us  [move(): return lax.ppermute(x, 'expert', shift(**by))]
    unnamed x38 -> x40, local copies, waits for them, and re-layouts: 5.58 us -> 9.04 us
    ppermute x27, starting transfers between devices: 20.9 us -> 23.6 us  [move(): return lax.ppermute(x, 'expert', shift(**by))]
    convert_element_type x3, other arithmetic: 0.3 us -> 2.36 us  [the longest x2 2.26 us: local(): leaving.append(total(gather_plane(k) + up).astype(BF))]
  transfers between devices with their start and end apart: 32 -> 32, of which waited for: 14 -> 16; matrix products, arithmetic and copies ran while one was open for 10% -> 11% of each run, Pallas kernels for 31% -> 32%
where the time goes in v3:
time: 182 us; the launch traced here: 181 us
  Pallas kernels  66.5 us (37%)
  waiting for transfers between devices  52.7 us (29%)
  starting transfers between devices  31.4 us (17%)
  matrix products  14.7 us (8%)
  local copies, waits for them, and re-layouts  9.84 us (5%)
  other arithmetic  5.23 us (3%)
    ppermute x27, waiting for transfers between devices, move(): return lax.ppermute(x, 'expert', shift(**by))  43.4 us
    pallas_call x5, Pallas kernels, forward_call(): pl.pallas_call(functools.partial(forward_kernel, cfg), grid=(hid // tile,...  32.8 us
    pallas_call x5, Pallas kernels, backward_call(): pl.pallas_call(functools.partial(backward_kernel, inner, tok, feat, hid,...  32.4 us
    ppermute x27, starting transfers between devices, move(): return lax.ppermute(x, 'expert', shift(**by))  23.6 us
    dot_general x3, matrix products, local(): lax.dot_general(a, b, contract_rows, preferred_element_type=F32).astype(BF)  14.7 us
    ppermute x5, waiting for transfers between devices, swap(): return [part, lax.ppermute(part, 'seq', [(0, 1), (1, 0)])]  9.26 us
    unnamed x40, local copies, waits for them, and re-layouts  9.04 us
    ppermute x5, starting transfers between devices, swap(): return [part, lax.ppermute(part, 'seq', [(0, 1), (1, 0)])]  7.72 us
  transfers between devices with their start and end apart: 32, of which 16 were waited for; matrix products, arithmetic and copies ran while one was open for 11% of the time, Pallas kernels for 32%

profile of v3, /device:TPU:0, one launch (start us, length us, event | category | flops | bytes accessed | tf_op | source)
XLA Modules:
  0.0 181.2 jit_solution(656533012758074039)
XLA Ops:
  0.6 1.3 shard_map.110.refs_0_
  1.9 0.5 collective-permute-start.1
  2.4 2.6 %collective-permute-start = (bf16[96,4224]{1,0:T(8,128)(2,1)S(1)}, bf16[96,4224]{1,0:T(8,128)(2,1)S(1)}, u32[]{:S(2)}, u32[]{:S(2)}) collective-permute-start(bf16[96,4224]{1,0:T(8,128)(2,1)S(1)} %shard_map.110.refs_0_), channel_id=1, source_target_pairs={{0,8},{2,10},{4,12},{6,14},{8,16},{10,18},{12,20},{14,22},{16,24},... | collective-permute-start | bytes 2433032 | tf_op jit(solution)/shard_map/ppermute | solution.py:377
  5.1 1.5 collective-permute-start.4
  6.6 7.4 %shard_map.111 = (bf16[108,2304]{1,0:T(8,128)(2,1)}, bf16[896,2048]{1,0:T(8,128)(2,1)}, bf16[896,2048]{1,0:T(8,128)(2,1)}, bf16[192,112]{1,0:T(8,128)(2,1)}, bf1...) custom-call(bf16[96,4224]{1,0:T(8,128)(2,1)S(1)} %shard_map.110.refs, ...), custom_call_target="tpu_custom_call" | custom-call | flops 1000 | bytes 1000 | tf_op jit(solution)/shard_map/pallas_call | solution.py:249
  14.0 1.6 collective-permute-start.2
  15.6 10.2 %collective-permute-done.refs_0_ = bf16[96,4224]{1,0:T(8,128)(2,1)S(1)} collective-permute-done((bf16[96,4224]{1,0:T(8,128)(2,1)S(1)}, bf16[96,4224]{1,0:T(8,128)(2,1)S(1)}, u32[]{:S(2)}, u32[]{:S(2)}) %collective-permute-start) | collective-permute-done | bytes 811040 | tf_op jit(solution)/shard_map/ppermute | solution.py:377
  25.8 2.1 %collective-permute-done.2.refs_1_ = bf16[108,2304]{1,0:T(8,128)(2,1)S(1)} collective-permute-done((bf16[108,2304]{1,0:T(8,128)(2,1)}, bf16[108,2304]{1,0:T(8,128)(2,1)S(1)}, u32[]{:S(2)}, u32[]{:S(2)}) %collective-permute-start.2) | collective-permute-done | bytes 497696 | tf_op jit(solution)/shard_map/ppermute | solution.py:385
  27.8 0.5 collective-permute-start.5
  28.3 1.6 collective-permute-start.3
  29.9 0.9 collective-permute-start.9
  30.8 5.7 %shard_map.114 = (bf16[1,96,2176]{2,1,0:T(8,128)(2,1)}, bf16[1,96,2176]{2,1,0:T(8,128)(2,1)}, bf16[896,768]{1,0:T(8,128)(2,1)}, bf16[896,768]{1,0:T(8,128)(2,1)}...) custom-call(bf16[108,2304]{1,0:T(8,128)(2,1)} %get-tuple-element.72.refs_0_, ...), custom_call_target="tpu_custom_call" | custom-call | flops 1000 | bytes 1000 | tf_op jit(solution)/shard_map/pallas_call | solution.py:340
  36.5 5.7 %shard_map.115 = (bf16[216,2304]{1,0:T(8,128)(2,1)}, bf16[896,2048]{1,0:T(8,128)(2,1)}, bf16[896,2048]{1,0:T(8,128)(2,1)}, bf16[384,224]{1,0:T(8,128)(2,1)}, bf16[224,128]{1,0:T(8,128)(2,1)}, /*index=5*/f32[8,128]{1,0:T(8,128)}) custom-call(bf16[96,4224]{1,0:T(8,128)(2,1)S(1)} %shard_map.113.refs_0_, ...), custom_call_target="tpu_custom_call", output_to_operand_aliasing={{1}: (8, {}), {2}: (9, {})} | custom-call | flops 1000 | bytes 1000 | tf_op jit(solution)/shard_map/pallas_call | solution.py:249
  42.2 1.5 collective-permute-start.8
  43.7 6.5 %collective-permute-done.3.refs_0_ = bf16[96,4224]{1,0:T(8,128)(2,1)S(1)} collective-permute-done((bf16[96,4224]{1,0:T(8,128)(2,1)S(1)}, bf16[96,4224]{1,0:T(8,128)(2,1)S(1)}, u32[]{:S(2)}, u32[]{:S(2)}) %collective-permute-start.3) | collective-permute-done | bytes 811040 | tf_op jit(solution)/shard_map/ppermute | solution.py:377
  50.2 0.7 copy-done.7
  50.9 0.5 collective-permute-start.10
  51.4 1.2 collective-permute-start.14
  52.6 1.5 collective-permute-start.7
  54.3 6.6 %shard_map.118 = (bf16[216,2304]{1,0:T(8,128)(2,1)}, bf16[896,2048]{1,0:T(8,128)(2,1)}, bf16[896,2048]{1,0:T(8,128)(2,1)}, bf16[384,224]{1,0:T(8,128)(2,1)}, bf1...) custom-call(bf16[96,4224]{1,0:T(8,128)(2,1)S(1)} %shard_map.117.refs, ...), custom_call_target="tpu_custom_call", output_to_operand_aliasing={{1}: (8, {}), {2}: (9, {})} | custom-call | flops 1000 | bytes 1000 | tf_op jit(solution)/shard_map/pallas_call | solution.py:249
  61.0 1.6 collective-permute-start.19
  62.5 4.7 %collective-permute-done.8.refs_1_ = bf16[216,2304]{1,0:T(8,128)(2,1)S(1)} collective-permute-done((bf16[216,2304]{1,0:T(8,128)(2,1)}, bf16[216,2304]{1,0:T(8,128)(2,1)S(1)}, u32[]{:S(2)}, u32[]{:S(2)}) %collective-permute-start.8) | collective-permute-done | bytes 995360 | tf_op jit(solution)/shard_map/ppermute | solution.py:385
  67.2 6.9 %shard_map.119 = (bf16[2,96,2176]{2,1,0:T(8,128)(2,1)}, bf16[2,96,2176]{2,1,0:T(8,128)(2,1)}, bf16[896,768]{1,0:T(8,128)(2,1)}, bf16[896,768]{1,0:T(8,128)(2,1)}...) custom-call(bf16[216,2304]{1,0:T(8,128)(2,1)} %get-tuple-element.83.refs_, ...), custom_call_target="tpu_custom_call", output_to_operand_aliasing={{2}: (7, {}), {3}: (8, {}), {4}: (9, {})} | custom-call | flops 1000 | bytes 1000 | tf_op jit(solution)/shard_map/pallas_call | solution.py:340
  74.1 0.7 copy-done.8
  74.8 0.5 collective-permute-start.15
  75.4 1.1 collective-permute-start.18
  76.4 1.2 collective-permute-done.15.refs_3_
  77.6 1.2 collective-permute-done.13.refs_1_
  78.8 7.5 %shard_map.122 = (bf16[216,2304]{1,0:T(8,128)(2,1)}, bf16[896,2048]{1,0:T(8,128)(2,1)}, bf16[896,2048]{1,0:T(8,128)(2,1)}, bf16[384,224]{1,0:T(8,128)(2,1)}, bf1...) custom-call(bf16[96,4224]{1,0:T(8,128)(2,1)S(1)} %shard_map.120.refs, ...), custom_call_target="tpu_custom_call", output_to_operand_aliasing={{1}: (8, {}), {2}: (9, {})} | custom-call | flops 1000 | bytes 1000 | tf_op jit(solution)/shard_map/pallas_call | solution.py:249
  86.3 1.6 collective-permute-start.23
  87.8 0.3 collective-permute-done.19.refs_1_
  88.1 6.9 %shard_map.123 = (bf16[2,96,2176]{2,1,0:T(8,128)(2,1)}, bf16[2,96,2176]{2,1,0:T(8,128)(2,1)}, bf16[896,768]{1,0:T(8,128)(2,1)}, bf16[896,768]{1,0:T(8,128)(2,1)}...) custom-call(bf16[216,2304]{1,0:T(8,128)(2,1)} %get-tuple-element.100.refs, ...), custom_call_target="tpu_custom_call", output_to_operand_aliasing={{2}: (7, {}), {3}: (8, {}), {4}: (9, {})} | custom-call | flops 1000 | bytes 1000 | tf_op jit(solution)/shard_map/pallas_call | solution.py:340
  95.0 0.7 collective-permute-done.18.refs_0_
  95.8 0.7 copy-done.9
  96.5 1.1 collective-permute-start.17
  97.5 1.2 collective-permute-done.20.refs_1_
  98.8 5.7 %shard_map.125 = (bf16[108,2304]{1,0:T(8,128)(2,1)}, bf16[896,2048]{1,0:T(8,128)(2,1)}, bf16[896,2048]{1,0:T(8,128)(2,1)}, bf16[192,112]{1,0:T(8,128)(2,1)}, bf1...) custom-call(bf16[96,4224]{1,0:T(8,128)(2,1)S(1)} %shard_map.124.refs, ...), custom_call_target="tpu_custom_call", output_to_operand_aliasing={{1}: (6, {}), {2}: (7, {})} | custom-call | flops 1000 | bytes 1000 | tf_op jit(solution)/shard_map/pallas_call | solution.py:249
  104.4 4.1 %collective-permute-done.17.refs_7_.refs_9_ = bf16[96,2176]{1,0:T(8,128)(2,1)S(1)} collective-permute-done((bf16[96,2176]{1,0:T(8,128)(2,1)S(1)}, bf16[96,2176]{1,0:T(8,128)(2,1)S(1)}, u32[]{:S(2)}, u32[]{:S(2)}) %collective-permute-start.17) | collective-permute-done | bytes 417824 | tf_op jit(solution)/shard_map/ppermute | solution.py:377
  108.5 2.1 %collective-permute-done.23.refs_1_ = bf16[216,2304]{1,0:T(8,128)(2,1)S(1)} collective-permute-done((bf16[216,2304]{1,0:T(8,128)(2,1)}, bf16[216,2304]{1,0:T(8,128)(2,1)S(1)}, u32[]{:S(2)}, u32[]{:S(2)}) %collective-permute-start.23) | collective-permute-done | bytes 995360 | tf_op jit(solution)/shard_map/ppermute | solution.py:385
  110.6 6.9 %shard_map.126 = (bf16[2,96,2176]{2,1,0:T(8,128)(2,1)}, bf16[2,96,2176]{2,1,0:T(8,128)(2,1)}, bf16[896,768]{1,0:T(8,128)(2,1)}, bf16[896,768]{1,0:T(8,128)(2,1)}...) custom-call(bf16[216,2304]{1,0:T(8,128)(2,1)} %get-tuple-element.113.ref, ...), custom_call_target="tpu_custom_call", output_to_operand_aliasing={{2}: (8, {}), {3}: (9, {}), {4}: (10, {})} | custom-call | flops 1000 | bytes 1000 | tf_op jit(solution)/shard_map/pallas_call | solution.py:340
  117.6 1.6 collective-permute-start.28
  119.2 1.1 collective-permute-start.22
  120.3 2.2 %fusion.3 = (bf16[96,2176]{1,0:T(8,128)(2,1)}, bf16[96,2176]{1,0:T(8,128)(2,1)}) fusion(bf16[2,96,2176]{2,1,0:T(8,128)(2,1)S(1)} %collective-permute-done.24, bf16[2,96,2176]{2,1,0:T(8,128)(2,1)} %get-tuple-element.120), kind=kLoop, calls=%fused_computation.14 | loop fusion | flops 1671168 | bytes 2506752 | tf_op jit(solution)/shard_map/convert_element_type | solution.py:429
  122.5 1.0 collective-permute-start.25
  123.6 8.4 %collective-permute-done.22.refs_10_ = bf16[96,2176]{1,0:T(8,128)(2,1)} collective-permute-done((bf16[96,2176]{1,0:T(8,128)(2,1)}, bf16[96,2176]{1,0:T(8,128)(2,1)}, u32[]{:S(2)}, u32[]{:S(2)}) %collective-permute-start.22) | collective-permute-done | bytes 417824 | tf_op jit(solution)/shard_map/ppermute | solution.py:377
  132.1 1.9 %copy-done.1 = bf16[2048,768]{1,0:T(8,128)(2,1)S(1)} copy-done((bf16[2048,768]{1,0:T(8,128)(2,1)S(1)}, bf16[2048,768]{1,0:T(8,128)(2,1)}, u32[]{:S(2)}) %copy-start.1) | copy-done | bytes 3145752
  134.0 1.0 copy-done.4
  135.0 1.0 copy-done.6
  136.0 6.0 %shard_map.127 = (bf16[1,96,2176]{2,1,0:T(8,128)(2,1)}, bf16[1,96,2176]{2,1,0:T(8,128)(2,1)}, bf16[896,768]{1,0:T(8,128)(2,1)}, bf16[896,768]{1,0:T(8,128)(2,1)}...) custom-call(bf16[108,2304]{1,0:T(8,128)(2,1)} %get-tuple-element.124.r, ...), custom_call_target="tpu_custom_call", output_to_operand_aliasing={{2}: (11, {}), {3}: (12, {}), {4}: (13, {})} | custom-call | flops 1000 | bytes 1000 | tf_op jit(solution)/shard_map/pallas_call | solution.py:340
  142.0 1.1 add_convert_fusion.4.refs_1_
  143.2 2.5 %collective-permute-start.26 = (bf16[96,2176]{1,0:T(8,128)(2,1)S(1)}, bf16[96,2176]{1,0:T(8,128)(2,1)S(1)}, u32[]{:S(2)}, u32[]{:S(2)}) collective-permute-start(bf16[96,2176]{1,0:T(8,128)(2,1)S(1)} %add_convert_fusion.4.refs_1_), channel_id=1, source_target_pairs={{0,24},{2,26},{4,28},{6,30},{8,0},{10,2},{12,4},{14,6},{16,8},{18,... | collective-permute-start | bytes 1253384 | tf_op jit(solution)/shard_map/ppermute | solution.py:377
  145.7 1.0 copy-done.16
  146.8 1.2 collective-permute-start.30
  148.0 4.9 %fusion.2 = bf16[1,768,2048]{2,1,0:T(8,128)(2,1)} fusion(bf16[896,768]{1,0:T(8,128)(2,1)S(1)} %copy-done.10, bf16[896,2048]{1,0:T(8,128)(2,1)S(1)} %shard_map.129), kind=kOutput, calls=%fused_computation.5 | convolution fusion | flops 2820145152 | bytes 8192000 | tf_op jit(solution)/shard_map/dot_general | solution.py:501
  152.8 2.7 %collective-permute-done.26 = bf16[96,2176]{1,0:T(8,128)(2,1)S(1)} collective-permute-done((bf16[96,2176]{1,0:T(8,128)(2,1)S(1)}, bf16[96,2176]{1,0:T(8,128)(2,1)S(1)}, u32[]{:S(2)}, u32[]{:S(2)}) %collective-permute-start.26) | collective-permute-done | bytes 417824 | tf_op jit(solution)/shard_map/ppermute | solution.py:377
  155.5 1.2 add_convert_fusion.3.refs_2_
  156.6 4.1 %collective-permute-start.27 = (bf16[96,2176]{1,0:T(8,128)(2,1)S(1)}, bf16[96,2176]{1,0:T(8,128)(2,1)S(1)}, u32[]{:S(2)}, u32[]{:S(2)}) collective-permute-start(bf16[96,2176]{1,0:T(8,128)(2,1)S(1)} %add_convert_fusion.3.refs_2_), channel_id=1, source_target_pairs={{0,24},{2,26},{4,28},{6,30},{8,0},{10,2},{12,4},{14,6},{16,8},{18,... | collective-permute-start | bytes 1253384 | tf_op jit(solution)/shard_map/ppermute | solution.py:377
  160.9 1.3 copy-done.12
  162.2 4.9 %fusion.1 = bf16[1,2048,768]{2,1,0:T(8,128)(2,1)} fusion(bf16[896,2048]{1,0:T(8,128)(2,1)S(1)} %shard_map.128, bf16[896,768]{1,0:T(8,128)(2,1)S(1)} %copy-done.12), kind=kOutput, calls=%fused_computation.4 | convolution fusion | flops 2820145152 | bytes 8192000 | tf_op jit(solution)/shard_map/dot_general | solution.py:501
  167.2 4.9 %fusion = bf16[1,2048,768]{2,1,0:T(8,128)(2,1)} fusion(bf16[896,2048]{1,0:T(8,128)(2,1)S(1)} %shard_map.128, bf16[896,768]{1,0:T(8,128)(2,1)S(1)} %copy-done.11), kind=kOutput, calls=%fused_computation.3 | convolution fusion | flops 2820145152 | bytes 8192000 | tf_op jit(solution)/shard_map/dot_general | solution.py:501
  172.1 7.1 %collective-permute-done.31 = bf16[96,2176]{1,0:T(8,128)(2,1)S(1)} collective-permute-done((bf16[96,2176]{1,0:T(8,128)(2,1)S(1)}, bf16[96,2176]{1,0:T(8,128)(2,1)S(1)}, u32[]{:S(2)}, u32[]{:S(2)}) %collective-permute-start.31) | collective-permute-done | bytes 417824 | tf_op jit(solution)/shard_map/ppermute | solution.py:377
  179.4 0.8 slice.34
  180.2 0.3 select_reduce_fusion
  180.5 0.7 copy.43
  (72 shorter events, 1.2 us)
Async XLA Ops:
  1.9 4.7 %collective-permute-start.1 = (bf16[96,4224]{1,0:T(8,128)(2,1)S(1)}, bf16[96,4224]{1,0:T(8,128)(2,1)S(1)}, u32[]{:S(2)}, u32[]{:S(2)}) collective-permute-start(bf16[96,4224]{1,0:T(8,128)(2,1)S(1)} %shard_map.110.refs_0_), channel_id=1, source_target_pairs={{0,2},{2,0},{4,6},{6,4},{8,10},{10,8},{12,14},{14,12},{16,18},{18,... | collective-permute-start | bytes 2433032 | tf_op jit(solution)/shard_map/ppermute | solution.py:377
  2.4 23.3 %collective-permute-start = (bf16[96,4224]{1,0:T(8,128)(2,1)S(1)}, bf16[96,4224]{1,0:T(8,128)(2,1)S(1)}, u32[]{:S(2)}, u32[]{:S(2)}) collective-permute-start(bf16[96,4224]{1,0:T(8,128)(2,1)S(1)} %shard_map.110.refs_0_), channel_id=1, source_target_pairs={{0,8},{2,10},{4,12},{6,14},{8,16},{10,18},{12,20},{14,22},{16,24},... | collective-permute-start | bytes 2433032 | tf_op jit(solution)/shard_map/ppermute | solution.py:377
  5.1 22.8 %collective-permute-start.4 = (bf16[96,4224]{1,0:T(8,128)(2,1)S(1)}, bf16[96,4224]{1,0:T(8,128)(2,1)S(1)}, u32[]{:S(2)}, u32[]{:S(2)}) collective-permute-start(bf16[96,4224]{1,0:T(8,128)(2,1)S(1)} %shard_map.110.refs_0_), channel_id=1, source_target_pairs={{0,4},{2,6},{4,0},{6,2},{8,12},{10,14},{12,8},{14,10},{16,20},{18,... | collective-permute-start | bytes 2433032 | tf_op jit(solution)/shard_map/ppermute | solution.py:377
  14.0 96.6 %copy-start = (bf16[2048,768]{1,0:T(8,128)(2,1)}, bf16[2048,768]{1,0:T(8,128)(2,1)S(1)}, u32[]{:S(2)}) copy-start(bf16[2048,768]{1,0:T(8,128)(2,1)S(1)} %get-tuple-element.74.refs_5_.refs_3_) | copy-start | bytes 9437188
  14.0 13.8 %collective-permute-start.2 = (bf16[108,2304]{1,0:T(8,128)(2,1)}, bf16[108,2304]{1,0:T(8,128)(2,1)S(1)}, u32[]{:S(2)}, u32[]{:S(2)}) collective-permute-start(bf16[108,2304]{1,0:T(8,128)(2,1)} %get-tuple-element.72.refs_0_), channel_id=1, source_target_pairs={{0,1},{1,0},{2,3},{3,2},{4,5},{5,4},{6,7},{7,6},{8,9},{9,8},{10,11... | collective-permute-start | bytes 1493000 | tf_op jit(solution)/shard_map/ppermute | solution.py:385
  27.8 8.7 %collective-permute-start.6 = (bf16[96,4224]{1,0:T(8,128)(2,1)S(1)}, bf16[96,4224]{1,0:T(8,128)(2,1)S(1)}, u32[]{:S(2)}, u32[]{:S(2)}) collective-permute-start(bf16[96,4224]{1,0:T(8,128)(2,1)S(1)} %shard_map.112.refs_2_), channel_id=1, source_target_pairs={{0,2},{2,0},{4,6},{6,4},{8,10},{10,8},{12,14},{14,12},{16,18},{18,... | collective-permute-start | bytes 2433032 | tf_op jit(solution)/shard_map/ppermute | solution.py:377
  27.8 8.7 %collective-permute-start.5 = (bf16[96,4224]{1,0:T(8,128)(2,1)S(1)}, bf16[96,4224]{1,0:T(8,128)(2,1)S(1)}, u32[]{:S(2)}, u32[]{:S(2)}) collective-permute-start(bf16[96,4224]{1,0:T(8,128)(2,1)S(1)} %shard_map.113.refs_0_), channel_id=1, source_target_pairs={{0,2},{2,0},{4,6},{6,4},{8,10},{10,8},{12,14},{14,12},{16,18},{18,... | collective-permute-start | bytes 2433032 | tf_op jit(solution)/shard_map/ppermute | solution.py:377
  28.3 21.8 %collective-permute-start.3 = (bf16[96,4224]{1,0:T(8,128)(2,1)S(1)}, bf16[96,4224]{1,0:T(8,128)(2,1)S(1)}, u32[]{:S(2)}, u32[]{:S(2)}) collective-permute-start(bf16[96,4224]{1,0:T(8,128)(2,1)S(1)} %shard_map.112.refs_2_), channel_id=1, source_target_pairs={{0,8},{2,10},{4,12},{6,14},{8,16},{10,18},{12,20},{14,22},{16,24},... | collective-permute-start | bytes 2433032 | tf_op jit(solution)/shard_map/ppermute | solution.py:377
  29.9 21.0 %collective-permute-start.9 = (bf16[96,4224]{1,0:T(8,128)(2,1)S(1)}, bf16[96,4224]{1,0:T(8,128)(2,1)S(1)}, u32[]{:S(2)}, u32[]{:S(2)}) collective-permute-start(bf16[96,4224]{1,0:T(8,128)(2,1)S(1)} %shard_map.112.refs_2_), channel_id=1, source_target_pairs={{0,4},{2,6},{4,0},{6,2},{8,12},{10,14},{12,8},{14,10},{16,20},{18,... | collective-permute-start | bytes 2433032 | tf_op jit(solution)/shard_map/ppermute | solution.py:377
  36.5 16.1 %collective-permute-start.12 = (bf16[1,96,2176]{2,1,0:T(8,128)(2,1)}, bf16[1,96,2176]{2,1,0:T(8,128)(2,1)S(1)}, u32[]{:S(2)}, u32[]{:S(2)}) collective-permute-start(bf16[1,96,2176]{2,1,0:T(8,128)(2,1)} %get-tuple-element.89), channel_id=1, source_target_pairs={{0,2},{2,0},{4,6},{6,4},{8,10},{10,8},{12,14},{14,12},{16,18},{18,... | collective-permute-start | bytes 1253384 | tf_op jit(solution)/shard_map/ppermute | solution.py:377
  42.2 25.0 %collective-permute-start.8 = (bf16[216,2304]{1,0:T(8,128)(2,1)}, bf16[216,2304]{1,0:T(8,128)(2,1)S(1)}, u32[]{:S(2)}, u32[]{:S(2)}) collective-permute-start(bf16[216,2304]{1,0:T(8,128)(2,1)} %get-tuple-element.83.refs_0_), channel_id=1, source_target_pairs={{0,1},{1,0},{2,3},{3,2},{4,5},{5,4},{6,7},{7,6},{8,9},{9,8},{10,11... | collective-permute-start | bytes 2985992 | tf_op jit(solution)/shard_map/ppermute | solution.py:385
  50.2 0.7 copy-start.7
  50.9 3.3 %collective-permute-start.11 = (bf16[96,4224]{1,0:T(8,128)(2,1)S(1)}, bf16[96,4224]{1,0:T(8,128)(2,1)S(1)}, u32[]{:S(2)}, u32[]{:S(2)}) collective-permute-start(bf16[96,4224]{1,0:T(8,128)(2,1)S(1)} %shard_map.116.refs_2_), channel_id=1, source_target_pairs={{0,2},{2,0},{4,6},{6,4},{8,10},{10,8},{12,14},{14,12},{16,18},{18,... | collective-permute-start | bytes 2433032 | tf_op jit(solution)/shard_map/ppermute | solution.py:377
  50.9 3.5 %collective-permute-start.10 = (bf16[96,4224]{1,0:T(8,128)(2,1)S(1)}, bf16[96,4224]{1,0:T(8,128)(2,1)S(1)}, u32[]{:S(2)}, u32[]{:S(2)}) collective-permute-start(bf16[96,4224]{1,0:T(8,128)(2,1)S(1)} %shard_map.117.refs_0_), channel_id=1, source_target_pairs={{0,2},{2,0},{4,6},{6,4},{8,10},{10,8},{12,14},{14,12},{16,18},{18,... | collective-permute-start | bytes 2433032 | tf_op jit(solution)/shard_map/ppermute | solution.py:377
  51.4 22.7 %collective-permute-start.14 = (bf16[96,4224]{1,0:T(8,128)(2,1)S(1)}, bf16[96,4224]{1,0:T(8,128)(2,1)S(1)}, u32[]{:S(2)}, u32[]{:S(2)}) collective-permute-start(bf16[96,4224]{1,0:T(8,128)(2,1)S(1)} %shard_map.110.refs_0_), channel_id=1, source_target_pairs={{0,24},{2,26},{4,28},{6,30},{8,0},{10,2},{12,4},{14,6},{16,8},{18,... | collective-permute-start | bytes 2433032 | tf_op jit(solution)/shard_map/ppermute | solution.py:377
  52.6 22.7 %collective-permute-start.7 = (bf16[96,4224]{1,0:T(8,128)(2,1)S(1)}, bf16[96,4224]{1,0:T(8,128)(2,1)S(1)}, u32[]{:S(2)}, u32[]{:S(2)}) collective-permute-start(bf16[96,4224]{1,0:T(8,128)(2,1)S(1)} %shard_map.116.refs_2_), channel_id=1, source_target_pairs={{0,4},{2,6},{4,0},{6,2},{8,12},{10,14},{12,8},{14,10},{16,20},{18,... | collective-permute-start | bytes 2433032 | tf_op jit(solution)/shard_map/ppermute | solution.py:377
  61.0 27.2 %collective-permute-start.19 = (bf16[216,2304]{1,0:T(8,128)(2,1)}, bf16[216,2304]{1,0:T(8,128)(2,1)S(1)}, u32[]{:S(2)}, u32[]{:S(2)}) collective-permute-start(bf16[216,2304]{1,0:T(8,128)(2,1)} %get-tuple-element.100.refs_0_), channel_id=1, source_target_pairs={{0,1},{1,0},{2,3},{3,2},{4,5},{5,4},{6,7},{7,6},{8,9},{9,8},{10,11... | collective-permute-start | bytes 2985992 | tf_op jit(solution)/shard_map/ppermute | solution.py:385
  74.1 4.7 %collective-permute-start.16 = (bf16[2,96,2176]{2,1,0:T(8,128)(2,1)}, bf16[2,96,2176]{2,1,0:T(8,128)(2,1)S(1)}, u32[]{:S(2)}, u32[]{:S(2)}) collective-permute-start(bf16[2,96,2176]{2,1,0:T(8,128)(2,1)} %get-tuple-element.98), channel_id=1, source_target_pairs={{0,2},{2,0},{4,6},{6,4},{8,10},{10,8},{12,14},{14,12},{16,18},{18,... | collective-permute-start | bytes 2506760 | tf_op jit(solution)/shard_map/ppermute | solution.py:377
  74.1 0.7 copy-start.8
  74.8 2.8 %collective-permute-start.15 = (bf16[96,4224]{1,0:T(8,128)(2,1)S(1)}, bf16[96,4224]{1,0:T(8,128)(2,1)S(1)}, u32[]{:S(2)}, u32[]{:S(2)}) collective-permute-start(bf16[96,4224]{1,0:T(8,128)(2,1)S(1)} %shard_map.121.refs_2_), channel_id=1, source_target_pairs={{0,2},{2,0},{4,6},{6,4},{8,10},{10,8},{12,14},{14,12},{16,18},{18,... | collective-permute-start | bytes 2433032 | tf_op jit(solution)/shard_map/ppermute | solution.py:377
  75.3 3.5 %collective-permute-start.13 = (bf16[96,4224]{1,0:T(8,128)(2,1)S(1)}, bf16[96,4224]{1,0:T(8,128)(2,1)S(1)}, u32[]{:S(2)}, u32[]{:S(2)}) collective-permute-start(bf16[96,4224]{1,0:T(8,128)(2,1)S(1)} %shard_map.120.refs_0_), channel_id=1, source_target_pairs={{0,2},{2,0},{4,6},{6,4},{8,10},{10,8},{12,14},{14,12},{16,18},{18,... | collective-permute-start | bytes 2433032 | tf_op jit(solution)/shard_map/ppermute | solution.py:377
  75.4 20.4 %collective-permute-start.18 = (bf16[96,4224]{1,0:T(8,128)(2,1)S(1)}, bf16[96,4224]{1,0:T(8,128)(2,1)S(1)}, u32[]{:S(2)}, u32[]{:S(2)}) collective-permute-start(bf16[96,4224]{1,0:T(8,128)(2,1)S(1)} %shard_map.121.refs_2_), channel_id=1, source_target_pairs={{0,4},{2,6},{4,0},{6,2},{8,12},{10,14},{12,8},{14,10},{16,20},{18,... | collective-permute-start | bytes 2433032 | tf_op jit(solution)/shard_map/ppermute | solution.py:377
  86.3 24.3 %collective-permute-start.23 = (bf16[216,2304]{1,0:T(8,128)(2,1)}, bf16[216,2304]{1,0:T(8,128)(2,1)S(1)}, u32[]{:S(2)}, u32[]{:S(2)}) collective-permute-start(bf16[216,2304]{1,0:T(8,128)(2,1)} %get-tuple-element.113.refs_0_), channel_id=1, source_target_pairs={{0,1},{1,0},{2,3},{3,2},{4,5},{5,4},{6,7},{7,6},{8,9},{9,8},{10,11... | collective-permute-start | bytes 2985992 | tf_op jit(solution)/shard_map/ppermute | solution.py:385
  88.1 8.3 %copy-start.18 = (bf16[96,2176]{1,0:T(8,128)(2,1)S(1)}, bf16[96,2176]{1,0:T(8,128)(2,1)}, u32[]{:S(2)}) copy-start(bf16[96,2176]{1,0:T(8,128)(2,1)} %get-tuple-element.99) | copy-start | bytes 1253380
  95.0 3.7 %collective-permute-start.21 = (bf16[2,96,2176]{2,1,0:T(8,128)(2,1)}, bf16[2,96,2176]{2,1,0:T(8,128)(2,1)S(1)}, u32[]{:S(2)}, u32[]{:S(2)}) collective-permute-start(bf16[2,96,2176]{2,1,0:T(8,128)(2,1)} %get-tuple-element.111), channel_id=1, source_target_pairs={{0,2},{2,0},{4,6},{6,4},{8,10},{10,8},{12,14},{14,12},{16,18},{18,... | collective-permute-start | bytes 2506760 | tf_op jit(solution)/shard_map/ppermute | solution.py:377
  95.8 0.7 copy-start.9
  96.5 2.3 %collective-permute-start.20 = (bf16[96,4224]{1,0:T(8,128)(2,1)S(1)}, bf16[96,4224]{1,0:T(8,128)(2,1)S(1)}, u32[]{:S(2)}, u32[]{:S(2)}) collective-permute-start(bf16[96,4224]{1,0:T(8,128)(2,1)S(1)} %shard_map.124.refs_0_), channel_id=1, source_target_pairs={{0,2},{2,0},{4,6},{6,4},{8,10},{10,8},{12,14},{14,12},{16,18},{18,... | collective-permute-start | bytes 2433032 | tf_op jit(solution)/shard_map/ppermute | solution.py:377
  96.5 12.1 %collective-permute-start.17 = (bf16[96,2176]{1,0:T(8,128)(2,1)S(1)}, bf16[96,2176]{1,0:T(8,128)(2,1)S(1)}, u32[]{:S(2)}, u32[]{:S(2)}) collective-permute-start(bf16[96,2176]{1,0:T(8,128)(2,1)S(1)} %copy-done.18), channel_id=1, source_target_pairs={{0,4},{2,6},{4,0},{6,2},{8,12},{10,14},{12,8},{14,10},{16,20},{18,... | collective-permute-start | bytes 1253384 | tf_op jit(solution)/shard_map/ppermute | solution.py:377
  108.5 9.0 %copy-start.5 = (bf16[96,2176]{1,0:T(8,128)(2,1)}, bf16[96,2176]{1,0:T(8,128)(2,1)S(1)}, u32[]{:S(2)}) copy-start(bf16[96,2176]{1,0:T(8,128)(2,1)S(1)} %collective-permute-done.17.refs_7_.refs_9_) | copy-start | bytes 1253380
  110.6 12.9 %copy-start.17 = (s32[96,8]{0,1:T(8,128)S(1)}, s32[96,8]{0,1:T(8,128)}, u32[]{:S(2)}) copy-start(s32[96,8]{0,1:T(8,128)} %param.9) | copy-start | bytes 9220
  117.5 2.7 %collective-permute-start.24 = (bf16[2,96,2176]{2,1,0:T(8,128)(2,1)}, bf16[2,96,2176]{2,1,0:T(8,128)(2,1)S(1)}, u32[]{:S(2)}, u32[]{:S(2)}) collective-permute-start(bf16[2,96,2176]{2,1,0:T(8,128)(2,1)} %get-tuple-element.121), channel_id=1, source_target_pairs={{0,2},{2,0},{4,6},{6,4},{8,10},{10,8},{12,14},{14,12},{16,18},{18,... | collective-permute-start | bytes 2506760 | tf_op jit(solution)/shard_map/ppermute | solution.py:377
  117.6 14.5 %collective-permute-start.28 = (bf16[108,2304]{1,0:T(8,128)(2,1)}, bf16[108,2304]{1,0:T(8,128)(2,1)}, u32[]{:S(2)}, u32[]{:S(2)}) collective-permute-start(bf16[108,2304]{1,0:T(8,128)(2,1)} %get-tuple-element.124.refs_0_), channel_id=1, source_target_pairs={{0,1},{1,0},{2,3},{3,2},{4,5},{5,4},{6,7},{7,6},{8,9},{9,8},{10,11... | collective-permute-start | bytes 1493000 | tf_op jit(solution)/shard_map/ppermute | solution.py:385
  119.2 12.8 %collective-permute-start.22 = (bf16[96,2176]{1,0:T(8,128)(2,1)}, bf16[96,2176]{1,0:T(8,128)(2,1)}, u32[]{:S(2)}, u32[]{:S(2)}) collective-permute-start(bf16[96,2176]{1,0:T(8,128)(2,1)} %get-tuple-element.112), channel_id=1, source_target_pairs={{0,4},{2,6},{4,0},{6,2},{8,12},{10,14},{12,8},{14,10},{16,20},{18,... | collective-permute-start | bytes 1253384 | tf_op jit(solution)/shard_map/ppermute | solution.py:377
  122.5 19.5 %collective-permute-start.25 = (bf16[96,2176]{1,0:T(8,128)(2,1)}, bf16[96,2176]{1,0:T(8,128)(2,1)}, u32[]{:S(2)}, u32[]{:S(2)}) collective-permute-start(bf16[96,2176]{1,0:T(8,128)(2,1)} %get-tuple-element.144.refs_7_), channel_id=1, source_target_pairs={{0,4},{2,6},{4,0},{6,2},{8,12},{10,14},{12,8},{14,10},{16,20},{18,... | collective-permute-start | bytes 1253384 | tf_op jit(solution)/shard_map/ppermute | solution.py:377
  132.1 1.9 %copy-start.1 = (bf16[2048,768]{1,0:T(8,128)(2,1)S(1)}, bf16[2048,768]{1,0:T(8,128)(2,1)}, u32[]{:S(2)}) copy-start(bf16[2048,768]{1,0:T(8,128)(2,1)} %copy-done) | copy-start | bytes 9437188
  134.0 1.0 copy-start.4
  135.0 1.0 copy-start.6
  136.0 6.0 %copy-start.15 = (bf16[96,2176]{1,0:T(8,128)(2,1)S(1)}, bf16[96,2176]{1,0:T(8,128)(2,1)}, u32[]{:S(2)}) copy-start(bf16[96,2176]{1,0:T(8,128)(2,1)} %get-tuple-element.122) | copy-start | bytes 1253380
  136.0 9.7 %copy-start.3 = (bf16[896,2048]{1,0:T(8,128)(2,1)S(1)}, bf16[896,2048]{1,0:T(8,128)(2,1)}, u32[]{:S(2)}) copy-start(bf16[896,2048]{1,0:T(8,128)(2,1)} %get-tuple-element.138.refs_0_) | copy-start | bytes 11010052
  142.0 3.7 %collective-permute-start.29 = (bf16[1,96,2176]{2,1,0:T(8,128)(2,1)}, bf16[1,96,2176]{2,1,0:T(8,128)(2,1)S(1)}, u32[]{:S(2)}, u32[]{:S(2)}) collective-permute-start(bf16[1,96,2176]{2,1,0:T(8,128)(2,1)} %get-tuple-element.132), channel_id=1, source_target_pairs={{0,2},{2,0},{4,6},{6,4},{8,10},{10,8},{12,14},{14,12},{16,18},{18,... | collective-permute-start | bytes 1253384 | tf_op jit(solution)/shard_map/ppermute | solution.py:377
  143.2 12.3 %collective-permute-start.26 = (bf16[96,2176]{1,0:T(8,128)(2,1)S(1)}, bf16[96,2176]{1,0:T(8,128)(2,1)S(1)}, u32[]{:S(2)}, u32[]{:S(2)}) collective-permute-start(bf16[96,2176]{1,0:T(8,128)(2,1)S(1)} %add_convert_fusion.4.refs_1_), channel_id=1, source_target_pairs={{0,24},{2,26},{4,28},{6,30},{8,0},{10,2},{12,4},{14,6},{16,8},{18,... | collective-permute-start | bytes 1253384 | tf_op jit(solution)/shard_map/ppermute | solution.py:377
  145.7 1.0 copy-start.16
  145.7 2.3 %copy-start.10 = (bf16[896,768]{1,0:T(8,128)(2,1)S(1)}, bf16[896,768]{1,0:T(8,128)(2,1)}, u32[]{:S(2)}) copy-start(bf16[896,768]{1,0:T(8,128)(2,1)} %get-tuple-element.137) | copy-start | bytes 4128772
  146.8 13.9 %collective-permute-start.30 = (bf16[96,2176]{1,0:T(8,128)(2,1)S(1)}, bf16[96,2176]{1,0:T(8,128)(2,1)S(1)}, u32[]{:S(2)}, u32[]{:S(2)}) collective-permute-start(bf16[96,2176]{1,0:T(8,128)(2,1)S(1)} %fusion.5), channel_id=1, source_target_pairs={{0,4},{2,6},{4,0},{6,2},{8,12},{10,14},{12,8},{14,10},{16,20},{18,... | collective-permute-start | bytes 1253384 | tf_op jit(solution)/shard_map/ppermute | solution.py:377
  147.9 7.5 %copy-start.14 = (bf16[96,2176]{1,0:T(8,128)(2,1)S(1)}, bf16[96,2176]{1,0:T(8,128)(2,1)}, u32[]{:S(2)}) copy-start(bf16[96,2176]{1,0:T(8,128)(2,1)} %get-tuple-element.123) | copy-start | bytes 1253380
  147.9 12.9 %copy-start.2 = (bf16[896,2048]{1,0:T(8,128)(2,1)S(1)}, bf16[896,2048]{1,0:T(8,128)(2,1)}, u32[]{:S(2)}) copy-start(bf16[896,2048]{1,0:T(8,128)(2,1)} %get-tuple-element.134.refs_0_) | copy-start | bytes 11010052
  156.6 15.5 %collective-permute-start.27 = (bf16[96,2176]{1,0:T(8,128)(2,1)S(1)}, bf16[96,2176]{1,0:T(8,128)(2,1)S(1)}, u32[]{:S(2)}, u32[]{:S(2)}) collective-permute-start(bf16[96,2176]{1,0:T(8,128)(2,1)S(1)} %add_convert_fusion.3.refs_2_), channel_id=1, source_target_pairs={{0,24},{2,26},{4,28},{6,30},{8,0},{10,2},{12,4},{14,6},{16,8},{18,... | collective-permute-start | bytes 1253384 | tf_op jit(solution)/shard_map/ppermute | solution.py:377
  160.8 18.4 %collective-permute-start.31 = (bf16[96,2176]{1,0:T(8,128)(2,1)S(1)}, bf16[96,2176]{1,0:T(8,128)(2,1)S(1)}, u32[]{:S(2)}, u32[]{:S(2)}) collective-permute-start(bf16[96,2176]{1,0:T(8,128)(2,1)S(1)} %add_convert_fusion.refs_3_), channel_id=1, source_target_pairs={{0,8},{2,10},{4,12},{6,14},{8,16},{10,18},{12,20},{14,22},{16,24},... | collective-permute-start | bytes 1253384 | tf_op jit(solution)/shard_map/ppermute | solution.py:377
  160.9 1.3 copy-start.12
  162.2 4.9 %copy-start.11 = (bf16[896,768]{1,0:T(8,128)(2,1)S(1)}, bf16[896,768]{1,0:T(8,128)(2,1)}, u32[]{:S(2)}) copy-start(bf16[896,768]{1,0:T(8,128)(2,1)} %get-tuple-element.135) | copy-start | bytes 4128772
  167.2 12.0 %copy-start.13 = (bf16[96,2176]{1,0:T(8,128)(2,1)S(1)}, bf16[96,2176]{1,0:T(8,128)(2,1)}, u32[]{:S(2)}) copy-start(bf16[96,2176]{1,0:T(8,128)(2,1)} %get-tuple-element.133) | copy-start | bytes 1253380

commit v4 on v3

--- a/solution.py
+++ b/solution.py
@@ -94,7 +94,7 @@
         input_output_aliases={0: 0},
         compiler_params=pltpu.CompilerParams(vmem_limit_bytes=1024 * 1024),
         cost_estimate=COST,
-    )(x, *after)
+    )(x, *[in_hbm([a])[0] if a.dtype == F32 else a for a in after])
 
 
 def block_kernel(tokens, cotangent, ids, gates, out):
@@ -377,7 +377,6 @@
         return lax.ppermute(x, "expert", shift(**by))
 
     wg, wu, wd = gate_weight[0], up_weight[0], down_weight[0]
-    hit = expert_ids[:, :, None] == jnp.arange(LANES, dtype=jnp.int32)
     block = make_block(tokens, cotangent, expert_ids, gate_values)
 
     def swap(part):
@@ -492,11 +491,11 @@
     for k in range(planes // 2 + 1, planes):
         leaving.append(total(gather_plane(k) + down).astype(BF))
         down = [move(leaving[-1], dz=1)]
-    totals = total(gather_plane(0) + up + down)
-
-    input_grad = totals[:, :feat].astype(BF)
-    slots = totals[:, feat:]
-    gate_grad = jnp.sum(jnp.where(hit, slots[:, None, :], 0.0), axis=2).astype(BF)
+    home = gather_plane(0) + up + down
+    input_grad = total([v[:, :feat] for v in home]).astype(BF)
+    slots = total([v[:, feat:] for v in home])
+    hit = expert_ids.T[:, :, None] == jnp.arange(LANES, dtype=jnp.int32)
+    gate_grad = jnp.sum(jnp.where(hit, slots[None], 0.0), axis=2).astype(BF).T
     contract_rows = (((0,), (0,)), ((), ()))
     wgrad = lambda a, b: lax.dot_general(a, b, contract_rows, preferred_element_type=F32).astype(BF)[None]
     x_all, sd_all = x_slab

time: 182 us -> 175 us (0.962)
  local copies, waits for them, and re-layouts: 9.84 us -> 2.36 us
  waiting for transfers between devices: 52.7 us -> 55.1 us
    unnamed x40 -> x26, local copies, waits for them, and re-layouts: 9.04 us -> 2.36 us
    ppermute x5, waiting for transfers between devices: 9.26 us -> 11.5 us  [swap(): return [part, lax.ppermute(part, 'seq', [(0, 1), (1, 0)])]]
    convert_element_type x2, other arithmetic: 2.26 us -> 0.27 us  [local(): leaving.append(total(gather_plane(k) + up).astype(BF))]
  transfers between devices with their start and end apart: 32 -> 32, of which waited for: 16 -> 17; matrix products, arithmetic and copies ran while one was open for 11% -> 9% of each run, Pallas kernels for 32% -> 33%
where the time goes in v4:
time: 175 us
  Pallas kernels  66.6 us (38%)
  waiting for transfers between devices  55.1 us (31%)
  starting transfers between devices  31.2 us (18%)
  matrix products  14.7 us (8%)
  other arithmetic  3.71 us (2%)
  local copies, waits for them, and re-layouts  2.36 us (1%)
    ppermute x27, waiting for transfers between devices, move(): return lax.ppermute(x, 'expert', shift(**by))  43.6 us
    pallas_call x5, Pallas kernels, forward_call(): pl.pallas_call(functools.partial(forward_kernel, cfg), grid=(hid // tile,...  33.1 us
    pallas_call x5, Pallas kernels, backward_call(): pl.pallas_call(functools.partial(backward_kernel, inner, tok, feat, hid,...  32.3 us
    ppermute x27, starting transfers between devices, move(): return lax.ppermute(x, 'expert', shift(**by))  23.5 us
    dot_general x3, matrix products, local(): lax.dot_general(a, b, contract_rows, preferred_element_type=F32).astype(BF)  14.7 us
    ppermute x5, waiting for transfers between devices, swap(): return [part, lax.ppermute(part, 'seq', [(0, 1), (1, 0)])]  11.5 us
    ppermute x5, starting transfers between devices, swap(): return [part, lax.ppermute(part, 'seq', [(0, 1), (1, 0)])]  7.71 us
  transfers between devices with their start and end apart: 32, of which 17 were waited for; matrix products, arithmetic and copies ran while one was open for 9% of the time, Pallas kernels for 33%

profile of v4, /device:TPU:0, one launch (start us, length us, event | category | flops | bytes accessed | tf_op | source)
XLA Modules:
  0.0 174.6 jit_solution(16262955670844176509)
XLA Ops:
  0.6 1.3 shard_map.110.refs_0_
  1.9 0.5 collective-permute-start.1
  2.4 2.6 %collective-permute-start = (bf16[96,4224]{1,0:T(8,128)(2,1)S(1)}, bf16[96,4224]{1,0:T(8,128)(2,1)S(1)}, u32[]{:S(2)}, u32[]{:S(2)}) collective-permute-start(bf16[96,4224]{1,0:T(8,128)(2,1)S(1)} %shard_map.110.refs_0_), channel_id=1, source_target_pairs={{0,8},{2,10},{4,12},{6,14},{8,16},{10,18},{12,20},{14,22},{16,24},... | collective-permute-start | bytes 2433032 | tf_op jit(solution)/shard_map/ppermute | solution.py:377
  5.1 1.5 collective-permute-start.4
  6.6 7.4 %shard_map.111 = (bf16[108,2304]{1,0:T(8,128)(2,1)}, bf16[896,2048]{1,0:T(8,128)(2,1)}, bf16[896,2048]{1,0:T(8,128)(2,1)}, bf16[192,112]{1,0:T(8,128)(2,1)}, bf1...) custom-call(bf16[96,4224]{1,0:T(8,128)(2,1)S(1)} %shard_map.110.refs, ...), custom_call_target="tpu_custom_call" | custom-call | flops 1000 | bytes 1000 | tf_op jit(solution)/shard_map/pallas_call | solution.py:249
  14.0 1.6 collective-permute-start.2
  15.6 10.2 %collective-permute-done.refs_0_ = bf16[96,4224]{1,0:T(8,128)(2,1)S(1)} collective-permute-done((bf16[96,4224]{1,0:T(8,128)(2,1)S(1)}, bf16[96,4224]{1,0:T(8,128)(2,1)S(1)}, u32[]{:S(2)}, u32[]{:S(2)}) %collective-permute-start) | collective-permute-done | bytes 811040 | tf_op jit(solution)/shard_map/ppermute | solution.py:377
  25.8 2.1 %collective-permute-done.2.refs_1_ = bf16[108,2304]{1,0:T(8,128)(2,1)S(1)} collective-permute-done((bf16[108,2304]{1,0:T(8,128)(2,1)}, bf16[108,2304]{1,0:T(8,128)(2,1)S(1)}, u32[]{:S(2)}, u32[]{:S(2)}) %collective-permute-start.2) | collective-permute-done | bytes 497696 | tf_op jit(solution)/shard_map/ppermute | solution.py:384
  27.9 0.5 collective-permute-start.5
  28.4 0.9 collective-permute-start.9
  29.3 1.6 collective-permute-start.3
  30.9 5.7 %shard_map.114 = (bf16[1,96,2176]{2,1,0:T(8,128)(2,1)}, bf16[1,96,2176]{2,1,0:T(8,128)(2,1)}, bf16[896,768]{1,0:T(8,128)(2,1)}, bf16[896,768]{1,0:T(8,128)(2,1)}...) custom-call(bf16[108,2304]{1,0:T(8,128)(2,1)} %get-tuple-element.72.refs_0_, ...), custom_call_target="tpu_custom_call" | custom-call | flops 1000 | bytes 1000 | tf_op jit(solution)/shard_map/pallas_call | solution.py:340
  36.6 5.7 %shard_map.115 = (bf16[216,2304]{1,0:T(8,128)(2,1)}, bf16[896,2048]{1,0:T(8,128)(2,1)}, bf16[896,2048]{1,0:T(8,128)(2,1)}, bf16[384,224]{1,0:T(8,128)(2,1)}, bf16[224,128]{1,0:T(8,128)(2,1)}, /*index=5*/f32[8,128]{1,0:T(8,128)}) custom-call(bf16[96,4224]{1,0:T(8,128)(2,1)S(1)} %shard_map.113.refs_0_, ...), custom_call_target="tpu_custom_call", output_to_operand_aliasing={{1}: (8, {}), {2}: (9, {})} | custom-call | flops 1000 | bytes 1000 | tf_op jit(solution)/shard_map/pallas_call | solution.py:249
  42.3 1.5 collective-permute-start.8
  43.8 4.6 %collective-permute-done.9.refs_0_ = bf16[96,4224]{1,0:T(8,128)(2,1)S(1)} collective-permute-done((bf16[96,4224]{1,0:T(8,128)(2,1)S(1)}, bf16[96,4224]{1,0:T(8,128)(2,1)S(1)}, u32[]{:S(2)}, u32[]{:S(2)}) %collective-permute-start.9) | collective-permute-done | bytes 811040 | tf_op jit(solution)/shard_map/ppermute | solution.py:377
  48.4 2.5 %collective-permute-done.3.refs_0_ = bf16[96,4224]{1,0:T(8,128)(2,1)S(1)} collective-permute-done((bf16[96,4224]{1,0:T(8,128)(2,1)S(1)}, bf16[96,4224]{1,0:T(8,128)(2,1)S(1)}, u32[]{:S(2)}, u32[]{:S(2)}) %collective-permute-start.3) | collective-permute-done | bytes 811040 | tf_op jit(solution)/shard_map/ppermute | solution.py:377
  50.9 1.7 collective-permute-start.14
  52.7 0.8 collective-permute-start.7
  53.5 6.7 %shard_map.118 = (bf16[216,2304]{1,0:T(8,128)(2,1)}, bf16[896,2048]{1,0:T(8,128)(2,1)}, bf16[896,2048]{1,0:T(8,128)(2,1)}, bf16[384,224]{1,0:T(8,128)(2,1)}, bf1...) custom-call(bf16[96,4224]{1,0:T(8,128)(2,1)S(1)} %shard_map.117.refs, ...), custom_call_target="tpu_custom_call", output_to_operand_aliasing={{1}: (8, {}), {2}: (9, {})} | custom-call | flops 1000 | bytes 1000 | tf_op jit(solution)/shard_map/pallas_call | solution.py:249
  60.2 1.6 collective-permute-start.19
  61.7 5.6 %collective-permute-done.8.refs_1_ = bf16[216,2304]{1,0:T(8,128)(2,1)S(1)} collective-permute-done((bf16[216,2304]{1,0:T(8,128)(2,1)}, bf16[216,2304]{1,0:T(8,128)(2,1)S(1)}, u32[]{:S(2)}, u32[]{:S(2)}) %collective-permute-start.8) | collective-permute-done | bytes 995360 | tf_op jit(solution)/shard_map/ppermute | solution.py:384
  67.3 6.9 %shard_map.119 = (bf16[2,96,2176]{2,1,0:T(8,128)(2,1)}, bf16[2,96,2176]{2,1,0:T(8,128)(2,1)}, bf16[896,768]{1,0:T(8,128)(2,1)}, bf16[896,768]{1,0:T(8,128)(2,1)}...) custom-call(bf16[216,2304]{1,0:T(8,128)(2,1)} %get-tuple-element.83.refs_, ...), custom_call_target="tpu_custom_call", output_to_operand_aliasing={{2}: (7, {}), {3}: (8, {}), {4}: (9, {})} | custom-call | flops 1000 | bytes 1000 | tf_op jit(solution)/shard_map/pallas_call | solution.py:340
  74.2 0.5 collective-permute-start.15
  74.7 0.1 collective-permute-start.13
  74.8 1.1 collective-permute-start.18
  75.9 1.8 %collective-permute-done.15.refs_3_ = bf16[96,4224]{1,0:T(8,128)(2,1)S(1)} collective-permute-done((bf16[96,4224]{1,0:T(8,128)(2,1)S(1)}, bf16[96,4224]{1,0:T(8,128)(2,1)S(1)}, u32[]{:S(2)}, u32[]{:S(2)}) %collective-permute-start.15) | collective-permute-done | bytes 811040 | tf_op jit(solution)/shard_map/ppermute | solution.py:377
  77.7 1.2 collective-permute-done.13.refs_1_
  78.9 7.5 %shard_map.122 = (bf16[216,2304]{1,0:T(8,128)(2,1)}, bf16[896,2048]{1,0:T(8,128)(2,1)}, bf16[896,2048]{1,0:T(8,128)(2,1)}, bf16[384,224]{1,0:T(8,128)(2,1)}, bf1...) custom-call(bf16[96,4224]{1,0:T(8,128)(2,1)S(1)} %shard_map.120.refs, ...), custom_call_target="tpu_custom_call", output_to_operand_aliasing={{1}: (8, {}), {2}: (9, {})} | custom-call | flops 1000 | bytes 1000 | tf_op jit(solution)/shard_map/pallas_call | solution.py:249
  86.4 1.6 collective-permute-start.23
  87.9 0.3 collective-permute-done.19.refs_1_
  88.2 6.9 %shard_map.123 = (bf16[2,96,2176]{2,1,0:T(8,128)(2,1)}, bf16[2,96,2176]{2,1,0:T(8,128)(2,1)}, bf16[896,768]{1,0:T(8,128)(2,1)}, bf16[896,768]{1,0:T(8,128)(2,1)}...) custom-call(bf16[216,2304]{1,0:T(8,128)(2,1)} %get-tuple-element.100.refs, ...), custom_call_target="tpu_custom_call", output_to_operand_aliasing={{2}: (7, {}), {3}: (8, {}), {4}: (9, {})} | custom-call | flops 1000 | bytes 1000 | tf_op jit(solution)/shard_map/pallas_call | solution.py:340
  95.2 0.1 collective-permute-done.18.refs_0_
  95.2 0.5 collective-permute-start.20
  95.7 1.1 collective-permute-start.17
  96.8 1.9 %collective-permute-done.20.refs_1_ = bf16[96,4224]{1,0:T(8,128)(2,1)S(1)} collective-permute-done((bf16[96,4224]{1,0:T(8,128)(2,1)S(1)}, bf16[96,4224]{1,0:T(8,128)(2,1)S(1)}, u32[]{:S(2)}, u32[]{:S(2)}) %collective-permute-start.20) | collective-permute-done | bytes 811040 | tf_op jit(solution)/shard_map/ppermute | solution.py:377
  98.7 5.7 %shard_map.125 = (bf16[108,2304]{1,0:T(8,128)(2,1)}, bf16[896,2048]{1,0:T(8,128)(2,1)}, bf16[896,2048]{1,0:T(8,128)(2,1)}, bf16[192,112]{1,0:T(8,128)(2,1)}, bf1...) custom-call(bf16[96,4224]{1,0:T(8,128)(2,1)S(1)} %shard_map.124.refs, ...), custom_call_target="tpu_custom_call", output_to_operand_aliasing={{1}: (6, {}), {2}: (7, {})} | custom-call | flops 1000 | bytes 1000 | tf_op jit(solution)/shard_map/pallas_call | solution.py:249
  104.4 2.9 %collective-permute-done.17.refs_7_.refs_9_ = bf16[96,2176]{1,0:T(8,128)(2,1)S(1)} collective-permute-done((bf16[96,2176]{1,0:T(8,128)(2,1)S(1)}, bf16[96,2176]{1,0:T(8,128)(2,1)S(1)}, u32[]{:S(2)}, u32[]{:S(2)}) %collective-permute-start.17) | collective-permute-done | bytes 417824 | tf_op jit(solution)/shard_map/ppermute | solution.py:377
  107.3 3.4 %collective-permute-done.23.refs_1_ = bf16[216,2304]{1,0:T(8,128)(2,1)S(1)} collective-permute-done((bf16[216,2304]{1,0:T(8,128)(2,1)}, bf16[216,2304]{1,0:T(8,128)(2,1)S(1)}, u32[]{:S(2)}, u32[]{:S(2)}) %collective-permute-start.23) | collective-permute-done | bytes 995360 | tf_op jit(solution)/shard_map/ppermute | solution.py:384
  110.7 7.0 %shard_map.126 = (bf16[2,96,2176]{2,1,0:T(8,128)(2,1)}, bf16[2,96,2176]{2,1,0:T(8,128)(2,1)}, bf16[896,768]{1,0:T(8,128)(2,1)}, bf16[896,768]{1,0:T(8,128)(2,1)}...) custom-call(bf16[216,2304]{1,0:T(8,128)(2,1)} %get-tuple-element.113.ref, ...), custom_call_target="tpu_custom_call", output_to_operand_aliasing={{2}: (8, {}), {3}: (9, {}), {4}: (10, {})} | custom-call | flops 1000 | bytes 1000 | tf_op jit(solution)/shard_map/pallas_call | solution.py:340
  117.7 1.6 collective-permute-start.28
  119.3 1.1 collective-permute-start.22
  120.4 1.3 fusion.3
  121.7 1.1 collective-permute-start.25
  122.7 9.0 %collective-permute-done.22.refs_10_ = bf16[96,2176]{1,0:T(8,128)(2,1)S(1)} collective-permute-done((bf16[96,2176]{1,0:T(8,128)(2,1)S(1)}, bf16[96,2176]{1,0:T(8,128)(2,1)S(1)}, u32[]{:S(2)}, u32[]{:S(2)}) %collective-permute-start.22) | collective-permute-done | bytes 417824 | tf_op jit(solution)/shard_map/ppermute | solution.py:377
  131.8 0.1 collective-permute-done.28.refs_1_
  131.9 5.9 %shard_map.127 = (bf16[1,96,2176]{2,1,0:T(8,128)(2,1)}, bf16[1,96,2176]{2,1,0:T(8,128)(2,1)}, bf16[896,768]{1,0:T(8,128)(2,1)}, bf16[896,768]{1,0:T(8,128)(2,1)}...) custom-call(bf16[108,2304]{1,0:T(8,128)(2,1)} %get-tuple-element.124.r, ...), custom_call_target="tpu_custom_call", output_to_operand_aliasing={{2}: (11, {}), {3}: (12, {}), {4}: (13, {})} | custom-call | flops 1000 | bytes 1000 | tf_op jit(solution)/shard_map/pallas_call | solution.py:340
  137.7 2.2 %collective-permute-done.25 = bf16[96,2176]{1,0:T(8,128)(2,1)S(1)} collective-permute-done((bf16[96,2176]{1,0:T(8,128)(2,1)S(1)}, bf16[96,2176]{1,0:T(8,128)(2,1)S(1)}, u32[]{:S(2)}, u32[]{:S(2)}) %collective-permute-start.25) | collective-permute-done | bytes 417824 | tf_op jit(solution)/shard_map/ppermute | solution.py:377
  139.9 0.1 add_convert_fusion.4.refs_1_
  140.0 2.5 %collective-permute-start.26 = (bf16[96,2176]{1,0:T(8,128)(2,1)S(1)}, bf16[96,2176]{1,0:T(8,128)(2,1)S(1)}, u32[]{:S(2)}, u32[]{:S(2)}) collective-permute-start(bf16[96,2176]{1,0:T(8,128)(2,1)S(1)} %add_convert_fusion.4.refs_1_), channel_id=1, source_target_pairs={{0,24},{2,26},{4,28},{6,30},{8,0},{10,2},{12,4},{14,6},{16,8},{18,... | collective-permute-start | bytes 1253384 | tf_op jit(solution)/shard_map/ppermute | solution.py:377
  142.6 1.0 copy-done.8
  143.6 0.1 fusion.5
  143.7 1.2 collective-permute-start.30
  144.8 4.9 %fusion.2 = bf16[1,768,2048]{2,1,0:T(8,128)(2,1)} fusion(bf16[896,768]{1,0:T(8,128)(2,1)S(1)} %copy-done.2, bf16[896,2048]{1,0:T(8,128)(2,1)S(1)} %shard_map.129), kind=kOutput, calls=%fused_computation.5 | convolution fusion | flops 2820145152 | bytes 8192000 | tf_op jit(solution)/shard_map/dot_general | solution.py:500
  149.7 1.5 collective-permute-done.26
  151.2 0.2 add_convert_fusion.3.refs_2_
  151.4 4.1 %collective-permute-start.27 = (bf16[96,2176]{1,0:T(8,128)(2,1)S(1)}, bf16[96,2176]{1,0:T(8,128)(2,1)S(1)}, u32[]{:S(2)}, u32[]{:S(2)}) collective-permute-start(bf16[96,2176]{1,0:T(8,128)(2,1)S(1)} %add_convert_fusion.3.refs_2_), channel_id=1, source_target_pairs={{0,24},{2,26},{4,28},{6,30},{8,0},{10,2},{12,4},{14,6},{16,8},{18,... | collective-permute-start | bytes 1253384 | tf_op jit(solution)/shard_map/ppermute | solution.py:377
  155.5 0.1 add_convert_fusion.refs_3_
  155.6 0.1 collective-permute-start.31
  155.7 1.3 copy-done.4
  157.0 4.9 %fusion.1 = bf16[1,2048,768]{2,1,0:T(8,128)(2,1)} fusion(bf16[896,2048]{1,0:T(8,128)(2,1)S(1)} %shard_map.128, bf16[896,768]{1,0:T(8,128)(2,1)S(1)} %copy-done.4), kind=kOutput, calls=%fused_computation.4 | convolution fusion | flops 2820145152 | bytes 8192000 | tf_op jit(solution)/shard_map/dot_general | solution.py:500
  161.9 5.0 %fusion = bf16[1,2048,768]{2,1,0:T(8,128)(2,1)} fusion(bf16[896,2048]{1,0:T(8,128)(2,1)S(1)} %shard_map.128, bf16[896,768]{1,0:T(8,128)(2,1)S(1)} %copy-done.3), kind=kOutput, calls=%fused_computation.3 | convolution fusion | flops 2820145152 | bytes 8192000 | tf_op jit(solution)/shard_map/dot_general | solution.py:500
  166.9 5.7 %collective-permute-done.31 = bf16[96,2176]{1,0:T(8,128)(2,1)S(1)} collective-permute-done((bf16[96,2176]{1,0:T(8,128)(2,1)S(1)}, bf16[96,2176]{1,0:T(8,128)(2,1)S(1)}, u32[]{:S(2)}, u32[]{:S(2)}) %collective-permute-start.31) | collective-permute-done | bytes 417824 | tf_op jit(solution)/shard_map/ppermute | solution.py:377
  172.7 0.9 select_reduce_fusion
  173.6 1.0 add_convert_fusion.6
  (57 shorter events, 0.1 us)
Async XLA Ops:
  1.9 4.7 %collective-permute-start.1 = (bf16[96,4224]{1,0:T(8,128)(2,1)S(1)}, bf16[96,4224]{1,0:T(8,128)(2,1)S(1)}, u32[]{:S(2)}, u32[]{:S(2)}) collective-permute-start(bf16[96,4224]{1,0:T(8,128)(2,1)S(1)} %shard_map.110.refs_0_), channel_id=1, source_target_pairs={{0,2},{2,0},{4,6},{6,4},{8,10},{10,8},{12,14},{14,12},{16,18},{18,... | collective-permute-start | bytes 2433032 | tf_op jit(solution)/shard_map/ppermute | solution.py:377
  2.4 23.3 %collective-permute-start = (bf16[96,4224]{1,0:T(8,128)(2,1)S(1)}, bf16[96,4224]{1,0:T(8,128)(2,1)S(1)}, u32[]{:S(2)}, u32[]{:S(2)}) collective-permute-start(bf16[96,4224]{1,0:T(8,128)(2,1)S(1)} %shard_map.110.refs_0_), channel_id=1, source_target_pairs={{0,8},{2,10},{4,12},{6,14},{8,16},{10,18},{12,20},{14,22},{16,24},... | collective-permute-start | bytes 2433032 | tf_op jit(solution)/shard_map/ppermute | solution.py:377
  5.1 22.8 %collective-permute-start.4 = (bf16[96,4224]{1,0:T(8,128)(2,1)S(1)}, bf16[96,4224]{1,0:T(8,128)(2,1)S(1)}, u32[]{:S(2)}, u32[]{:S(2)}) collective-permute-start(bf16[96,4224]{1,0:T(8,128)(2,1)S(1)} %shard_map.110.refs_0_), channel_id=1, source_target_pairs={{0,4},{2,6},{4,0},{6,2},{8,12},{10,14},{12,8},{14,10},{16,20},{18,... | collective-permute-start | bytes 2433032 | tf_op jit(solution)/shard_map/ppermute | solution.py:377
  14.0 13.8 %collective-permute-start.2 = (bf16[108,2304]{1,0:T(8,128)(2,1)}, bf16[108,2304]{1,0:T(8,128)(2,1)S(1)}, u32[]{:S(2)}, u32[]{:S(2)}) collective-permute-start(bf16[108,2304]{1,0:T(8,128)(2,1)} %get-tuple-element.72.refs_0_), channel_id=1, source_target_pairs={{0,1},{1,0},{2,3},{3,2},{4,5},{5,4},{6,7},{7,6},{8,9},{9,8},{10,11... | collective-permute-start | bytes 1493000 | tf_op jit(solution)/shard_map/ppermute | solution.py:384
  27.8 8.7 %collective-permute-start.6 = (bf16[96,4224]{1,0:T(8,128)(2,1)S(1)}, bf16[96,4224]{1,0:T(8,128)(2,1)S(1)}, u32[]{:S(2)}, u32[]{:S(2)}) collective-permute-start(bf16[96,4224]{1,0:T(8,128)(2,1)S(1)} %shard_map.112.refs_2_), channel_id=1, source_target_pairs={{0,2},{2,0},{4,6},{6,4},{8,10},{10,8},{12,14},{14,12},{16,18},{18,... | collective-permute-start | bytes 2433032 | tf_op jit(solution)/shard_map/ppermute | solution.py:377
  27.9 8.7 %collective-permute-start.5 = (bf16[96,4224]{1,0:T(8,128)(2,1)S(1)}, bf16[96,4224]{1,0:T(8,128)(2,1)S(1)}, u32[]{:S(2)}, u32[]{:S(2)}) collective-permute-start(bf16[96,4224]{1,0:T(8,128)(2,1)S(1)} %shard_map.113.refs_0_), channel_id=1, source_target_pairs={{0,2},{2,0},{4,6},{6,4},{8,10},{10,8},{12,14},{14,12},{16,18},{18,... | collective-permute-start | bytes 2433032 | tf_op jit(solution)/shard_map/ppermute | solution.py:377
  28.4 20.0 %collective-permute-start.9 = (bf16[96,4224]{1,0:T(8,128)(2,1)S(1)}, bf16[96,4224]{1,0:T(8,128)(2,1)S(1)}, u32[]{:S(2)}, u32[]{:S(2)}) collective-permute-start(bf16[96,4224]{1,0:T(8,128)(2,1)S(1)} %shard_map.112.refs_2_), channel_id=1, source_target_pairs={{0,4},{2,6},{4,0},{6,2},{8,12},{10,14},{12,8},{14,10},{16,20},{18,... | collective-permute-start | bytes 2433032 | tf_op jit(solution)/shard_map/ppermute | solution.py:377
  29.3 21.6 %collective-permute-start.3 = (bf16[96,4224]{1,0:T(8,128)(2,1)S(1)}, bf16[96,4224]{1,0:T(8,128)(2,1)S(1)}, u32[]{:S(2)}, u32[]{:S(2)}) collective-permute-start(bf16[96,4224]{1,0:T(8,128)(2,1)S(1)} %shard_map.112.refs_2_), channel_id=1, source_target_pairs={{0,8},{2,10},{4,12},{6,14},{8,16},{10,18},{12,20},{14,22},{16,24},... | collective-permute-start | bytes 2433032 | tf_op jit(solution)/shard_map/ppermute | solution.py:377
  36.6 16.1 %collective-permute-start.12 = (bf16[1,96,2176]{2,1,0:T(8,128)(2,1)}, bf16[1,96,2176]{2,1,0:T(8,128)(2,1)S(1)}, u32[]{:S(2)}, u32[]{:S(2)}) collective-permute-start(bf16[1,96,2176]{2,1,0:T(8,128)(2,1)} %get-tuple-element.89), channel_id=1, source_target_pairs={{0,2},{2,0},{4,6},{6,4},{8,10},{10,8},{12,14},{14,12},{16,18},{18,... | collective-permute-start | bytes 1253384 | tf_op jit(solution)/shard_map/ppermute | solution.py:377
  42.3 25.0 %collective-permute-start.8 = (bf16[216,2304]{1,0:T(8,128)(2,1)}, bf16[216,2304]{1,0:T(8,128)(2,1)S(1)}, u32[]{:S(2)}, u32[]{:S(2)}) collective-permute-start(bf16[216,2304]{1,0:T(8,128)(2,1)} %get-tuple-element.83.refs_0_), channel_id=1, source_target_pairs={{0,1},{1,0},{2,3},{3,2},{4,5},{5,4},{6,7},{7,6},{8,9},{9,8},{10,11... | collective-permute-start | bytes 2985992 | tf_op jit(solution)/shard_map/ppermute | solution.py:384
  48.4 5.1 %collective-permute-start.10 = (bf16[96,4224]{1,0:T(8,128)(2,1)S(1)}, bf16[96,4224]{1,0:T(8,128)(2,1)S(1)}, u32[]{:S(2)}, u32[]{:S(2)}) collective-permute-start(bf16[96,4224]{1,0:T(8,128)(2,1)S(1)} %shard_map.117.refs_0_), channel_id=1, source_target_pairs={{0,2},{2,0},{4,6},{6,4},{8,10},{10,8},{12,14},{14,12},{16,18},{18,... | collective-permute-start | bytes 2433032 | tf_op jit(solution)/shard_map/ppermute | solution.py:377
  50.9 2.5 %collective-permute-start.11 = (bf16[96,4224]{1,0:T(8,128)(2,1)S(1)}, bf16[96,4224]{1,0:T(8,128)(2,1)S(1)}, u32[]{:S(2)}, u32[]{:S(2)}) collective-permute-start(bf16[96,4224]{1,0:T(8,128)(2,1)S(1)} %shard_map.116.refs_2_), channel_id=1, source_target_pairs={{0,2},{2,0},{4,6},{6,4},{8,10},{10,8},{12,14},{14,12},{16,18},{18,... | collective-permute-start | bytes 2433032 | tf_op jit(solution)/shard_map/ppermute | solution.py:377
  50.9 23.3 %collective-permute-start.14 = (bf16[96,4224]{1,0:T(8,128)(2,1)S(1)}, bf16[96,4224]{1,0:T(8,128)(2,1)S(1)}, u32[]{:S(2)}, u32[]{:S(2)}) collective-permute-start(bf16[96,4224]{1,0:T(8,128)(2,1)S(1)} %shard_map.110.refs_0_), channel_id=1, source_target_pairs={{0,24},{2,26},{4,28},{6,30},{8,0},{10,2},{12,4},{14,6},{16,8},{18,... | collective-permute-start | bytes 2433032 | tf_op jit(solution)/shard_map/ppermute | solution.py:377
  52.7 22.1 %collective-permute-start.7 = (bf16[96,4224]{1,0:T(8,128)(2,1)S(1)}, bf16[96,4224]{1,0:T(8,128)(2,1)S(1)}, u32[]{:S(2)}, u32[]{:S(2)}) collective-permute-start(bf16[96,4224]{1,0:T(8,128)(2,1)S(1)} %shard_map.116.refs_2_), channel_id=1, source_target_pairs={{0,4},{2,6},{4,0},{6,2},{8,12},{10,14},{12,8},{14,10},{16,20},{18,... | collective-permute-start | bytes 2433032 | tf_op jit(solution)/shard_map/ppermute | solution.py:377
  60.2 28.1 %collective-permute-start.19 = (bf16[216,2304]{1,0:T(8,128)(2,1)}, bf16[216,2304]{1,0:T(8,128)(2,1)S(1)}, u32[]{:S(2)}, u32[]{:S(2)}) collective-permute-start(bf16[216,2304]{1,0:T(8,128)(2,1)} %get-tuple-element.100.refs_0_), channel_id=1, source_target_pairs={{0,1},{1,0},{2,3},{3,2},{4,5},{5,4},{6,7},{7,6},{8,9},{9,8},{10,11... | collective-permute-start | bytes 2985992 | tf_op jit(solution)/shard_map/ppermute | solution.py:384
  74.2 4.7 %collective-permute-start.16 = (bf16[2,96,2176]{2,1,0:T(8,128)(2,1)}, bf16[2,96,2176]{2,1,0:T(8,128)(2,1)S(1)}, u32[]{:S(2)}, u32[]{:S(2)}) collective-permute-start(bf16[2,96,2176]{2,1,0:T(8,128)(2,1)} %get-tuple-element.98), channel_id=1, source_target_pairs={{0,2},{2,0},{4,6},{6,4},{8,10},{10,8},{12,14},{14,12},{16,18},{18,... | collective-permute-start | bytes 2506760 | tf_op jit(solution)/shard_map/ppermute | solution.py:377
  74.2 3.5 %collective-permute-start.15 = (bf16[96,4224]{1,0:T(8,128)(2,1)S(1)}, bf16[96,4224]{1,0:T(8,128)(2,1)S(1)}, u32[]{:S(2)}, u32[]{:S(2)}) collective-permute-start(bf16[96,4224]{1,0:T(8,128)(2,1)S(1)} %shard_map.121.refs_2_), channel_id=1, source_target_pairs={{0,2},{2,0},{4,6},{6,4},{8,10},{10,8},{12,14},{14,12},{16,18},{18,... | collective-permute-start | bytes 2433032 | tf_op jit(solution)/shard_map/ppermute | solution.py:377
  74.7 4.2 %collective-permute-start.13 = (bf16[96,4224]{1,0:T(8,128)(2,1)S(1)}, bf16[96,4224]{1,0:T(8,128)(2,1)S(1)}, u32[]{:S(2)}, u32[]{:S(2)}) collective-permute-start(bf16[96,4224]{1,0:T(8,128)(2,1)S(1)} %shard_map.120.refs_0_), channel_id=1, source_target_pairs={{0,2},{2,0},{4,6},{6,4},{8,10},{10,8},{12,14},{14,12},{16,18},{18,... | collective-permute-start | bytes 2433032 | tf_op jit(solution)/shard_map/ppermute | solution.py:377
  74.8 20.4 %collective-permute-start.18 = (bf16[96,4224]{1,0:T(8,128)(2,1)S(1)}, bf16[96,4224]{1,0:T(8,128)(2,1)S(1)}, u32[]{:S(2)}, u32[]{:S(2)}) collective-permute-start(bf16[96,4224]{1,0:T(8,128)(2,1)S(1)} %shard_map.121.refs_2_), channel_id=1, source_target_pairs={{0,4},{2,6},{4,0},{6,2},{8,12},{10,14},{12,8},{14,10},{16,20},{18,... | collective-permute-start | bytes 2433032 | tf_op jit(solution)/shard_map/ppermute | solution.py:377
  86.4 24.3 %collective-permute-start.23 = (bf16[216,2304]{1,0:T(8,128)(2,1)}, bf16[216,2304]{1,0:T(8,128)(2,1)S(1)}, u32[]{:S(2)}, u32[]{:S(2)}) collective-permute-start(bf16[216,2304]{1,0:T(8,128)(2,1)} %get-tuple-element.113.refs_0_), channel_id=1, source_target_pairs={{0,1},{1,0},{2,3},{3,2},{4,5},{5,4},{6,7},{7,6},{8,9},{9,8},{10,11... | collective-permute-start | bytes 2985992 | tf_op jit(solution)/shard_map/ppermute | solution.py:384
  88.2 7.4 %copy-start.11 = (bf16[96,2176]{1,0:T(8,128)(2,1)S(1)}, bf16[96,2176]{1,0:T(8,128)(2,1)}, u32[]{:S(2)}) copy-start(bf16[96,2176]{1,0:T(8,128)(2,1)} %get-tuple-element.99) | copy-start | bytes 1253380
  95.2 3.5 %collective-permute-start.21 = (bf16[2,96,2176]{2,1,0:T(8,128)(2,1)}, bf16[2,96,2176]{2,1,0:T(8,128)(2,1)S(1)}, u32[]{:S(2)}, u32[]{:S(2)}) collective-permute-start(bf16[2,96,2176]{2,1,0:T(8,128)(2,1)} %get-tuple-element.111), channel_id=1, source_target_pairs={{0,2},{2,0},{4,6},{6,4},{8,10},{10,8},{12,14},{14,12},{16,18},{18,... | collective-permute-start | bytes 2506760 | tf_op jit(solution)/shard_map/ppermute | solution.py:377
  95.2 3.5 %collective-permute-start.20 = (bf16[96,4224]{1,0:T(8,128)(2,1)S(1)}, bf16[96,4224]{1,0:T(8,128)(2,1)S(1)}, u32[]{:S(2)}, u32[]{:S(2)}) collective-permute-start(bf16[96,4224]{1,0:T(8,128)(2,1)S(1)} %shard_map.124.refs_0_), channel_id=1, source_target_pairs={{0,2},{2,0},{4,6},{6,4},{8,10},{10,8},{12,14},{14,12},{16,18},{18,... | collective-permute-start | bytes 2433032 | tf_op jit(solution)/shard_map/ppermute | solution.py:377
  95.7 11.6 %collective-permute-start.17 = (bf16[96,2176]{1,0:T(8,128)(2,1)S(1)}, bf16[96,2176]{1,0:T(8,128)(2,1)S(1)}, u32[]{:S(2)}, u32[]{:S(2)}) collective-permute-start(bf16[96,2176]{1,0:T(8,128)(2,1)S(1)} %copy-done.11), channel_id=1, source_target_pairs={{0,4},{2,6},{4,0},{6,2},{8,12},{10,14},{12,8},{14,10},{16,20},{18,... | collective-permute-start | bytes 1253384 | tf_op jit(solution)/shard_map/ppermute | solution.py:377
  110.7 7.0 %copy-start.5 = (bf16[108,2304]{1,0:T(8,128)(2,1)S(1)}, bf16[108,2304]{1,0:T(8,128)(2,1)}, u32[]{:S(2)}) copy-start(bf16[108,2304]{1,0:T(8,128)(2,1)} %get-tuple-element.124.refs_0_) | copy-start | bytes 1492996
  110.7 8.5 %copy-start.12 = (bf16[96,2176]{1,0:T(8,128)(2,1)S(1)}, bf16[96,2176]{1,0:T(8,128)(2,1)}, u32[]{:S(2)}) copy-start(bf16[96,2176]{1,0:T(8,128)(2,1)} %get-tuple-element.112) | copy-start | bytes 1253380
  117.7 2.7 %collective-permute-start.24 = (bf16[2,96,2176]{2,1,0:T(8,128)(2,1)}, bf16[2,96,2176]{2,1,0:T(8,128)(2,1)S(1)}, u32[]{:S(2)}, u32[]{:S(2)}) collective-permute-start(bf16[2,96,2176]{2,1,0:T(8,128)(2,1)} %get-tuple-element.121), channel_id=1, source_target_pairs={{0,2},{2,0},{4,6},{6,4},{8,10},{10,8},{12,14},{14,12},{16,18},{18,... | collective-permute-start | bytes 2506760 | tf_op jit(solution)/shard_map/ppermute | solution.py:377
  117.7 14.2 %collective-permute-start.28 = (bf16[108,2304]{1,0:T(8,128)(2,1)S(1)}, bf16[108,2304]{1,0:T(8,128)(2,1)S(1)}, u32[]{:S(2)}, u32[]{:S(2)}) collective-permute-start(bf16[108,2304]{1,0:T(8,128)(2,1)S(1)} %copy-done.5), channel_id=1, source_target_pairs={{0,1},{1,0},{2,3},{3,2},{4,5},{5,4},{6,7},{7,6},{8,9},{9,8},{10,11... | collective-permute-start | bytes 1493000 | tf_op jit(solution)/shard_map/ppermute | solution.py:384
  119.3 12.5 %collective-permute-start.22 = (bf16[96,2176]{1,0:T(8,128)(2,1)S(1)}, bf16[96,2176]{1,0:T(8,128)(2,1)S(1)}, u32[]{:S(2)}, u32[]{:S(2)}) collective-permute-start(bf16[96,2176]{1,0:T(8,128)(2,1)S(1)} %copy-done.12), channel_id=1, source_target_pairs={{0,4},{2,6},{4,0},{6,2},{8,12},{10,14},{12,8},{14,10},{16,20},{18,... | collective-permute-start | bytes 1253384 | tf_op jit(solution)/shard_map/ppermute | solution.py:377
  121.7 18.2 %collective-permute-start.25 = (bf16[96,2176]{1,0:T(8,128)(2,1)S(1)}, bf16[96,2176]{1,0:T(8,128)(2,1)S(1)}, u32[]{:S(2)}, u32[]{:S(2)}) collective-permute-start(bf16[96,2176]{1,0:T(8,128)(2,1)S(1)} %get-tuple-element.139.refs_7_), channel_id=1, source_target_pairs={{0,4},{2,6},{4,0},{6,2},{8,12},{10,14},{12,8},{14,10},{16,20},{18,... | collective-permute-start | bytes 1253384 | tf_op jit(solution)/shard_map/ppermute | solution.py:377
  131.9 8.1 %copy-start.7 = (bf16[96,2176]{1,0:T(8,128)(2,1)S(1)}, bf16[96,2176]{1,0:T(8,128)(2,1)}, u32[]{:S(2)}) copy-start(bf16[96,2176]{1,0:T(8,128)(2,1)} %get-tuple-element.122) | copy-start | bytes 1253380
  131.9 10.7 %copy-start.1 = (bf16[896,2048]{1,0:T(8,128)(2,1)S(1)}, bf16[896,2048]{1,0:T(8,128)(2,1)}, u32[]{:S(2)}) copy-start(bf16[896,2048]{1,0:T(8,128)(2,1)} %get-tuple-element.138.refs_0_) | copy-start | bytes 11010052
  137.7 4.8 %collective-permute-start.29 = (bf16[1,96,2176]{2,1,0:T(8,128)(2,1)}, bf16[1,96,2176]{2,1,0:T(8,128)(2,1)S(1)}, u32[]{:S(2)}, u32[]{:S(2)}) collective-permute-start(bf16[1,96,2176]{2,1,0:T(8,128)(2,1)} %get-tuple-element.132), channel_id=1, source_target_pairs={{0,2},{2,0},{4,6},{6,4},{8,10},{10,8},{12,14},{14,12},{16,18},{18,... | collective-permute-start | bytes 1253384 | tf_op jit(solution)/shard_map/ppermute | solution.py:377
  140.0 11.2 %collective-permute-start.26 = (bf16[96,2176]{1,0:T(8,128)(2,1)S(1)}, bf16[96,2176]{1,0:T(8,128)(2,1)S(1)}, u32[]{:S(2)}, u32[]{:S(2)}) collective-permute-start(bf16[96,2176]{1,0:T(8,128)(2,1)S(1)} %add_convert_fusion.4.refs_1_), channel_id=1, source_target_pairs={{0,24},{2,26},{4,28},{6,30},{8,0},{10,2},{12,4},{14,6},{16,8},{18,... | collective-permute-start | bytes 1253384 | tf_op jit(solution)/shard_map/ppermute | solution.py:377
  142.6 1.0 copy-start.8
  142.6 2.3 %copy-start.2 = (bf16[896,768]{1,0:T(8,128)(2,1)S(1)}, bf16[896,768]{1,0:T(8,128)(2,1)}, u32[]{:S(2)}) copy-start(bf16[896,768]{1,0:T(8,128)(2,1)} %get-tuple-element.137) | copy-start | bytes 4128772
  143.7 11.8 %collective-permute-start.30 = (bf16[96,2176]{1,0:T(8,128)(2,1)S(1)}, bf16[96,2176]{1,0:T(8,128)(2,1)S(1)}, u32[]{:S(2)}, u32[]{:S(2)}) collective-permute-start(bf16[96,2176]{1,0:T(8,128)(2,1)S(1)} %fusion.5), channel_id=1, source_target_pairs={{0,4},{2,6},{4,0},{6,2},{8,12},{10,14},{12,8},{14,10},{16,20},{18,... | collective-permute-start | bytes 1253384 | tf_op jit(solution)/shard_map/ppermute | solution.py:377
  144.8 6.4 %copy-start.6 = (bf16[96,2176]{1,0:T(8,128)(2,1)S(1)}, bf16[96,2176]{1,0:T(8,128)(2,1)}, u32[]{:S(2)}) copy-start(bf16[96,2176]{1,0:T(8,128)(2,1)} %get-tuple-element.123) | copy-start | bytes 1253380
  144.8 10.8 %copy-start = (bf16[896,2048]{1,0:T(8,128)(2,1)S(1)}, bf16[896,2048]{1,0:T(8,128)(2,1)}, u32[]{:S(2)}) copy-start(bf16[896,2048]{1,0:T(8,128)(2,1)} %get-tuple-element.134.refs_0_) | copy-start | bytes 11010052
  151.4 15.5 %collective-permute-start.27 = (bf16[96,2176]{1,0:T(8,128)(2,1)S(1)}, bf16[96,2176]{1,0:T(8,128)(2,1)S(1)}, u32[]{:S(2)}, u32[]{:S(2)}) collective-permute-start(bf16[96,2176]{1,0:T(8,128)(2,1)S(1)} %add_convert_fusion.3.refs_2_), channel_id=1, source_target_pairs={{0,24},{2,26},{4,28},{6,30},{8,0},{10,2},{12,4},{14,6},{16,8},{18,... | collective-permute-start | bytes 1253384 | tf_op jit(solution)/shard_map/ppermute | solution.py:377
  155.6 17.1 %collective-permute-start.31 = (bf16[96,2176]{1,0:T(8,128)(2,1)S(1)}, bf16[96,2176]{1,0:T(8,128)(2,1)S(1)}, u32[]{:S(2)}, u32[]{:S(2)}) collective-permute-start(bf16[96,2176]{1,0:T(8,128)(2,1)S(1)} %add_convert_fusion.refs_3_), channel_id=1, source_target_pairs={{0,8},{2,10},{4,12},{6,14},{8,16},{10,18},{12,20},{14,22},{16,24},... | collective-permute-start | bytes 1253384 | tf_op jit(solution)/shard_map/ppermute | solution.py:377
  155.6 1.3 copy-start.4
  157.0 4.9 %copy-start.3 = (bf16[896,768]{1,0:T(8,128)(2,1)S(1)}, bf16[896,768]{1,0:T(8,128)(2,1)}, u32[]{:S(2)}) copy-start(bf16[896,768]{1,0:T(8,128)(2,1)} %get-tuple-element.135) | copy-start | bytes 4128772
  161.9 10.7 %copy-start.9 = (bf16[96,2176]{1,0:T(8,128)(2,1)S(1)}, bf16[96,2176]{1,0:T(8,128)(2,1)}, u32[]{:S(2)}) copy-start(bf16[96,2176]{1,0:T(8,128)(2,1)} %get-tuple-element.133) | copy-start | bytes 1253380
  161.9 10.7 %copy-start.10 = (s32[96,8]{0,1:T(8,128)S(1)}, s32[96,8]{0,1:T(8,128)}, u32[]{:S(2)}) copy-start(s32[96,8]{0,1:T(8,128)} %param.9) | copy-start | bytes 9220

commit v5 on v4

--- a/solution.py
+++ b/solution.py
@@ -214,7 +214,7 @@
     in_specs = [whole(b.shape) for b in blocks] + [ANY if fresh else VMEM] * 3 + [ANY] * (len(after) + len(slabs))
     args = list(blocks) + (in_hbm(weights) if fresh else in_vmem(weights)) + in_hbm(after[:1]) + list(after[1:])
     aliases = {len(args) + i: 1 + i for i in range(len(slabs))}
-    args += [*slabs, *in_hbm(added[:1]), *added[1:]]
+    args += [*slabs, *added]
     in_specs += [whole(a.shape) for a in added]
     out_specs = [
         whole((rows, 3 * hid)),
@@ -225,7 +225,7 @@
         whole((8, LANES)),
     ]
     out_shape = [
-        pltpu.HBM((rows, 3 * hid), BF),
+        jax.ShapeDtypeStruct((rows, 3 * hid), BF),
         pltpu.HBM((total, feat), BF),
         pltpu.HBM((total, feat), BF),
         pltpu.HBM((inner * tok, pad), BF),
@@ -328,14 +328,14 @@
     wide = feat + LANES
     whole = lambda shape: pl.BlockSpec(shape, lambda i: (0,) * len(shape))
     slab = pl.BlockSpec((pad, hid), lambda i: (index, 0))
-    args = in_hbm(parts[:1]) + list(parts[1:]) + in_hbm([st, grow]) + in_vmem([wg, wu]) + in_hbm(after[:1]) + list(after[1:])
+    args = list(parts) + in_hbm([st, grow]) + in_vmem([wg, wu]) + in_hbm(after[:1]) + list(after[1:])
     in_specs = [whole(a.shape) for a in args[: len(parts) + 2]] + [VMEM] * 2 + [ANY] * len(after)
     aliases = {}
     if slabs:
         aliases = {len(args) + i: 2 + i for i in range(3)}
         args += list(slabs)
         in_specs += [ANY] * 3
-    half = pltpu.HBM((inner // 2, tok, wide), BF)
+    half = jax.ShapeDtypeStruct((inner // 2, tok, wide), BF)
     saved = pltpu.HBM((total, hid), BF)
     return pl.pallas_call(
         functools.partial(backward_kernel, inner, tok, feat, hid, tile, len(parts)),

time: 175 us -> 171 us (0.977)
  Pallas kernels: 66.6 us -> 56.6 us
  waiting for transfers between devices: 55.1 us -> 64.3 us
    ppermute x27, waiting for transfers between devices: 43.6 us -> 50.8 us  [move(): return lax.ppermute(x, 'expert', shift(**by))]
    pallas_call x5, Pallas kernels: 32.3 us -> 26.1 us  [backward_call(): pl.pallas_call(functools.partial(backward_kernel, inner, tok, feat, hid,...]
    pallas_call x5, Pallas kernels: 33.1 us -> 29.2 us  [forward_call(): pl.pallas_call(functools.partial(forward_kernel, cfg), grid=(hid // tile,...]
    ppermute x5, waiting for transfers between devices: 11.5 us -> 13.5 us  [swap(): return [part, lax.ppermute(part, 'seq', [(0, 1), (1, 0)])]]
  transfers between devices with their start and end apart: 32 -> 32, of which waited for: 17 -> 18; matrix products, arithmetic and copies ran while one was open for 9% -> 9% of each run, Pallas kernels for 33% -> 29%
where the time goes in v5:
time: 171 us; the launch traced here: 170 us
  waiting for transfers between devices  64.3 us (38%)
  Pallas kernels  56.6 us (33%)
  starting transfers between devices  29.9 us (17%)
  matrix products  14.7 us (9%)
  other arithmetic  2.55 us (1%)
    ppermute x27, waiting for transfers between devices, move(): return lax.ppermute(x, 'expert', shift(**by))  50.8 us
    pallas_call x5, Pallas kernels, forward_call(): pl.pallas_call(functools.partial(forward_kernel, cfg), grid=(hid // tile,...  29.2 us
    pallas_call x5, Pallas kernels, backward_call(): pl.pallas_call(functools.partial(backward_kernel, inner, tok, feat, hid,...  26.1 us
    ppermute x27, starting transfers between devices, move(): return lax.ppermute(x, 'expert', shift(**by))  22.4 us
    dot_general x3, matrix products, local(): lax.dot_general(a, b, contract_rows, preferred_element_type=F32).astype(BF)  14.7 us
    ppermute x5, waiting for transfers between devices, swap(): return [part, lax.ppermute(part, 'seq', [(0, 1), (1, 0)])]  13.5 us
    ppermute x5, starting transfers between devices, swap(): return [part, lax.ppermute(part, 'seq', [(0, 1), (1, 0)])]  7.45 us
  transfers between devices with their start and end apart: 32, of which 18 were waited for; matrix products, arithmetic and copies ran while one was open for 9% of the time, Pallas kernels for 29%

profile of v5, /device:TPU:0, one launch (start us, length us, event | category | flops | bytes accessed | tf_op | source)
XLA Modules:
  0.0 170.2 jit_solution(4448322937641036166)
XLA Ops:
  0.6 1.3 shard_map.110.refs_0_
  1.9 0.5 collective-permute-start.1
  2.4 2.6 %collective-permute-start = (bf16[96,4224]{1,0:T(8,128)(2,1)S(1)}, bf16[96,4224]{1,0:T(8,128)(2,1)S(1)}, u32[]{:S(2)}, u32[]{:S(2)}) collective-permute-start(bf16[96,4224]{1,0:T(8,128)(2,1)S(1)} %shard_map.110.refs_0_), channel_id=1, source_target_pairs={{0,8},{2,10},{4,12},{6,14},{8,16},{10,18},{12,20},{14,22},{16,24},... | collective-permute-start | bytes 2433032 | tf_op jit(solution)/shard_map/ppermute | solution.py:377
  5.1 1.5 collective-permute-start.4
  6.6 7.1 %shard_map.111 = (bf16[108,2304]{1,0:T(8,128)(2,1)S(1)}, bf16[896,2048]{1,0:T(8,128)(2,1)}, bf16[896,2048]{1,0:T(8,128)(2,1)}, bf16[192,112]{1,0:T(8,128)(2,1)},...) custom-call(bf16[96,4224]{1,0:T(8,128)(2,1)S(1)} %shard_map.110.refs, ...), custom_call_target="tpu_custom_call" | custom-call | flops 1000 | bytes 1000 | tf_op jit(solution)/shard_map/pallas_call | solution.py:249
  13.7 1.6 collective-permute-start.2
  15.2 10.5 %collective-permute-done.refs_0_ = bf16[96,4224]{1,0:T(8,128)(2,1)S(1)} collective-permute-done((bf16[96,4224]{1,0:T(8,128)(2,1)S(1)}, bf16[96,4224]{1,0:T(8,128)(2,1)S(1)}, u32[]{:S(2)}, u32[]{:S(2)}) %collective-permute-start) | collective-permute-done | bytes 811040 | tf_op jit(solution)/shard_map/ppermute | solution.py:377
  25.8 1.5 collective-permute-done.2.refs_1_
  27.3 0.5 collective-permute-start.5
  27.8 0.9 collective-permute-start.9
  28.7 1.6 collective-permute-start.3
  30.3 4.8 %shard_map.114 = (bf16[1,96,2176]{2,1,0:T(8,128)(2,1)S(1)}, bf16[1,96,2176]{2,1,0:T(8,128)(2,1)S(1)}, bf16[896,768]{1,0:T(8,128)(2,1)}, bf16[896,768]{1,0:T(8,12...) custom-call(bf16[108,2304]{1,0:T(8,128)(2,1)S(1)} %get-tuple-element.72.refs_0_, ...), custom_call_target="tpu_custom_call" | custom-call | flops 1000 | bytes 1000 | tf_op jit(solution)/shard_map/pallas_call | solution.py:340
  35.1 5.6 %shard_map.115 = (bf16[216,2304]{1,0:T(8,128)(2,1)S(1)}, bf16[896,2048]{1,0:T(8,128)(2,1)}, bf16[896,2048]{1,0:T(8,128)(2,1)}, bf16[384,224]{1,0:T(8,128)(2,1)},...) custom-call(bf16[96,4224]{1,0:T(8,128)(2,1)S(1)} %shard_map.113.refs_0_, ...), custom_call_target="tpu_custom_call", output_to_operand_aliasing={{1}: (8, {}), {2}: (9, {})} | custom-call | flops 1000 | bytes 1000 | tf_op jit(solution)/shard_map/pallas_call | solution.py:249
  40.7 1.5 collective-permute-start.8
  42.1 5.7 %collective-permute-done.9.refs_0_ = bf16[96,4224]{1,0:T(8,128)(2,1)S(1)} collective-permute-done((bf16[96,4224]{1,0:T(8,128)(2,1)S(1)}, bf16[96,4224]{1,0:T(8,128)(2,1)S(1)}, u32[]{:S(2)}, u32[]{:S(2)}) %collective-permute-start.9) | collective-permute-done | bytes 811040 | tf_op jit(solution)/shard_map/ppermute | solution.py:377
  47.8 2.5 %collective-permute-done.3.refs_0_ = bf16[96,4224]{1,0:T(8,128)(2,1)S(1)} collective-permute-done((bf16[96,4224]{1,0:T(8,128)(2,1)S(1)}, bf16[96,4224]{1,0:T(8,128)(2,1)S(1)}, u32[]{:S(2)}, u32[]{:S(2)}) %collective-permute-start.3) | collective-permute-done | bytes 811040 | tf_op jit(solution)/shard_map/ppermute | solution.py:377
  50.3 1.7 %collective-permute-start.14 = (bf16[96,4224]{1,0:T(8,128)(2,1)S(1)}, bf16[96,4224]{1,0:T(8,128)(2,1)S(1)}, u32[]{:S(2)}, u32[]{:S(2)}) collective-permute-start(bf16[96,4224]{1,0:T(8,128)(2,1)S(1)} %shard_map.110.refs_0_), channel_id=1, source_target_pairs={{0,24},{2,26},{4,28},{6,30},{8,0},{10,2},{12,4},{14,6},{16,8},{18,... | collective-permute-start | bytes 2433032 | tf_op jit(solution)/shard_map/ppermute | solution.py:377
  52.1 0.8 collective-permute-start.7
  52.9 5.8 %shard_map.118 = (bf16[216,2304]{1,0:T(8,128)(2,1)S(1)}, bf16[896,2048]{1,0:T(8,128)(2,1)}, bf16[896,2048]{1,0:T(8,128)(2,1)}, bf16[384,224]{1,0:T(8,128)(2,1)},...) custom-call(bf16[96,4224]{1,0:T(8,128)(2,1)S(1)} %shard_map.117.refs, ...), custom_call_target="tpu_custom_call", output_to_operand_aliasing={{1}: (8, {}), {2}: (9, {})} | custom-call | flops 1000 | bytes 1000 | tf_op jit(solution)/shard_map/pallas_call | solution.py:249
  58.7 1.5 collective-permute-start.19
  60.2 5.3 %collective-permute-done.8.refs_1_ = bf16[216,2304]{1,0:T(8,128)(2,1)S(1)} collective-permute-done((bf16[216,2304]{1,0:T(8,128)(2,1)S(1)}, bf16[216,2304]{1,0:T(8,128)(2,1)S(1)}, u32[]{:S(2)}, u32[]{:S(2)}) %collective-permute-start.8) | collective-permute-done | bytes 995360 | tf_op jit(solution)/shard_map/ppermute | solution.py:384
  65.5 5.5 %shard_map.119 = (bf16[2,96,2176]{2,1,0:T(8,128)(2,1)S(1)}, bf16[2,96,2176]{2,1,0:T(8,128)(2,1)S(1)}, bf16[896,768]{1,0:T(8,128)(2,1)}, bf16[896,768]{1,0:T(8,12...) custom-call(bf16[216,2304]{1,0:T(8,128)(2,1)S(1)} %get-tuple-element, ...), custom_call_target="tpu_custom_call", output_to_operand_aliasing={{2}: (7, {}), {3}: (8, {}), {4}: (9, {})} | custom-call | flops 1000 | bytes 1000 | tf_op jit(solution)/shard_map/pallas_call | solution.py:340
  71.0 0.5 collective-permute-start.15
  71.5 0.8 collective-permute-done.7.refs_0_
  72.3 0.5 collective-permute-start.18
  72.8 1.7 collective-permute-done.15.refs_3_
  74.5 1.2 collective-permute-done.13.refs_1_
  75.6 6.1 %shard_map.122 = (bf16[216,2304]{1,0:T(8,128)(2,1)S(1)}, bf16[896,2048]{1,0:T(8,128)(2,1)}, bf16[896,2048]{1,0:T(8,128)(2,1)}, bf16[384,224]{1,0:T(8,128)(2,1)},...) custom-call(bf16[96,4224]{1,0:T(8,128)(2,1)S(1)} %shard_map.120.refs, ...), custom_call_target="tpu_custom_call", output_to_operand_aliasing={{1}: (8, {}), {2}: (9, {})} | custom-call | flops 1000 | bytes 1000 | tf_op jit(solution)/shard_map/pallas_call | solution.py:249
  81.8 1.5 collective-permute-start.23
  83.3 3.6 %collective-permute-done.19.refs_1_ = bf16[216,2304]{1,0:T(8,128)(2,1)S(1)} collective-permute-done((bf16[216,2304]{1,0:T(8,128)(2,1)S(1)}, bf16[216,2304]{1,0:T(8,128)(2,1)S(1)}, u32[]{:S(2)}, u32[]{:S(2)}) %collective-permute-start.19) | collective-permute-done | bytes 995360 | tf_op jit(solution)/shard_map/ppermute | solution.py:384
  86.8 5.5 %shard_map.123 = (bf16[2,96,2176]{2,1,0:T(8,128)(2,1)S(1)}, bf16[2,96,2176]{2,1,0:T(8,128)(2,1)S(1)}, bf16[896,768]{1,0:T(8,128)(2,1)}, bf16[896,768]{1,0:T(8,12...) custom-call(bf16[216,2304]{1,0:T(8,128)(2,1)S(1)} %get-tuple-element, ...), custom_call_target="tpu_custom_call", output_to_operand_aliasing={{2}: (7, {}), {3}: (8, {}), {4}: (9, {})} | custom-call | flops 1000 | bytes 1000 | tf_op jit(solution)/shard_map/pallas_call | solution.py:340
  92.4 0.4 collective-permute-done.18.refs_0_
  92.8 0.1 collective-permute-start.20
  92.9 1.1 collective-permute-start.17
  94.0 1.9 %collective-permute-done.20.refs_1_ = bf16[96,4224]{1,0:T(8,128)(2,1)S(1)} collective-permute-done((bf16[96,4224]{1,0:T(8,128)(2,1)S(1)}, bf16[96,4224]{1,0:T(8,128)(2,1)S(1)}, u32[]{:S(2)}, u32[]{:S(2)}) %collective-permute-start.20) | collective-permute-done | bytes 811040 | tf_op jit(solution)/shard_map/ppermute | solution.py:377
  95.9 4.6 %shard_map.125 = (bf16[108,2304]{1,0:T(8,128)(2,1)S(1)}, bf16[896,2048]{1,0:T(8,128)(2,1)}, bf16[896,2048]{1,0:T(8,128)(2,1)}, bf16[192,112]{1,0:T(8,128)(2,1)},...) custom-call(bf16[96,4224]{1,0:T(8,128)(2,1)S(1)} %shard_map.124.refs, ...), custom_call_target="tpu_custom_call", output_to_operand_aliasing={{1}: (6, {}), {2}: (7, {})} | custom-call | flops 1000 | bytes 1000 | tf_op jit(solution)/shard_map/pallas_call | solution.py:249
  100.5 4.3 %collective-permute-done.17.refs_7_.refs_9_ = bf16[96,2176]{1,0:T(8,128)(2,1)S(1)} collective-permute-done((bf16[96,2176]{1,0:T(8,128)(2,1)S(1)}, bf16[96,2176]{1,0:T(8,128)(2,1)S(1)}, u32[]{:S(2)}, u32[]{:S(2)}) %collective-permute-start.17) | collective-permute-done | bytes 417824 | tf_op jit(solution)/shard_map/ppermute | solution.py:377
  104.8 2.9 %collective-permute-done.23.refs_1_ = bf16[216,2304]{1,0:T(8,128)(2,1)S(1)} collective-permute-done((bf16[216,2304]{1,0:T(8,128)(2,1)S(1)}, bf16[216,2304]{1,0:T(8,128)(2,1)S(1)}, u32[]{:S(2)}, u32[]{:S(2)}) %collective-permute-start.23) | collective-permute-done | bytes 995360 | tf_op jit(solution)/shard_map/ppermute | solution.py:384
  107.7 5.5 %shard_map.126 = (bf16[2,96,2176]{2,1,0:T(8,128)(2,1)S(1)}, bf16[2,96,2176]{2,1,0:T(8,128)(2,1)S(1)}, bf16[896,768]{1,0:T(8,128)(2,1)}, bf16[896,768]{1,0:T(8,12...) custom-call(bf16[216,2304]{1,0:T(8,128)(2,1)S(1)} %get-tuple-element, ...), custom_call_target="tpu_custom_call", output_to_operand_aliasing={{2}: (8, {}), {3}: (9, {}), {4}: (10, {})} | custom-call | flops 1000 | bytes 1000 | tf_op jit(solution)/shard_map/pallas_call | solution.py:340
  113.3 1.5 collective-permute-start.28
  114.8 1.1 collective-permute-start.22
  115.9 0.2 fusion.3
  116.1 1.0 collective-permute-start.25
  117.0 10.2 %collective-permute-done.22.refs_10_ = bf16[96,2176]{1,0:T(8,128)(2,1)S(1)} collective-permute-done((bf16[96,2176]{1,0:T(8,128)(2,1)S(1)}, bf16[96,2176]{1,0:T(8,128)(2,1)S(1)}, u32[]{:S(2)}, u32[]{:S(2)}) %collective-permute-start.22) | collective-permute-done | bytes 417824 | tf_op jit(solution)/shard_map/ppermute | solution.py:377
  127.2 0.2 collective-permute-done.28.refs_1_
  127.4 4.8 %shard_map.127 = (bf16[1,96,2176]{2,1,0:T(8,128)(2,1)S(1)}, bf16[1,96,2176]{2,1,0:T(8,128)(2,1)S(1)}, bf16[896,768]{1,0:T(8,128)(2,1)}, bf16[896,768]{1,0:T(8,12...) custom-call(bf16[108,2304]{1,0:T(8,128)(2,1)S(1)} %get-tuple-element, ...), custom_call_target="tpu_custom_call", output_to_operand_aliasing={{2}: (11, {}), {3}: (12, {}), {4}: (13, {})} | custom-call | flops 1000 | bytes 1000 | tf_op jit(solution)/shard_map/pallas_call | solution.py:340
  132.3 3.2 %collective-permute-done.25 = bf16[96,2176]{1,0:T(8,128)(2,1)S(1)} collective-permute-done((bf16[96,2176]{1,0:T(8,128)(2,1)S(1)}, bf16[96,2176]{1,0:T(8,128)(2,1)S(1)}, u32[]{:S(2)}, u32[]{:S(2)}) %collective-permute-start.25) | collective-permute-done | bytes 417824 | tf_op jit(solution)/shard_map/ppermute | solution.py:377
  135.5 0.1 add_convert_fusion.4.refs_1_
  135.6 2.5 %collective-permute-start.26 = (bf16[96,2176]{1,0:T(8,128)(2,1)S(1)}, bf16[96,2176]{1,0:T(8,128)(2,1)S(1)}, u32[]{:S(2)}, u32[]{:S(2)}) collective-permute-start(bf16[96,2176]{1,0:T(8,128)(2,1)S(1)} %add_convert_fusion.4.refs_1_), channel_id=1, source_target_pairs={{0,24},{2,26},{4,28},{6,30},{8,0},{10,2},{12,4},{14,6},{16,8},{18,... | collective-permute-start | bytes 1253384 | tf_op jit(solution)/shard_map/ppermute | solution.py:377
  138.1 0.1 fusion.5
  138.2 1.2 collective-permute-start.30
  139.4 0.1 copy-done.2
  139.5 4.8 %fusion.2 = bf16[1,768,2048]{2,1,0:T(8,128)(2,1)} fusion(bf16[896,768]{1,0:T(8,128)(2,1)S(1)} %copy-done.2, bf16[896,2048]{1,0:T(8,128)(2,1)S(1)} %shard_map.129), kind=kOutput, calls=%fused_computation.5 | convolution fusion | flops 2820145152 | bytes 8192000 | tf_op jit(solution)/shard_map/dot_general | solution.py:500
  144.3 2.5 %collective-permute-done.26 = bf16[96,2176]{1,0:T(8,128)(2,1)S(1)} collective-permute-done((bf16[96,2176]{1,0:T(8,128)(2,1)S(1)}, bf16[96,2176]{1,0:T(8,128)(2,1)S(1)}, u32[]{:S(2)}, u32[]{:S(2)}) %collective-permute-start.26) | collective-permute-done | bytes 417824 | tf_op jit(solution)/shard_map/ppermute | solution.py:377
  146.8 0.2 add_convert_fusion.3.refs_2_
  147.0 4.1 %collective-permute-start.27 = (bf16[96,2176]{1,0:T(8,128)(2,1)S(1)}, bf16[96,2176]{1,0:T(8,128)(2,1)S(1)}, u32[]{:S(2)}, u32[]{:S(2)}) collective-permute-start(bf16[96,2176]{1,0:T(8,128)(2,1)S(1)} %add_convert_fusion.3.refs_2_), channel_id=1, source_target_pairs={{0,24},{2,26},{4,28},{6,30},{8,0},{10,2},{12,4},{14,6},{16,8},{18,... | collective-permute-start | bytes 1253384 | tf_op jit(solution)/shard_map/ppermute | solution.py:377
  151.1 0.1 add_convert_fusion.refs_3_
  151.2 0.1 collective-permute-start.31
  151.3 1.3 copy-done.4
  152.6 4.9 %fusion.1 = bf16[1,2048,768]{2,1,0:T(8,128)(2,1)} fusion(bf16[896,2048]{1,0:T(8,128)(2,1)S(1)} %shard_map.128, bf16[896,768]{1,0:T(8,128)(2,1)S(1)} %copy-done.4), kind=kOutput, calls=%fused_computation.4 | convolution fusion | flops 2820145152 | bytes 8192000 | tf_op jit(solution)/shard_map/dot_general | solution.py:500
  157.5 4.9 %fusion = bf16[1,2048,768]{2,1,0:T(8,128)(2,1)} fusion(bf16[896,2048]{1,0:T(8,128)(2,1)S(1)} %shard_map.128, bf16[896,768]{1,0:T(8,128)(2,1)S(1)} %copy-done.3), kind=kOutput, calls=%fused_computation.3 | convolution fusion | flops 2820145152 | bytes 8192000 | tf_op jit(solution)/shard_map/dot_general | solution.py:500
  162.5 5.8 %collective-permute-done.31 = bf16[96,2176]{1,0:T(8,128)(2,1)S(1)} collective-permute-done((bf16[96,2176]{1,0:T(8,128)(2,1)S(1)}, bf16[96,2176]{1,0:T(8,128)(2,1)S(1)}, u32[]{:S(2)}, u32[]{:S(2)}) %collective-permute-start.31) | collective-permute-done | bytes 417824 | tf_op jit(solution)/shard_map/ppermute | solution.py:377
  168.4 0.9 select_reduce_fusion
  169.3 0.9 add_convert_fusion.6
  (53 shorter events, 0.1 us)
Async XLA Ops:
  1.9 4.7 %collective-permute-start.1 = (bf16[96,4224]{1,0:T(8,128)(2,1)S(1)}, bf16[96,4224]{1,0:T(8,128)(2,1)S(1)}, u32[]{:S(2)}, u32[]{:S(2)}) collective-permute-start(bf16[96,4224]{1,0:T(8,128)(2,1)S(1)} %shard_map.110.refs_0_), channel_id=1, source_target_pairs={{0,2},{2,0},{4,6},{6,4},{8,10},{10,8},{12,14},{14,12},{16,18},{18,... | collective-permute-start | bytes 2433032 | tf_op jit(solution)/shard_map/ppermute | solution.py:377
  2.4 23.3 %collective-permute-start = (bf16[96,4224]{1,0:T(8,128)(2,1)S(1)}, bf16[96,4224]{1,0:T(8,128)(2,1)S(1)}, u32[]{:S(2)}, u32[]{:S(2)}) collective-permute-start(bf16[96,4224]{1,0:T(8,128)(2,1)S(1)} %shard_map.110.refs_0_), channel_id=1, source_target_pairs={{0,8},{2,10},{4,12},{6,14},{8,16},{10,18},{12,20},{14,22},{16,24},... | collective-permute-start | bytes 2433032 | tf_op jit(solution)/shard_map/ppermute | solution.py:377
  5.1 22.2 %collective-permute-start.4 = (bf16[96,4224]{1,0:T(8,128)(2,1)S(1)}, bf16[96,4224]{1,0:T(8,128)(2,1)S(1)}, u32[]{:S(2)}, u32[]{:S(2)}) collective-permute-start(bf16[96,4224]{1,0:T(8,128)(2,1)S(1)} %shard_map.110.refs_0_), channel_id=1, source_target_pairs={{0,4},{2,6},{4,0},{6,2},{8,12},{10,14},{12,8},{14,10},{16,20},{18,... | collective-permute-start | bytes 2433032 | tf_op jit(solution)/shard_map/ppermute | solution.py:377
  13.7 13.6 %collective-permute-start.2 = (bf16[108,2304]{1,0:T(8,128)(2,1)S(1)}, bf16[108,2304]{1,0:T(8,128)(2,1)S(1)}, u32[]{:S(2)}, u32[]{:S(2)}) collective-permute-start(bf16[108,2304]{1,0:T(8,128)(2,1)S(1)} %get-tuple-element.72.refs_0_), channel_id=1, source_target_pairs={{0,1},{1,0},{2,3},{3,2},{4,5},{5,4},{6,7},{7,6},{8,9},{9,8},{10,11... | collective-permute-start | bytes 1493000 | tf_op jit(solution)/shard_map/ppermute | solution.py:384
  27.3 7.8 %collective-permute-start.6 = (bf16[96,4224]{1,0:T(8,128)(2,1)S(1)}, bf16[96,4224]{1,0:T(8,128)(2,1)S(1)}, u32[]{:S(2)}, u32[]{:S(2)}) collective-permute-start(bf16[96,4224]{1,0:T(8,128)(2,1)S(1)} %shard_map.112.refs_2_), channel_id=1, source_target_pairs={{0,2},{2,0},{4,6},{6,4},{8,10},{10,8},{12,14},{14,12},{16,18},{18,... | collective-permute-start | bytes 2433032 | tf_op jit(solution)/shard_map/ppermute | solution.py:377
  27.3 7.8 %collective-permute-start.5 = (bf16[96,4224]{1,0:T(8,128)(2,1)S(1)}, bf16[96,4224]{1,0:T(8,128)(2,1)S(1)}, u32[]{:S(2)}, u32[]{:S(2)}) collective-permute-start(bf16[96,4224]{1,0:T(8,128)(2,1)S(1)} %shard_map.113.refs_0_), channel_id=1, source_target_pairs={{0,2},{2,0},{4,6},{6,4},{8,10},{10,8},{12,14},{14,12},{16,18},{18,... | collective-permute-start | bytes 2433032 | tf_op jit(solution)/shard_map/ppermute | solution.py:377
  27.8 20.0 %collective-permute-start.9 = (bf16[96,4224]{1,0:T(8,128)(2,1)S(1)}, bf16[96,4224]{1,0:T(8,128)(2,1)S(1)}, u32[]{:S(2)}, u32[]{:S(2)}) collective-permute-start(bf16[96,4224]{1,0:T(8,128)(2,1)S(1)} %shard_map.112.refs_2_), channel_id=1, source_target_pairs={{0,4},{2,6},{4,0},{6,2},{8,12},{10,14},{12,8},{14,10},{16,20},{18,... | collective-permute-start | bytes 2433032 | tf_op jit(solution)/shard_map/ppermute | solution.py:377
  28.7 21.6 %collective-permute-start.3 = (bf16[96,4224]{1,0:T(8,128)(2,1)S(1)}, bf16[96,4224]{1,0:T(8,128)(2,1)S(1)}, u32[]{:S(2)}, u32[]{:S(2)}) collective-permute-start(bf16[96,4224]{1,0:T(8,128)(2,1)S(1)} %shard_map.112.refs_2_), channel_id=1, source_target_pairs={{0,8},{2,10},{4,12},{6,14},{8,16},{10,18},{12,20},{14,22},{16,24},... | collective-permute-start | bytes 2433032 | tf_op jit(solution)/shard_map/ppermute | solution.py:377
  35.0 17.0 %collective-permute-start.12 = (bf16[1,96,2176]{2,1,0:T(8,128)(2,1)S(1)}, bf16[1,96,2176]{2,1,0:T(8,128)(2,1)S(1)}, u32[]{:S(2)}, u32[]{:S(2)}) collective-permute-start(bf16[1,96,2176]{2,1,0:T(8,128)(2,1)S(1)} %get-tuple-element.89), channel_id=1, source_target_pairs={{0,2},{2,0},{4,6},{6,4},{8,10},{10,8},{12,14},{14,12},{16,18},{18,... | collective-permute-start | bytes 1253384 | tf_op jit(solution)/shard_map/ppermute | solution.py:377
  40.7 24.8 %collective-permute-start.8 = (bf16[216,2304]{1,0:T(8,128)(2,1)S(1)}, bf16[216,2304]{1,0:T(8,128)(2,1)S(1)}, u32[]{:S(2)}, u32[]{:S(2)}) collective-permute-start(bf16[216,2304]{1,0:T(8,128)(2,1)S(1)} %get-tuple-element.83.refs_0_), channel_id=1, source_target_pairs={{0,1},{1,0},{2,3},{3,2},{4,5},{5,4},{6,7},{7,6},{8,9},{9,8},{10,11... | collective-permute-start | bytes 2985992 | tf_op jit(solution)/shard_map/ppermute | solution.py:384
  47.8 5.0 %collective-permute-start.10 = (bf16[96,4224]{1,0:T(8,128)(2,1)S(1)}, bf16[96,4224]{1,0:T(8,128)(2,1)S(1)}, u32[]{:S(2)}, u32[]{:S(2)}) collective-permute-start(bf16[96,4224]{1,0:T(8,128)(2,1)S(1)} %shard_map.117.refs_0_), channel_id=1, source_target_pairs={{0,2},{2,0},{4,6},{6,4},{8,10},{10,8},{12,14},{14,12},{16,18},{18,... | collective-permute-start | bytes 2433032 | tf_op jit(solution)/shard_map/ppermute | solution.py:377
  50.3 2.5 %collective-permute-start.11 = (bf16[96,4224]{1,0:T(8,128)(2,1)S(1)}, bf16[96,4224]{1,0:T(8,128)(2,1)S(1)}, u32[]{:S(2)}, u32[]{:S(2)}) collective-permute-start(bf16[96,4224]{1,0:T(8,128)(2,1)S(1)} %shard_map.116.refs_2_), channel_id=1, source_target_pairs={{0,2},{2,0},{4,6},{6,4},{8,10},{10,8},{12,14},{14,12},{16,18},{18,... | collective-permute-start | bytes 2433032 | tf_op jit(solution)/shard_map/ppermute | solution.py:377
  50.3 20.6 %collective-permute-start.14 = (bf16[96,4224]{1,0:T(8,128)(2,1)S(1)}, bf16[96,4224]{1,0:T(8,128)(2,1)S(1)}, u32[]{:S(2)}, u32[]{:S(2)}) collective-permute-start(bf16[96,4224]{1,0:T(8,128)(2,1)S(1)} %shard_map.110.refs_0_), channel_id=1, source_target_pairs={{0,24},{2,26},{4,28},{6,30},{8,0},{10,2},{12,4},{14,6},{16,8},{18,... | collective-permute-start | bytes 2433032 | tf_op jit(solution)/shard_map/ppermute | solution.py:377
  52.1 20.2 %collective-permute-start.7 = (bf16[96,4224]{1,0:T(8,128)(2,1)S(1)}, bf16[96,4224]{1,0:T(8,128)(2,1)S(1)}, u32[]{:S(2)}, u32[]{:S(2)}) collective-permute-start(bf16[96,4224]{1,0:T(8,128)(2,1)S(1)} %shard_map.116.refs_2_), channel_id=1, source_target_pairs={{0,4},{2,6},{4,0},{6,2},{8,12},{10,14},{12,8},{14,10},{16,20},{18,... | collective-permute-start | bytes 2433032 | tf_op jit(solution)/shard_map/ppermute | solution.py:377
  58.7 28.2 %collective-permute-start.19 = (bf16[216,2304]{1,0:T(8,128)(2,1)S(1)}, bf16[216,2304]{1,0:T(8,128)(2,1)S(1)}, u32[]{:S(2)}, u32[]{:S(2)}) collective-permute-start(bf16[216,2304]{1,0:T(8,128)(2,1)S(1)} %get-tuple-element.100.refs_0_), channel_id=1, source_target_pairs={{0,1},{1,0},{2,3},{3,2},{4,5},{5,4},{6,7},{7,6},{8,9},{9,8},{10,11... | collective-permute-start | bytes 2985992 | tf_op jit(solution)/shard_map/ppermute | solution.py:384
  71.0 4.7 %collective-permute-start.16 = (bf16[2,96,2176]{2,1,0:T(8,128)(2,1)S(1)}, bf16[2,96,2176]{2,1,0:T(8,128)(2,1)S(1)}, u32[]{:S(2)}, u32[]{:S(2)}) collective-permute-start(bf16[2,96,2176]{2,1,0:T(8,128)(2,1)S(1)} %get-tuple-element.98), channel_id=1, source_target_pairs={{0,2},{2,0},{4,6},{6,4},{8,10},{10,8},{12,14},{14,12},{16,18},{18,... | collective-permute-start | bytes 2506760 | tf_op jit(solution)/shard_map/ppermute | solution.py:377
  71.0 3.5 %collective-permute-start.15 = (bf16[96,4224]{1,0:T(8,128)(2,1)S(1)}, bf16[96,4224]{1,0:T(8,128)(2,1)S(1)}, u32[]{:S(2)}, u32[]{:S(2)}) collective-permute-start(bf16[96,4224]{1,0:T(8,128)(2,1)S(1)} %shard_map.121.refs_2_), channel_id=1, source_target_pairs={{0,2},{2,0},{4,6},{6,4},{8,10},{10,8},{12,14},{14,12},{16,18},{18,... | collective-permute-start | bytes 2433032 | tf_op jit(solution)/shard_map/ppermute | solution.py:377
  72.3 3.4 %collective-permute-start.13 = (bf16[96,4224]{1,0:T(8,128)(2,1)S(1)}, bf16[96,4224]{1,0:T(8,128)(2,1)S(1)}, u32[]{:S(2)}, u32[]{:S(2)}) collective-permute-start(bf16[96,4224]{1,0:T(8,128)(2,1)S(1)} %shard_map.120.refs_0_), channel_id=1, source_target_pairs={{0,2},{2,0},{4,6},{6,4},{8,10},{10,8},{12,14},{14,12},{16,18},{18,... | collective-permute-start | bytes 2433032 | tf_op jit(solution)/shard_map/ppermute | solution.py:377
  72.3 20.5 %collective-permute-start.18 = (bf16[96,4224]{1,0:T(8,128)(2,1)S(1)}, bf16[96,4224]{1,0:T(8,128)(2,1)S(1)}, u32[]{:S(2)}, u32[]{:S(2)}) collective-permute-start(bf16[96,4224]{1,0:T(8,128)(2,1)S(1)} %shard_map.121.refs_2_), channel_id=1, source_target_pairs={{0,4},{2,6},{4,0},{6,2},{8,12},{10,14},{12,8},{14,10},{16,20},{18,... | collective-permute-start | bytes 2433032 | tf_op jit(solution)/shard_map/ppermute | solution.py:377
  81.8 25.9 %collective-permute-start.23 = (bf16[216,2304]{1,0:T(8,128)(2,1)S(1)}, bf16[216,2304]{1,0:T(8,128)(2,1)S(1)}, u32[]{:S(2)}, u32[]{:S(2)}) collective-permute-start(bf16[216,2304]{1,0:T(8,128)(2,1)S(1)} %get-tuple-element.113.refs_0_), channel_id=1, source_target_pairs={{0,1},{1,0},{2,3},{3,2},{4,5},{5,4},{6,7},{7,6},{8,9},{9,8},{10,11... | collective-permute-start | bytes 2985992 | tf_op jit(solution)/shard_map/ppermute | solution.py:384
  86.8 6.1 %copy-start.9 = (bf16[96,2176]{1,0:T(8,128)(2,1)S(1)}, bf16[96,2176]{1,0:T(8,128)(2,1)}, u32[]{:S(2)}) copy-start(bf16[96,2176]{1,0:T(8,128)(2,1)} %get-tuple-element.99) | copy-start | bytes 1253380
  92.4 3.5 %collective-permute-start.21 = (bf16[2,96,2176]{2,1,0:T(8,128)(2,1)S(1)}, bf16[2,96,2176]{2,1,0:T(8,128)(2,1)S(1)}, u32[]{:S(2)}, u32[]{:S(2)}) collective-permute-start(bf16[2,96,2176]{2,1,0:T(8,128)(2,1)S(1)} %get-tuple-element.111), channel_id=1, source_target_pairs={{0,2},{2,0},{4,6},{6,4},{8,10},{10,8},{12,14},{14,12},{16,18},{18,... | collective-permute-start | bytes 2506760 | tf_op jit(solution)/shard_map/ppermute | solution.py:377
  92.8 3.1 %collective-permute-start.20 = (bf16[96,4224]{1,0:T(8,128)(2,1)S(1)}, bf16[96,4224]{1,0:T(8,128)(2,1)S(1)}, u32[]{:S(2)}, u32[]{:S(2)}) collective-permute-start(bf16[96,4224]{1,0:T(8,128)(2,1)S(1)} %shard_map.124.refs_0_), channel_id=1, source_target_pairs={{0,2},{2,0},{4,6},{6,4},{8,10},{10,8},{12,14},{14,12},{16,18},{18,... | collective-permute-start | bytes 2433032 | tf_op jit(solution)/shard_map/ppermute | solution.py:377
  92.9 11.9 %collective-permute-start.17 = (bf16[96,2176]{1,0:T(8,128)(2,1)S(1)}, bf16[96,2176]{1,0:T(8,128)(2,1)S(1)}, u32[]{:S(2)}, u32[]{:S(2)}) collective-permute-start(bf16[96,2176]{1,0:T(8,128)(2,1)S(1)} %copy-done.9), channel_id=1, source_target_pairs={{0,4},{2,6},{4,0},{6,2},{8,12},{10,14},{12,8},{14,10},{16,20},{18,... | collective-permute-start | bytes 1253384 | tf_op jit(solution)/shard_map/ppermute | solution.py:377
  107.7 7.0 %copy-start.10 = (bf16[96,2176]{1,0:T(8,128)(2,1)S(1)}, bf16[96,2176]{1,0:T(8,128)(2,1)}, u32[]{:S(2)}) copy-start(bf16[96,2176]{1,0:T(8,128)(2,1)} %get-tuple-element.112) | copy-start | bytes 1253380
  113.3 2.6 %collective-permute-start.24 = (bf16[2,96,2176]{2,1,0:T(8,128)(2,1)S(1)}, bf16[2,96,2176]{2,1,0:T(8,128)(2,1)S(1)}, u32[]{:S(2)}, u32[]{:S(2)}) collective-permute-start(bf16[2,96,2176]{2,1,0:T(8,128)(2,1)S(1)} %get-tuple-element.121), channel_id=1, source_target_pairs={{0,2},{2,0},{4,6},{6,4},{8,10},{10,8},{12,14},{14,12},{16,18},{18,... | collective-permute-start | bytes 2506760 | tf_op jit(solution)/shard_map/ppermute | solution.py:377
  113.3 14.2 %collective-permute-start.28 = (bf16[108,2304]{1,0:T(8,128)(2,1)S(1)}, bf16[108,2304]{1,0:T(8,128)(2,1)S(1)}, u32[]{:S(2)}, u32[]{:S(2)}) collective-permute-start(bf16[108,2304]{1,0:T(8,128)(2,1)S(1)} %get-tuple-element.124.refs_0_), channel_id=1, source_target_pairs={{0,1},{1,0},{2,3},{3,2},{4,5},{5,4},{6,7},{7,6},{8,9},{9,8},{10,11... | collective-permute-start | bytes 1493000 | tf_op jit(solution)/shard_map/ppermute | solution.py:384
  114.8 12.5 %collective-permute-start.22 = (bf16[96,2176]{1,0:T(8,128)(2,1)S(1)}, bf16[96,2176]{1,0:T(8,128)(2,1)S(1)}, u32[]{:S(2)}, u32[]{:S(2)}) collective-permute-start(bf16[96,2176]{1,0:T(8,128)(2,1)S(1)} %copy-done.10), channel_id=1, source_target_pairs={{0,4},{2,6},{4,0},{6,2},{8,12},{10,14},{12,8},{14,10},{16,20},{18,... | collective-permute-start | bytes 1253384 | tf_op jit(solution)/shard_map/ppermute | solution.py:377
  116.1 19.4 %collective-permute-start.25 = (bf16[96,2176]{1,0:T(8,128)(2,1)S(1)}, bf16[96,2176]{1,0:T(8,128)(2,1)S(1)}, u32[]{:S(2)}, u32[]{:S(2)}) collective-permute-start(bf16[96,2176]{1,0:T(8,128)(2,1)S(1)} %get-tuple-element.139.refs_7_), channel_id=1, source_target_pairs={{0,4},{2,6},{4,0},{6,2},{8,12},{10,14},{12,8},{14,10},{16,20},{18,... | collective-permute-start | bytes 1253384 | tf_op jit(solution)/shard_map/ppermute | solution.py:377
  127.4 8.0 %copy-start.6 = (bf16[96,2176]{1,0:T(8,128)(2,1)S(1)}, bf16[96,2176]{1,0:T(8,128)(2,1)}, u32[]{:S(2)}) copy-start(bf16[96,2176]{1,0:T(8,128)(2,1)} %get-tuple-element.122) | copy-start | bytes 1253380
  127.4 10.7 %copy-start.1 = (bf16[896,2048]{1,0:T(8,128)(2,1)S(1)}, bf16[896,2048]{1,0:T(8,128)(2,1)}, u32[]{:S(2)}) copy-start(bf16[896,2048]{1,0:T(8,128)(2,1)} %get-tuple-element.138.refs_0_) | copy-start | bytes 11010052
  132.3 5.8 %collective-permute-start.29 = (bf16[1,96,2176]{2,1,0:T(8,128)(2,1)S(1)}, bf16[1,96,2176]{2,1,0:T(8,128)(2,1)S(1)}, u32[]{:S(2)}, u32[]{:S(2)}) collective-permute-start(bf16[1,96,2176]{2,1,0:T(8,128)(2,1)S(1)} %get-tuple-element.132), channel_id=1, source_target_pairs={{0,2},{2,0},{4,6},{6,4},{8,10},{10,8},{12,14},{14,12},{16,18},{18,... | collective-permute-start | bytes 1253384 | tf_op jit(solution)/shard_map/ppermute | solution.py:377
  135.6 11.2 %collective-permute-start.26 = (bf16[96,2176]{1,0:T(8,128)(2,1)S(1)}, bf16[96,2176]{1,0:T(8,128)(2,1)S(1)}, u32[]{:S(2)}, u32[]{:S(2)}) collective-permute-start(bf16[96,2176]{1,0:T(8,128)(2,1)S(1)} %add_convert_fusion.4.refs_1_), channel_id=1, source_target_pairs={{0,24},{2,26},{4,28},{6,30},{8,0},{10,2},{12,4},{14,6},{16,8},{18,... | collective-permute-start | bytes 1253384 | tf_op jit(solution)/shard_map/ppermute | solution.py:377
  138.1 1.3 copy-start.2
  138.2 12.8 %collective-permute-start.30 = (bf16[96,2176]{1,0:T(8,128)(2,1)S(1)}, bf16[96,2176]{1,0:T(8,128)(2,1)S(1)}, u32[]{:S(2)}, u32[]{:S(2)}) collective-permute-start(bf16[96,2176]{1,0:T(8,128)(2,1)S(1)} %fusion.5), channel_id=1, source_target_pairs={{0,4},{2,6},{4,0},{6,2},{8,12},{10,14},{12,8},{14,10},{16,20},{18,... | collective-permute-start | bytes 1253384 | tf_op jit(solution)/shard_map/ppermute | solution.py:377
  139.5 7.4 %copy-start.5 = (bf16[96,2176]{1,0:T(8,128)(2,1)S(1)}, bf16[96,2176]{1,0:T(8,128)(2,1)}, u32[]{:S(2)}) copy-start(bf16[96,2176]{1,0:T(8,128)(2,1)} %get-tuple-element.123) | copy-start | bytes 1253380
  139.5 11.8 %copy-start = (bf16[896,2048]{1,0:T(8,128)(2,1)S(1)}, bf16[896,2048]{1,0:T(8,128)(2,1)}, u32[]{:S(2)}) copy-start(bf16[896,2048]{1,0:T(8,128)(2,1)} %get-tuple-element.134.refs_0_) | copy-start | bytes 11010052
  147.0 15.5 %collective-permute-start.27 = (bf16[96,2176]{1,0:T(8,128)(2,1)S(1)}, bf16[96,2176]{1,0:T(8,128)(2,1)S(1)}, u32[]{:S(2)}, u32[]{:S(2)}) collective-permute-start(bf16[96,2176]{1,0:T(8,128)(2,1)S(1)} %add_convert_fusion.3.refs_2_), channel_id=1, source_target_pairs={{0,24},{2,26},{4,28},{6,30},{8,0},{10,2},{12,4},{14,6},{16,8},{18,... | collective-permute-start | bytes 1253384 | tf_op jit(solution)/shard_map/ppermute | solution.py:377
  151.2 17.1 %collective-permute-start.31 = (bf16[96,2176]{1,0:T(8,128)(2,1)S(1)}, bf16[96,2176]{1,0:T(8,128)(2,1)S(1)}, u32[]{:S(2)}, u32[]{:S(2)}) collective-permute-start(bf16[96,2176]{1,0:T(8,128)(2,1)S(1)} %add_convert_fusion.refs_3_), channel_id=1, source_target_pairs={{0,8},{2,10},{4,12},{6,14},{8,16},{10,18},{12,20},{14,22},{16,24},... | collective-permute-start | bytes 1253384 | tf_op jit(solution)/shard_map/ppermute | solution.py:377
  151.3 1.3 copy-start.4
  152.6 4.9 %copy-start.3 = (bf16[896,768]{1,0:T(8,128)(2,1)S(1)}, bf16[896,768]{1,0:T(8,128)(2,1)}, u32[]{:S(2)}) copy-start(bf16[896,768]{1,0:T(8,128)(2,1)} %get-tuple-element.135) | copy-start | bytes 4128772
  157.5 10.8 %copy-start.7 = (bf16[96,2176]{1,0:T(8,128)(2,1)S(1)}, bf16[96,2176]{1,0:T(8,128)(2,1)}, u32[]{:S(2)}) copy-start(bf16[96,2176]{1,0:T(8,128)(2,1)} %get-tuple-element.133) | copy-start | bytes 1253380
  157.5 10.8 %copy-start.8 = (s32[96,8]{0,1:T(8,128)S(1)}, s32[96,8]{0,1:T(8,128)}, u32[]{:S(2)}) copy-start(s32[96,8]{0,1:T(8,128)} %param.9) | copy-start | bytes 9220
